TPU v7x, 128 devices: a whole 4x4x4 slice. The times are simulated.
128 devices in a mesh: dp: 8 (over y, core), ctx: 16 (over x, z).
Axes of the slice: x: 4, y: 4, z: 4, core: 2. Of those that a mesh axis runs over, the one named last changes fastest.
Arguments:
- normed: bfloat16 [8, 2048, 8192], P('dp', 'ctx'), may hold values from -6 to 6
- queries: bfloat16 [8, 2048, 4096], P('dp', 'ctx'), may hold values from -4.5 to 4.5
- rotated_keys: bfloat16 [8, 2048, 512], P('dp', 'ctx'), may hold values from -4.5 to 4.5
- value_weight: bfloat16 [8192, 512], replicated, may hold values from -0.0625 to 0.0625
- adapter_down: bfloat16 [8192, 64], replicated, may hold values from -0.0625 to 0.0625
- adapter_up: bfloat16 [64, 512], replicated, may hold values from -0.75 to 0.75
- attention_cotangent: bfloat16 [8, 2048, 4096], P('dp', 'ctx'), may hold values from -6 to 6
- document_index: int32 [8, 2048], P('dp', 'ctx'), may hold values from 0 to 3, never falling along the last dimension, each value on 1 to 1024 neighbouring positions
- owner_routing: int32 [8, 2048, 1], P('dp', 'ctx'), may hold values from 0 to 15; in each aligned block of 128 rows (0 to 127, 128 to 255, ..., all dimensions but the last counted through in order) at most 12 rows name the same one
Outputs:
- attention_output: bfloat16 [8, 2048, 4096], P('dp', 'ctx')
- query_gradient: bfloat16 [8, 2048, 4096], P('dp', 'ctx')
- d_key: bfloat16 [8, 2048, 512], P('dp', 'ctx')
- normed_input_gradient: bfloat16 [8, 2048, 8192], P('dp', 'ctx')
- down_factor_gradient: float32 [8192, 64], replicated
- up_factor_gradient: float32 [64, 512], replicated
- row_logsumexp: float32 [8, 3072, 32], P('dp', 'ctx')
Inputs may be any that keep to these rules, and one draw needn't show every extreme that they name: `document_index`: along a window the numbers never fall; each document covers 1 to 1024 positions, and one covers exactly 1024. `owner_routing`: among the 128 tokens of one device no owner is named by more than 12 tokens, a bound that some block reaches.
All inputs are finite; a program needn't handle non-finite values.
Results may differ from a plain program's by a relative error of at most 0.023.
Values may be sent and summed in bfloat16 or wider, within the bound.
No kernel may reach another device: no remote copies, remote signals or barrier semaphores. Data moves between devices by JAX's collectives and lax.ppermute only.
A program may use at most 192 MiB of HBM per device.

v0:
```python
import math

import jax
import jax.numpy as jnp
from jax import lax
from jax.sharding import PartitionSpec as P

HEAD_SIZE = 128
HQ = 32
KEY_HEADS = 4
CAP = 12


ADAPTER_SCALE = 0.5
NEG_FILL = -1e30


def pair_allowed(query_segs, query_spots, key_segs, key_spots):
    return (
        (query_segs[:, None] == key_segs[None, :])
        & (key_spots[None, :] <= query_spots[:, None])
        & (query_segs[:, None] >= 0)
    )


def head_scores(query_heads, key_part):
    inv_root = 1.0 / math.sqrt(query_heads.shape[-1])
    return (
        jnp.einsum("rgjd,kgd->gjrk", query_heads, key_part, preferred_element_type=jnp.float32)
        * inv_root
    )


def split_blocks(key_all, seg_all, block_len):
    seq_len = key_all.shape[0]
    block_len = min(block_len, seq_len)
    block_count = seq_len // block_len
    key_blocks = key_all.reshape(block_count, block_len, 2, KEY_HEADS, HEAD_SIZE)
    seg_blocks = seg_all.reshape(block_count, block_len)
    spot_blocks = jnp.arange(seq_len, dtype=jnp.int32).reshape(block_count, block_len)
    return (key_blocks, seg_blocks, spot_blocks)


def forward_pass(query_heads, query_segs, query_spots, key_blocks, seg_blocks, spot_blocks):
    slot_count = query_heads.shape[0]
    live_rows = query_segs >= 0
    marker = jnp.zeros((), jnp.float32)

    def stat_step(running, inputs):
        key_block, key_segs, key_spots = inputs
        allowed = pair_allowed(query_segs, query_spots, key_segs, key_spots)
        row_peak, row_total = running
        scores = head_scores(query_heads, key_block[:, 0])
        new_peak = jnp.maximum(row_peak, jnp.max(jnp.where(allowed, scores, NEG_FILL), axis=-1))
        factor = jnp.exp(row_peak - new_peak)
        probs = jnp.where(allowed, jnp.exp(scores - new_peak[..., None]), 0.0)
        new_total = row_total * factor + jnp.sum(probs, axis=-1)
        return ((new_peak, new_total), marker)

    initial = (
        jnp.full((KEY_HEADS, HQ // KEY_HEADS, slot_count), NEG_FILL, jnp.float32),
        jnp.zeros((KEY_HEADS, HQ // KEY_HEADS, slot_count), jnp.float32),
    )
    (row_peak, row_total), _ = lax.scan(stat_step, initial, (key_blocks, seg_blocks, spot_blocks))
    safe_total = jnp.where(live_rows, row_total, 1.0)
    row_logsumexp = jnp.where(live_rows, row_peak + jnp.log(safe_total), 0.0)

    def value_step(running, inputs):
        key_block, key_segs, key_spots = inputs
        allowed = pair_allowed(query_segs, query_spots, key_segs, key_spots)
        scores = head_scores(query_heads, key_block[:, 0])
        weights = jnp.where(allowed, jnp.exp(scores - row_logsumexp[..., None]), 0.0).astype(
            jnp.bfloat16
        )
        added = jnp.einsum(
            "gjrk,kgd->rgjd", weights, key_block[:, 1], preferred_element_type=jnp.float32
        )
        return (running + added, marker)

    summed, _ = lax.scan(
        value_step, jnp.zeros(query_heads.shape, jnp.float32), (key_blocks, seg_blocks, spot_blocks)
    )
    return (row_logsumexp, summed.reshape(slot_count, -1).astype(jnp.bfloat16))


def backward_pass(
    query_heads,
    grad_heads,
    query_segs,
    query_spots,
    key_blocks,
    seg_blocks,
    spot_blocks,
    row_logsumexp,
    attn_rows,
):
    slot_count = query_heads.shape[0]
    inv_root = 1.0 / math.sqrt(query_heads.shape[-1])
    row_delta = jnp.sum(
        grad_heads.astype(jnp.float32) * attn_rows.reshape(grad_heads.shape).astype(jnp.float32),
        axis=-1,
    ).transpose(1, 2, 0)

    def back_step(running, inputs):
        key_block, key_segs, key_spots = inputs
        allowed = pair_allowed(query_segs, query_spots, key_segs, key_spots)
        scores = head_scores(query_heads, key_block[:, 0])
        weights32 = jnp.where(allowed, jnp.exp(scores - row_logsumexp[..., None]), 0.0)
        weights = weights32.astype(jnp.bfloat16)
        d_prob = jnp.einsum(
            "rgjd,kgd->gjrk", grad_heads, key_block[:, 1], preferred_element_type=jnp.float32
        )
        d_scores = (weights32 * (d_prob - row_delta[..., None])).astype(jnp.bfloat16)
        updated = running + jnp.einsum(
            "gjrk,kgd->rgjd", d_scores, key_block[:, 0], preferred_element_type=jnp.float32
        )
        key_gradient = (
            jnp.einsum("gjrk,rgjd->kgd", d_scores, query_heads, preferred_element_type=jnp.float32)
            * inv_root
        )
        d_values = jnp.einsum(
            "gjrk,rgjd->kgd", weights, grad_heads, preferred_element_type=jnp.float32
        )
        return (updated, jnp.stack([key_gradient, d_values], axis=1))

    summed, key_grads = lax.scan(
        back_step, jnp.zeros(query_heads.shape, jnp.float32), (key_blocks, seg_blocks, spot_blocks)
    )
    d_rows = (summed * inv_root).reshape(slot_count, -1).astype(jnp.bfloat16)
    seq_len = key_blocks.shape[0] * key_blocks.shape[1]
    return (d_rows, key_grads.reshape(seq_len, -1))


def local(
    normed,
    queries,
    rotated_keys,
    value_weight,
    adapter_down,
    adapter_up,
    attention_cotangent,
    document_index,
    owner_routing,
):
    tok_rows = normed.shape[1]
    peer_count = lax.axis_size("ctx")
    slot_count = peer_count * CAP
    query_width = queries.shape[2]
    key_width = rotated_keys.shape[2]
    flattened_rows = normed[0]
    adapter_product = jnp.dot(
        flattened_rows, adapter_down, preferred_element_type=jnp.float32
    ).astype(jnp.bfloat16)
    value_rows = (
        jnp.dot(flattened_rows, value_weight, preferred_element_type=jnp.float32)
        + ADAPTER_SCALE * jnp.dot(adapter_product, adapter_up, preferred_element_type=jnp.float32)
    ).astype(jnp.bfloat16)
    key_value = jnp.concatenate([rotated_keys[0], value_rows], axis=1)[None]
    key_all, seg_all = (
        lax.all_gather(key_value, "ctx", axis=1, tiled=True),
        lax.all_gather(document_index, "ctx", axis=1, tiled=True),
    )
    owners = owner_routing[0, :, 0]
    onehot = (owners[:, None] == jnp.arange(peer_count, dtype=jnp.int32)[None, :]).astype(jnp.int32)
    slot_rank = jnp.sum((jnp.cumsum(onehot, axis=0) - onehot) * onehot, axis=1)
    slot_index = owners * CAP + slot_rank
    row_spots = lax.axis_index("ctx") * tok_rows + jnp.arange(tok_rows, dtype=jnp.int32)
    send_queries = jnp.zeros((slot_count, query_width), jnp.bfloat16).at[slot_index].set(queries[0])
    send_grads = (
        jnp.zeros((slot_count, query_width), jnp.bfloat16)
        .at[slot_index]
        .set(attention_cotangent[0])
    )
    send_meta = (
        jnp.full((slot_count, 2), -1, jnp.int32)
        .at[slot_index]
        .set(jnp.stack([row_spots, document_index[0]], axis=1))
    )
    got_queries, got_grads, got_meta = (
        lax.all_to_all(
            send_queries.reshape(peer_count, CAP, query_width),
            "ctx",
            split_axis=0,
            concat_axis=0,
            tiled=True,
        ),
        lax.all_to_all(
            send_grads.reshape(peer_count, CAP, query_width),
            "ctx",
            split_axis=0,
            concat_axis=0,
            tiled=True,
        ),
        lax.all_to_all(
            send_meta.reshape(peer_count, CAP, 2), "ctx", split_axis=0, concat_axis=0, tiled=True
        ),
    )
    query_heads = got_queries.reshape(slot_count, KEY_HEADS, HQ // KEY_HEADS, HEAD_SIZE)
    grad_heads = got_grads.reshape(slot_count, KEY_HEADS, HQ // KEY_HEADS, HEAD_SIZE)
    row_meta = got_meta.reshape(slot_count, 2)
    query_spots = row_meta[:, 0]
    query_segs = row_meta[:, 1]
    key_blocks, seg_blocks, spot_blocks = split_blocks(key_all[0], seg_all[0], 512)
    row_logsumexp, attn_rows = forward_pass(
        query_heads, query_segs, query_spots, key_blocks, seg_blocks, spot_blocks
    )
    lse_rows = row_logsumexp.transpose(2, 0, 1).reshape(slot_count, HQ)
    d_rows, key_grads = backward_pass(
        query_heads,
        grad_heads,
        query_segs,
        query_spots,
        key_blocks,
        seg_blocks,
        spot_blocks,
        row_logsumexp,
        attn_rows,
    )
    attn_home, grad_home = (
        lax.all_to_all(
            attn_rows.reshape(peer_count, CAP, query_width),
            "ctx",
            split_axis=0,
            concat_axis=0,
            tiled=True,
        ),
        lax.all_to_all(
            d_rows.reshape(peer_count, CAP, query_width),
            "ctx",
            split_axis=0,
            concat_axis=0,
            tiled=True,
        ),
    )
    attention_output = attn_home.reshape(slot_count, query_width)[slot_index]
    query_gradient = grad_home.reshape(slot_count, query_width)[slot_index]
    key_value_grads = lax.psum_scatter(key_grads, "ctx", scatter_dimension=0, tiled=True)
    d_key = key_value_grads[:, :key_width].astype(jnp.bfloat16)
    value_gradient = key_value_grads[:, key_width:].astype(jnp.bfloat16)
    adapter_middle = (
        ADAPTER_SCALE * jnp.dot(value_gradient, adapter_up.T, preferred_element_type=jnp.float32)
    ).astype(jnp.bfloat16)
    normed_input_gradient = (
        jnp.dot(value_gradient, value_weight.T, preferred_element_type=jnp.float32)
        + jnp.dot(adapter_middle, adapter_down.T, preferred_element_type=jnp.float32)
    ).astype(jnp.bfloat16)
    down_gradient_total = jnp.dot(
        flattened_rows.T, adapter_middle, preferred_element_type=jnp.float32
    )
    up_gradient_total = ADAPTER_SCALE * jnp.dot(
        adapter_product.T, value_gradient, preferred_element_type=jnp.float32
    )
    total_down, total_up = lax.psum((down_gradient_total, up_gradient_total), ("dp", "ctx"))
    return (
        attention_output[None],
        query_gradient[None],
        d_key[None],
        normed_input_gradient[None],
        total_down,
        total_up,
        lse_rows[None],
    )


def solution(mesh):
    placed = (
        P("dp", "ctx", None),
        P("dp", "ctx", None),
        P("dp", "ctx", None),
        P(),
        P(),
        P(),
        P("dp", "ctx", None),
        P("dp", "ctx"),
        P("dp", "ctx", None),
    )
    return jax.shard_map(
        local,
        mesh=mesh,
        in_specs=placed,
        out_specs=(
            P("dp", "ctx", None),
            P("dp", "ctx", None),
            P("dp", "ctx", None),
            P("dp", "ctx", None),
            P(),
            P(),
            P("dp", "ctx", None),
        ),
        check_vma=False,
    )
```

profile of v0, /device:TPU:1, one launch (start us, length us, event | category | flops | bytes accessed | tf_op | source)
XLA Modules:
  0.0 640.0 jit_solution(5360654860056371631)
XLA Ops:
  10.9 4.7 fusion.42
  19.0 8.4 %all-to-all-start = ((s32[16,12,2]{1,2,0:T(2,128)}), s32[16,12,2]{1,2,0:T(2,128)S(1)}, u32[]{:S(2)}, u32[]{:S(2)}) async-start(s32[16,12,2]{1,2,0:T(2,128)} %copy.34), calls=%async_computation | async-start | bytes 32768 | tf_op jit(solution)/shard_map/all_to_all | solution.py:194
  27.4 3.3 scatter_custom_fusion.1
  30.7 3.5 reshape.127
  34.2 6.8 %all-to-all-start.1 = ((bf16[16,12,4096]{2,1,0:T(8,128)(2,1)}), bf16[16,12,4096]{2,1,0:T(8,128)(2,1)}, u32[]{:S(2)}, u32[]{:S(2)}) async-start(bf16[16,12,4096]{2,1,0:T(8,128)(2,1)} %reshape.127), calls=%async_computation.1 | async-start | bytes 4194304 | tf_op jit(solution)/shard_map/all_to_all | solution.py:180
  41.0 3.3 scatter_custom_fusion.2
  44.3 3.4 reshape.130
  47.7 27.4 %all-to-all-done.1 = bf16[16,12,4096]{2,1,0:T(8,128)(2,1)} async-done(((bf16[16,12,4096]{2,1,0:T(8,128)(2,1)}), bf16[16,12,4096]{2,1,0:T(8,128)(2,1)}, u32[]{:S(2)}, u32[]{:S(2)}) %all-to-all-start.1) | async-done | bytes 1572896 | tf_op jit(solution)/shard_map/all_to_all | solution.py:180
  75.2 7.2 %all-to-all-start.3 = ((bf16[16,12,4096]{2,1,0:T(8,128)(2,1)}), bf16[16,12,4096]{2,1,0:T(8,128)(2,1)}, u32[]{:S(2)}, u32[]{:S(2)}) async-start(bf16[16,12,4096]{2,1,0:T(8,128)(2,1)} %reshape.130), calls=%async_computation.3 | async-start | bytes 4194304 | tf_op jit(solution)/shard_map/all_to_all | solution.py:187
  82.5 34.0 %all_gather.7 = s32[1,2048]{1,0:T(1,128)S(1)} all-gather(s32[1,128]{1,0:T(1,128)S(1)} %copy-done.17), channel_id=1, replica_groups=mesh['dp'=8,'ctx'=16] {'ctx'}, dimensions={1}, use_global_device_ids=true | all-gather | bytes 8704 | tf_op jit(solution)/shard_map/all_gather | solution.py:161
  117.9 3.9 reshape.128
  121.8 3.3 copy.39
  125.0 3.9 reshape.131
  128.9 3.1 copy.43
  132.1 7.8 %reshape_squeeze.6 = bf16[4,512,2,4,128]{4,3,2,1,0:T(4,128)(2,1)} reshape(bf16[2048,1024]{1,0:T(8,128)(2,1)} %all-gather.3.cloned.1.call-done) | data formatting | bytes 8388608 | tf_op jit(solution)/shard_map/reshape;squeeze | solution.py:38
  139.9 5.2 copy.38
  145.1 31.4 %while.37 = (s32[]{:T(128)}, f32[4,8,192]{2,1,0:T(8,128)S(1)}, f32[4,8,192]{2,1,0:T(8,128)S(1)}, s32[192,1]{0,1:T(1,128)S(1)}, s32[4,512]{1,0:T(4,128)S(1)}, /*i...) while((s32[]{:T(128)}, f32[4,8,192]{2,1,0:T(8,128)S(1)}, ...), condition=%wide.region_7.8_spmd.clone, body=%wide.region_4.0_spmd.clone.sunk | while | flops 827750592 | bytes 36281120 | solution.py:64
  149.0 3.9 fusion.102
  156.8 3.9 fusion.102
  164.7 3.9 fusion.102
  172.5 3.9 fusion.102
  176.6 34.4 %while.38 = (s32[]{:T(128)}, f32[192,4,8,128]{3,0,2,1:T(8,128)}, bf16[4,512,2,4,128]{4,1,3,2,0:T(8,128)(2,1)}, s32[192,1]{0,1:T(1,128)S(1)}, s32[4,512]{1,0:T(4,...) while((s32[]{:T(128)}, f32[192,4,8,128]{3,0,2,1:T(8,128)}, ...), condition=%wide.region_9.10_spmd.clone, body=%wide.region_8.9_spmd.clone.sunk | while | flops 1625161984 | bytes 11246343 | solution.py:80
  178.1 6.7 %bitcast_add_fusion.5 = f32[192,4,8,128]{3,0,2,1:T(8,128)} fusion(f32[192,4,8,128]{3,0,2,1:T(8,128)} %get-tuple-element.677, f32[4,8,192]{2,1,0:T(8,128)S(1)} %get-tuple-element.695, pred[192,512]{1,0:T(8,128)(4,1)S(1)} %and_and_fusion.7, bf16[192,4,8,128]{3,0,2,1:T(8,128)(2,1)} %get-tuple-element.694, pred[]{:T(512)S(6)} %compare.10, ...), kind=kOutput, calls=%fused_computation.30.clone.1 | convolution fusion | flops 1624768512 | bytes 9035777 | tf_op jit(solution)/shard_map/while/body/eval_jaxpr/gjrk,kgd->rgjd/dot_general | solution.py:75
  186.3 7.2 %bitcast_add_fusion.5 = f32[192,4,8,128]{3,0,2,1:T(8,128)} fusion(f32[192,4,8,128]{3,0,2,1:T(8,128)} %get-tuple-element.677, f32[4,8,192]{2,1,0:T(8,128)S(1)} %get-tuple-element.695, pred[192,512]{1,0:T(8,128)(4,1)S(1)} %and_and_fusion.7, bf16[192,4,8,128]{3,0,2,1:T(8,128)(2,1)} %get-tuple-element.694, pred[]{:T(512)S(6)} %compare.10, ...), kind=kOutput, calls=%fused_computation.30.clone.1 | convolution fusion | flops 1624768512 | bytes 9035777 | tf_op jit(solution)/shard_map/while/body/eval_jaxpr/gjrk,kgd->rgjd/dot_general | solution.py:75
  195.0 7.2 %bitcast_add_fusion.5 = f32[192,4,8,128]{3,0,2,1:T(8,128)} fusion(f32[192,4,8,128]{3,0,2,1:T(8,128)} %get-tuple-element.677, f32[4,8,192]{2,1,0:T(8,128)S(1)} %get-tuple-element.695, pred[192,512]{1,0:T(8,128)(4,1)S(1)} %and_and_fusion.7, bf16[192,4,8,128]{3,0,2,1:T(8,128)(2,1)} %get-tuple-element.694, pred[]{:T(512)S(6)} %compare.10, ...), kind=kOutput, calls=%fused_computation.30.clone.1 | convolution fusion | flops 1624768512 | bytes 9035777 | tf_op jit(solution)/shard_map/while/body/eval_jaxpr/gjrk,kgd->rgjd/dot_general | solution.py:75
  203.7 7.2 %bitcast_add_fusion.5 = f32[192,4,8,128]{3,0,2,1:T(8,128)} fusion(f32[192,4,8,128]{3,0,2,1:T(8,128)} %get-tuple-element.677, f32[4,8,192]{2,1,0:T(8,128)S(1)} %get-tuple-element.695, pred[192,512]{1,0:T(8,128)(4,1)S(1)} %and_and_fusion.7, bf16[192,4,8,128]{3,0,2,1:T(8,128)(2,1)} %get-tuple-element.694, pred[]{:T(512)S(6)} %compare.10, ...), kind=kOutput, calls=%fused_computation.30.clone.1 | convolution fusion | flops 1624768512 | bytes 9035777 | tf_op jit(solution)/shard_map/while/body/eval_jaxpr/gjrk,kgd->rgjd/dot_general | solution.py:75
  210.9 5.7 multiply_reduce_fusion
  216.8 123.5 %while.39 = (s32[]{:T(128)}, f32[192,4,8,128]{3,0,2,1:T(8,128)}, f32[4,512,2,4,128]{4,3,2,1,0:T(4,128)}, bf16[4,512,2,4,128]{4,1,3,2,0:T(8,128)(2,1)}, s32[192,1...) while((s32[]{:T(128)}, f32[192,4,8,128]{3,0,2,1:T(8,128)}, ...), condition=%wide.region_13.14_spmd.clone, body=%wide.region_12.13_spmd.clone.sunk | while | flops 4060741888 | bytes 121510808 | solution.py:126
  218.7 6.3 fusion.113
  225.1 7.6 %fusion.115 = f32[512,1,4,128]{3,0,2,1:T(8,128)S(1)} fusion(bf16[192,4,8,128]{3,0,2,1:T(8,128)(2,1)S(1)} %copy-done.6, f32[4,512,192,8]{1,2,3,0:T(8,128)} %fusion.113, f32[4,8,192]{2,1,0:T(8,128)S(1)} %get-tuple-element.735, pred[192,512]{1,0:T(8,128)(4,1)S(1)} %and_and_fusion.8), kind=kOutput, calls=%fused_computation.53.clone.1 | convolution fusion | flops 817889280 | bytes 15327232 | tf_op jit(solution)/shard_map/while/body/eval_jaxpr/gjrk,rgjd->kgd/dot_general | solution.py:121
  232.7 7.2 %fusion.114 = bf16[4,8,192,512]{3,2,1,0:T(8,128)(2,1)S(1)} fusion(f32[4,512,192,8]{1,2,3,0:T(8,128)} %fusion.113, f32[4,8,192]{2,1,0:T(8,128)S(1)} %get-tuple-element.737, f32[4,8,192]{2,1,0:T(8,128)S(1)} %get-tuple-element.735, pred[192,512]{1,0:T(8,128)(4,1)S(1)} %and_and_fusion.8, bf16[192,4,8,128]{3,0,2,1:T(8,128)(2,1)S(1)} %copy-done.6, ...), kind=kOutput, calls=%fused_computation.43.clone.1 | convolution fusion | flops 824180736 | bytes 21135360 | tf_op jit(solution)/shard_map/while/body/eval_jaxpr/rgjd,kgd->gjrk/dot_general | solution.py:110
  239.9 2.3 fusion.116
  242.3 2.7 bitcast_add_fusion.6
  245.1 2.7 copy_dynamic-update-slice_fusion.2
  249.6 6.3 fusion.113
  255.9 7.6 %fusion.115 = f32[512,1,4,128]{3,0,2,1:T(8,128)S(1)} fusion(bf16[192,4,8,128]{3,0,2,1:T(8,128)(2,1)S(1)} %copy-done.6, f32[4,512,192,8]{1,2,3,0:T(8,128)} %fusion.113, f32[4,8,192]{2,1,0:T(8,128)S(1)} %get-tuple-element.735, pred[192,512]{1,0:T(8,128)(4,1)S(1)} %and_and_fusion.8), kind=kOutput, calls=%fused_computation.53.clone.1 | convolution fusion | flops 817889280 | bytes 15327232 | tf_op jit(solution)/shard_map/while/body/eval_jaxpr/gjrk,rgjd->kgd/dot_general | solution.py:121
  263.5 7.2 %fusion.114 = bf16[4,8,192,512]{3,2,1,0:T(8,128)(2,1)S(1)} fusion(f32[4,512,192,8]{1,2,3,0:T(8,128)} %fusion.113, f32[4,8,192]{2,1,0:T(8,128)S(1)} %get-tuple-element.737, f32[4,8,192]{2,1,0:T(8,128)S(1)} %get-tuple-element.735, pred[192,512]{1,0:T(8,128)(4,1)S(1)} %and_and_fusion.8, bf16[192,4,8,128]{3,0,2,1:T(8,128)(2,1)S(1)} %copy-done.6, ...), kind=kOutput, calls=%fused_computation.43.clone.1 | convolution fusion | flops 824180736 | bytes 21135360 | tf_op jit(solution)/shard_map/while/body/eval_jaxpr/rgjd,kgd->gjrk/dot_general | solution.py:110
  270.7 2.3 fusion.116
  273.1 2.7 bitcast_add_fusion.6
  276.0 2.7 copy_dynamic-update-slice_fusion.2
  280.3 6.3 fusion.113
  286.7 7.6 %fusion.115 = f32[512,1,4,128]{3,0,2,1:T(8,128)S(1)} fusion(bf16[192,4,8,128]{3,0,2,1:T(8,128)(2,1)S(1)} %copy-done.6, f32[4,512,192,8]{1,2,3,0:T(8,128)} %fusion.113, f32[4,8,192]{2,1,0:T(8,128)S(1)} %get-tuple-element.735, pred[192,512]{1,0:T(8,128)(4,1)S(1)} %and_and_fusion.8), kind=kOutput, calls=%fused_computation.53.clone.1 | convolution fusion | flops 817889280 | bytes 15327232 | tf_op jit(solution)/shard_map/while/body/eval_jaxpr/gjrk,rgjd->kgd/dot_general | solution.py:121
  294.3 7.2 %fusion.114 = bf16[4,8,192,512]{3,2,1,0:T(8,128)(2,1)S(1)} fusion(f32[4,512,192,8]{1,2,3,0:T(8,128)} %fusion.113, f32[4,8,192]{2,1,0:T(8,128)S(1)} %get-tuple-element.737, f32[4,8,192]{2,1,0:T(8,128)S(1)} %get-tuple-element.735, pred[192,512]{1,0:T(8,128)(4,1)S(1)} %and_and_fusion.8, bf16[192,4,8,128]{3,0,2,1:T(8,128)(2,1)S(1)} %copy-done.6, ...), kind=kOutput, calls=%fused_computation.43.clone.1 | convolution fusion | flops 824180736 | bytes 21135360 | tf_op jit(solution)/shard_map/while/body/eval_jaxpr/rgjd,kgd->gjrk/dot_general | solution.py:110
  303.9 2.7 bitcast_add_fusion.6
  306.7 2.7 copy_dynamic-update-slice_fusion.2
  311.2 6.3 fusion.113
  317.5 7.6 %fusion.115 = f32[512,1,4,128]{3,0,2,1:T(8,128)S(1)} fusion(bf16[192,4,8,128]{3,0,2,1:T(8,128)(2,1)S(1)} %copy-done.6, f32[4,512,192,8]{1,2,3,0:T(8,128)} %fusion.113, f32[4,8,192]{2,1,0:T(8,128)S(1)} %get-tuple-element.735, pred[192,512]{1,0:T(8,128)(4,1)S(1)} %and_and_fusion.8), kind=kOutput, calls=%fused_computation.53.clone.1 | convolution fusion | flops 817889280 | bytes 15327232 | tf_op jit(solution)/shard_map/while/body/eval_jaxpr/gjrk,rgjd->kgd/dot_general | solution.py:121
  325.1 7.2 %fusion.114 = bf16[4,8,192,512]{3,2,1,0:T(8,128)(2,1)S(1)} fusion(f32[4,512,192,8]{1,2,3,0:T(8,128)} %fusion.113, f32[4,8,192]{2,1,0:T(8,128)S(1)} %get-tuple-element.737, f32[4,8,192]{2,1,0:T(8,128)S(1)} %get-tuple-element.735, pred[192,512]{1,0:T(8,128)(4,1)S(1)} %and_and_fusion.8, bf16[192,4,8,128]{3,0,2,1:T(8,128)(2,1)S(1)} %copy-done.6, ...), kind=kOutput, calls=%fused_computation.43.clone.1 | convolution fusion | flops 824180736 | bytes 21135360 | tf_op jit(solution)/shard_map/while/body/eval_jaxpr/rgjd,kgd->gjrk/dot_general | solution.py:110
  334.7 2.7 bitcast_add_fusion.6
  337.6 2.7 copy_dynamic-update-slice_fusion.2
  340.2 10.6 %reshape.133 = f32[2048,1024]{1,0:T(8,128)} reshape(f32[4,512,2,4,128]{4,3,2,1,0:T(4,128)} %get-tuple-element.169) | data formatting | bytes 16777216 | tf_op jit(solution)/shard_map/reshape | solution.py:131
  350.8 3.9 convert_element_type.51
  354.8 4.4 all-to-all-start.2
  363.7 3.9 convert_element_type.55
  367.6 14.8 %all-to-all-done.2 = bf16[16,12,4096]{2,1,0:T(8,128)(2,1)} async-done(((bf16[16,12,4096]{2,1,0:T(8,128)(2,1)}), bf16[16,12,4096]{2,1,0:T(8,128)(2,1)}, u32[]{:S(2)}, u32[]{:S(2)}) %all-to-all-start.2) | async-done | bytes 1572896 | tf_op jit(solution)/shard_map/all_to_all | solution.py:220
  382.5 7.5 %all-to-all-start.4 = ((bf16[16,12,4096]{2,1,0:T(8,128)(2,1)}), bf16[16,12,4096]{2,1,0:T(8,128)(2,1)}, u32[]{:S(2)}, u32[]{:S(2)}) async-start(bf16[16,12,4096]{2,1,0:T(8,128)(2,1)} %convert_element_type.55), calls=%async_computation.4 | async-start | bytes 4194304 | tf_op jit(solution)/shard_map/all_to_all | solution.py:227
  390.1 81.6 %reduce-scatter.2.cloned.1.call-done = f32[128,1024]{1,0:T(8,128)} async-done(((f32[2048,1024]{1,0:T(8,128)}), f32[128,1024]{1,0:T(8,128)}) %reduce-scatter.2.cloned.1.call-update) | async-done | bytes 524304 | tf_op jit(solution)/shard_map/reduce_scatter | solution.py:237
  475.5 3.6 reshape.129
  479.1 4.8 gather_fusion
  483.9 3.6 reshape.132
  487.5 4.8 gather_fusion.1
  492.9 6.4 fusion.58
  501.4 127.9 %all-reduce.3.cloned.1.call-done = (f32[8192,64]{0,1:T(8,128)}, f32[64,512]{1,0:T(8,128)}) async-done(((f32[8192,64]{0,1:T(8,128)}, f32[64,512]{1,0:T(8,128)}), (f32[8192,64]{0,1:T(8,128)}, f32[64,512]{1,0:T(8,128)})) %all-reduce.3.cloned.1.call-update) | async-done | bytes 2228240 | tf_op jit(solution)/shard_map/psum | solution.py:253
  629.3 3.1 copy.90
  (189 shorter events, 53.6 us)
Async XLA Ops:
  7.2 1.6 copy-start
  7.2 124.9 %all-gather.3.cloned.1.call-start = ((), (), s32[]{:S(2)}) async-start(), calls=%async_computation.7 | async-start | bytes 4456448 | tf_op jit(solution)/shard_map/all_gather | solution.py:160
  10.8 4.8 copy-start.9
  10.8 4.8 copy-start.13
  10.9 5.0 copy-start.12
  10.9 5.8 copy-start.17
  10.9 5.9 copy-start.16
  10.9 16.5 %copy-start.7 = (bf16[1,128,4096]{2,1,0:T(8,128)(2,1)S(1)}, bf16[1,128,4096]{2,1,0:T(8,128)(2,1)}, u32[]{:S(2)}) copy-start(bf16[1,128,4096]{2,1,0:T(8,128)(2,1)} %param.16) | copy-start | bytes 3145732
  17.3 23.7 %copy-start.18 = (s32[128]{0:T(128)}, s32[128]{0:T(128)S(1)}, u32[]{:S(2)}) copy-start(s32[128]{0:T(128)S(1)} %fusion.63) | copy-start | bytes 1540
  19.0 15.3 %all-to-all-start = ((s32[16,12,2]{1,2,0:T(2,128)}), s32[16,12,2]{1,2,0:T(2,128)S(1)}, u32[]{:S(2)}, u32[]{:S(2)}) async-start(s32[16,12,2]{1,2,0:T(2,128)} %copy.34), calls=%async_computation | async-start | bytes 32768 | tf_op jit(solution)/shard_map/all_to_all | solution.py:194
  30.7 10.3 %copy-start.8 = (bf16[1,128,4096]{2,1,0:T(8,128)(2,1)S(1)}, bf16[1,128,4096]{2,1,0:T(8,128)(2,1)}, u32[]{:S(2)}) copy-start(bf16[1,128,4096]{2,1,0:T(8,128)(2,1)} %param.21) | copy-start | bytes 3145732
  34.2 41.0 %all-to-all-start.1 = ((bf16[16,12,4096]{2,1,0:T(8,128)(2,1)}), bf16[16,12,4096]{2,1,0:T(8,128)(2,1)}, u32[]{:S(2)}, u32[]{:S(2)}) async-start(bf16[16,12,4096]{2,1,0:T(8,128)(2,1)} %reshape.127), calls=%async_computation.1 | async-start | bytes 4194304 | tf_op jit(solution)/shard_map/all_to_all | solution.py:180
  75.2 49.9 %all-to-all-start.3 = ((bf16[16,12,4096]{2,1,0:T(8,128)(2,1)}), bf16[16,12,4096]{2,1,0:T(8,128)(2,1)}, u32[]{:S(2)}, u32[]{:S(2)}) async-start(bf16[16,12,4096]{2,1,0:T(8,128)(2,1)} %reshape.130), calls=%async_computation.3 | async-start | bytes 4194304 | tf_op jit(solution)/shard_map/all_to_all | solution.py:187
  82.4 389.2 %reduce-scatter.2.cloned.1.call-start = ((), (), s32[]{:S(2)}) async-start(), calls=%async_computation.6 | async-start | bytes 8912896 | tf_op jit(solution)/shard_map/reduce_scatter | solution.py:237
  145.1 1.7 copy-start.1
  152.9 1.7 copy-start.1
  160.8 1.7 copy-start.1
  168.7 1.7 copy-start.1
  217.0 1.7 copy-start.2
  218.7 6.3 copy-start.6
  239.9 2.4 copy-start.3
  245.0 2.9 copy-start.4
  247.8 1.7 copy-start.2
  249.6 6.3 copy-start.6
  270.7 2.4 copy-start.3
  275.8 2.8 copy-start.4
  278.6 1.7 copy-start.2
  280.3 6.3 copy-start.6
  301.5 2.4 copy-start.3
  306.6 2.9 copy-start.4
  309.4 1.7 copy-start.2
  311.2 6.3 copy-start.6
  332.3 2.4 copy-start.3
  337.4 2.8 copy-start.4
  340.2 10.6 %copy-start.15 = (f32[4,8,192]{2,1,0:T(8,128)}, f32[4,8,192]{2,1,0:T(8,128)S(1)}, u32[]{:S(2)}) copy-start(f32[4,8,192]{2,1,0:T(8,128)S(1)} %get-tuple-element.787) | copy-start | bytes 73732
  354.8 27.7 %all-to-all-start.2 = ((bf16[16,12,4096]{2,1,0:T(8,128)(2,1)}), bf16[16,12,4096]{2,1,0:T(8,128)(2,1)}, u32[]{:S(2)}, u32[]{:S(2)}) async-start(bf16[16,12,4096]{2,1,0:T(8,128)(2,1)} %convert_element_type.51), calls=%async_computation.2 | async-start | bytes 4194304 | tf_op jit(solution)/shard_map/all_to_all | solution.py:220
  367.6 105.1 %copy-start.14 = (bf16[64,512]{1,0:T(8,128)(2,1)S(1)}, bf16[64,512]{1,0:T(8,128)(2,1)}, u32[]{:S(2)}) copy-start(bf16[64,512]{1,0:T(8,128)(2,1)} %param.20) | copy-start | bytes 196612
  367.6 105.3 %copy-start.10 = (bf16[128,64]{0,1:T(8,128)(2,1)S(1)}, bf16[128,64]{0,1:T(8,128)(2,1)}, u32[]{:S(2)}) copy-start(bf16[128,64]{0,1:T(8,128)(2,1)} %copy-done.9) | copy-start | bytes 49156
  382.5 101.4 %all-to-all-start.4 = ((bf16[16,12,4096]{2,1,0:T(8,128)(2,1)}), bf16[16,12,4096]{2,1,0:T(8,128)(2,1)}, u32[]{:S(2)}, u32[]{:S(2)}) async-start(bf16[16,12,4096]{2,1,0:T(8,128)(2,1)} %convert_element_type.55), calls=%async_computation.4 | async-start | bytes 4194304 | tf_op jit(solution)/shard_map/all_to_all | solution.py:227
  390.0 239.3 %all-reduce.3.cloned.1.call-start = ((), (), s32[]{:S(2)}) async-start(), calls=%async_computation.8 | async-start | bytes 4456448 | tf_op jit(solution)/shard_map/psum | solution.py:253
  473.7 1.8 copy-start.19
  492.9 6.4 copy-start.5
  629.3 3.1 copy-start.11
Sparse Core Ops, SparseCore 0:
  16.8 69.5 all-gather.2
  351.0 120.6 reduce-scatter.1
  477.2 152.0 all-reduce.2
where the time goes:
time: 648 us; the launch traced here: 640 us
  waiting for transfers between devices  252 us (39%)
  matrix products  160 us (25%)
  local copies, waits for them, and re-layouts  115 us (18%)
  starting transfers between devices  34.5 us (5%)
  blocking collectives  34 us (5%)
  other arithmetic  29.3 us (5%)
  between operations  14.6 us (2%)
    psum x1, waiting for transfers between devices, local(): lax.psum((down_gradient_total, up_gradient_total), ('dp', 'ctx'))  128 us
    reduce_scatter x1, waiting for transfers between devices, local(): lax.psum_scatter(key_grads, 'ctx', scatter_dimension=0, tiled=True)  81.6 us
    all_gather x1, blocking collectives, local(): lax.all_gather(document_index, 'ctx', axis=1, tiled=True)  34 us
    dot_general x8, matrix products, head_scores(): jnp.einsum('rgjd,kgd->gjrk', query_heads, key_part, preferred_element_typ...  33.8 us
    dot_general x4, matrix products, back_step(): jnp.einsum('gjrk,rgjd->kgd', weights, grad_heads, preferred_element_type=...  30.4 us
    dot_general x4, matrix products, back_step(): jnp.einsum('rgjd,kgd->gjrk', grad_heads, key_block[:, 1], preferred_eleme...  28.9 us
    dot_general x4, matrix products, value_step(): jnp.einsum('gjrk,kgd->rgjd', weights, key_block[:, 1], preferred_element_...  28.4 us
    all_to_all x1, waiting for transfers between devices, local(): lax.all_to_all(send_queries.reshape(peer_count, CAP, query_width), 'ctx',...  27.4 us
  transfers between devices with their start and end apart: 8, of which 4 were waited for; matrix products, arithmetic and copies ran while one was open for 11% of the time, Pallas kernels for 0%

commit v1 on v0

v1 whole, which is shorter than its diff:
```python
import functools
import math

import jax
import jax.numpy as jnp
from jax import lax
from jax.experimental import pallas as pl
from jax.experimental.pallas import tpu as pltpu
from jax.sharding import PartitionSpec as P

HEAD = 128
HQ = 32
GROUPS = 4
PER_GROUP = HQ // GROUPS
PAIRS = PER_GROUP // 2
CAP = 12
TOK = 128
REACH = 8
BLOCKS = REACH + 1
KEYS = BLOCKS * TOK
DOC_ROWS = 16
PACK = TOK + DOC_ROWS
KV = GROUPS * HEAD
ADAPTER_SCALE = 0.5
INV_ROOT = 1.0 / math.sqrt(HEAD)
LOG2E = 1.4426950408889634
LN2 = 0.6931471805599453
MASKED = -1e30
VMEM = 56 << 20
BF = jnp.bfloat16
F32 = jnp.float32
NT = (((1,), (1,)), ((), ()))
NN = (((1,), (0,)), ((), ()))


def dot(a, b, dims=NN):
    return lax.dot_general(a, b, dims, preferred_element_type=F32)


def window_part(own, pairs, distance):
    if distance % 4 == 0:
        return own[distance // 4]
    return pairs[distance % 4 - 1].at[distance // 4]


def fill_bias(here, parts, docs_own, bias):
    own = docs_own.astype(F32)
    real = [jnp.where(here - REACH + k >= 0, 1.0, 0.0) for k in range(BLOCKS)]
    docs = [parts[k][pl.ds(TOK, DOC_ROWS), :].astype(F32) for k in range(BLOCKS)]
    missing = jnp.maximum(REACH - here, 0) * TOK
    start = jnp.zeros((1, TOK), F32)
    for number in (1, 2, 3):
        lower = jnp.zeros((DOC_ROWS, TOK), F32)
        for k in range(BLOCKS):
            lower = lower + jnp.where(docs[k] < number, real[k], 0.0)
        start = jnp.where(own == number, jnp.sum(lower) / DOC_ROWS, start)
    first = start.astype(jnp.int32) + missing
    lane = lax.broadcasted_iota(jnp.int32, (TOK, TOK), 1)
    row = lax.broadcasted_iota(jnp.int32, (TOK, TOK), 0)
    for k in range(BLOCKS):
        spot = row + k * TOK
        seen = (spot >= first) & (spot <= REACH * TOK + lane)
        bias[pl.ds(k * TOK, TOK), :] = jnp.where(seen, 0.0, MASKED)


def pair_rows(ref, pair):
    return jnp.concatenate(
        [ref[:, (2 * pair + n) * HEAD : (2 * pair + n + 1) * HEAD] for n in range(2)], axis=0
    )


def block(k):
    return pl.ds(k * TOK, TOK)


def fold(x, op):
    return op(x.reshape(TOK // 8, 8, 2 * TOK), axis=0)


def scores_kernel(here_ref, docs_ref, owners_ref, q_ref, g_ref, *rest):
    key_own, key_pairs = rest[:3], rest[3:6]
    lse_ref, slots_ref, *outs = rest[6:12]
    bias, scores, weights, lse_all = rest[12:]
    group = pl.program_id(0)
    here = here_ref[0]
    parts = [window_part(key_own, key_pairs, REACH - k) for k in range(BLOCKS)]

    @pl.when(group == 0)
    def _():
        fill_bias(here, parts, docs_ref[...], bias)

    keys = [part[pl.ds(0, TOK), :] for part in parts]
    for pair in range(PAIRS):
        q2 = pair_rows(q_ref, pair)
        peak = jnp.full((8, 2 * TOK), MASKED, F32)
        for k in range(BLOCKS):
            b = bias[block(k), :]
            t = dot(keys[k], q2, NT) * (INV_ROOT * LOG2E) + jnp.concatenate(
                [b, b], axis=1
            )
            scores[block(k), :] = t
            peak = jnp.maximum(peak, fold(t, jnp.max))
        peak = jnp.max(peak, axis=0, keepdims=True)
        total = jnp.zeros((8, 2 * TOK), F32)
        for k in range(BLOCKS):
            total = total + fold(jnp.exp2(scores[block(k), :] - peak), jnp.sum)
        lse2 = peak + jnp.log2(jnp.sum(total, axis=0, keepdims=True))
        for n in range(2):
            lse = lse2[:, n * TOK : (n + 1) * TOK] * LN2
            lse_ref[0, 2 * pair + n : 2 * pair + n + 1, :] = lse
            lse_all[pl.ds(group * PER_GROUP + 2 * pair + n, 1), :] = lse
        for k in range(BLOCKS):
            weights[block(k), pl.ds(pair * 2 * TOK, 2 * TOK)] = jnp.exp2(
                scores[block(k), :] - lse2
            ).astype(BF)
    rows = jnp.concatenate([pair_rows(g_ref, pair) for pair in range(PAIRS)], axis=0)
    for k in range(BLOCKS):
        put_partial(outs, REACH - k, dot(weights[block(k), :], rows).astype(BF))

    @pl.when(group == GROUPS - 1)
    def _():
        put_slots(owners_ref[...], lse_all[...], slots_ref)


def put_slots(owners, lse, slots_ref):
    peers = slots_ref.shape[0]
    named = lax.broadcasted_iota(jnp.int32, (peers, TOK), 0) == owners
    onehot = jnp.where(named, 1.0, 0.0)
    before = lax.broadcasted_iota(jnp.int32, (TOK, TOK), 0) < lax.broadcasted_iota(
        jnp.int32, (TOK, TOK), 1
    )
    earlier = dot(onehot.astype(BF), jnp.where(before, 1.0, 0.0).astype(BF))
    for slot in range(CAP):
        place = jnp.where(named & (earlier == slot), 1.0, 0.0)
        slots_ref[:, slot * HQ : (slot + 1) * HQ] = lax.dot_general(
            place, lse, NT, precision=lax.Precision.HIGHEST, preferred_element_type=F32
        )


def put_partial(outs, distance, value):
    if distance % 4 == 0:
        outs[0][distance // 4] = value
    else:
        outs[4 - distance % 4][distance // 4] = value


def grads_kernel(here_ref, docs_ref, q_ref, g_ref, lse_ref, *rest):
    key_own, key_pairs, value_own, value_pairs = rest[:3], rest[3:6], rest[6:9], rest[9:12]
    out_ref, dq_ref, *outs = rest[12:18]
    bias, keys_t, values_t, weights32, weights, d_scores = rest[18:]
    group = pl.program_id(0)
    here = here_ref[0]
    parts = [window_part(key_own, key_pairs, REACH - k) for k in range(BLOCKS)]

    @pl.when(group == 0)
    def _():
        fill_bias(here, parts, docs_ref[...], bias)

    keys = [part[pl.ds(0, TOK), :] for part in parts]
    values = [window_part(value_own, value_pairs, REACH - k)[...] for k in range(BLOCKS)]
    for k in range(BLOCKS):
        keys_t[:, block(k)] = keys[k].astype(F32).T.astype(BF)
        values_t[:, block(k)] = values[k].astype(F32).T.astype(BF)
    for pair in range(PAIRS):
        q2 = pair_rows(q_ref, pair)
        g2 = pair_rows(g_ref, pair)
        lse2 = (
            jnp.concatenate(
                [lse_ref[0, 2 * pair + n : 2 * pair + n + 1, :] for n in range(2)], axis=1
            )
            * LOG2E
        )
        for k in range(BLOCKS):
            b = bias[block(k), :]
            t = dot(keys[k], q2, NT) * (INV_ROOT * LOG2E) + jnp.concatenate(
                [b, b], axis=1
            )
            w = jnp.exp2(t - lse2)
            weights32[block(k), :] = w
            weights[block(k), :] = w.astype(BF)
        out_t = dot(values_t[...], weights[...]).astype(BF).astype(F32)
        g2_t = jnp.concatenate(
            [g2[n * TOK : (n + 1) * TOK].astype(F32).T for n in range(2)], axis=1
        )
        delta = jnp.sum(out_t * g2_t, axis=0, keepdims=True)
        for k in range(BLOCKS):
            d_prob = dot(values[k], g2, NT)
            d_scores[block(k), pl.ds(pair * 2 * TOK, 2 * TOK)] = (
                weights32[block(k), :] * (d_prob - delta)
            ).astype(BF)
        dq_t = dot(keys_t[...], d_scores[:, pl.ds(pair * 2 * TOK, 2 * TOK)]) * INV_ROOT
        for n in range(2):
            head = slice((2 * pair + n) * HEAD, (2 * pair + n + 1) * HEAD)
            out_ref[:, head] = out_t[:, n * TOK : (n + 1) * TOK].T.astype(BF)
            dq_ref[:, head] = dq_t[:, n * TOK : (n + 1) * TOK].T.astype(BF)
    rows = jnp.concatenate([pair_rows(q_ref, pair) for pair in range(PAIRS)], axis=0)
    for k in range(BLOCKS):
        put_partial(
            outs, REACH - k, (dot(d_scores[block(k), :], rows) * INV_ROOT).astype(BF)
        )


def smem():
    return pl.BlockSpec(memory_space=pltpu.SMEM)


def partial_outs():
    shapes = [jax.ShapeDtypeStruct((n, TOK, KV), BF) for n in (3, 2, 2, 2)]
    specs = [pl.BlockSpec((n, TOK, HEAD), lambda g: (0, 0, g)) for n in (3, 2, 2, 2)]
    return shapes, specs


def part_specs(rows):
    own = pl.BlockSpec((rows, HEAD), lambda g: (0, g))
    pair = pl.BlockSpec((2, rows, HEAD), lambda g: (0, 0, g))
    return [own] * 3 + [pair] * 3


def run_scores(here, docs_own, owners, queries, grads, keys):
    shapes, specs = partial_outs()
    wide = pl.BlockSpec((TOK, PER_GROUP * HEAD), lambda g: (0, g))
    line = pl.BlockSpec((1, TOK), lambda g: (0, 0))
    return pl.pallas_call(
        scores_kernel,
        grid=(GROUPS,),
        in_specs=[smem(), line, line, wide, wide] + part_specs(PACK),
        out_specs=[
            pl.BlockSpec((1, PER_GROUP, TOK), lambda g: (g, 0, 0)),
            pl.BlockSpec((16, CAP * HQ), lambda g: (0, 0)),
        ]
        + specs,
        out_shape=[
            jax.ShapeDtypeStruct((GROUPS, PER_GROUP, TOK), F32),
            jax.ShapeDtypeStruct((16, CAP * HQ), F32),
        ]
        + shapes,
        scratch_shapes=[
            pltpu.VMEM((KEYS, TOK), F32),
            pltpu.VMEM((KEYS, 2 * TOK), F32),
            pltpu.VMEM((KEYS, PER_GROUP * TOK), BF),
            pltpu.VMEM((HQ, TOK), F32),
        ],
        compiler_params=pltpu.CompilerParams(
            vmem_limit_bytes=VMEM, dimension_semantics=("arbitrary",)
        ),
        cost_estimate=pl.CostEstimate(
            flops=2 * 2 * HQ * TOK * KEYS * HEAD, bytes_accessed=6 << 20, transcendentals=2 * HQ * TOK * KEYS
        ),
        name="scores",
    )(here, docs_own, owners, queries, grads, *keys)


def run_grads(here, docs_own, queries, grads, lse, keys, values):
    shapes, specs = partial_outs()
    wide = pl.BlockSpec((TOK, PER_GROUP * HEAD), lambda g: (0, g))
    return pl.pallas_call(
        grads_kernel,
        grid=(GROUPS,),
        in_specs=[
            smem(),
            pl.BlockSpec((1, TOK), lambda g: (0, 0)),
            wide,
            wide,
            pl.BlockSpec((1, PER_GROUP, TOK), lambda g: (g, 0, 0)),
        ]
        + part_specs(PACK)
        + part_specs(TOK),
        out_specs=[wide, wide] + specs,
        out_shape=[jax.ShapeDtypeStruct((TOK, HQ * HEAD), BF)] * 2 + shapes,
        scratch_shapes=[
            pltpu.VMEM((KEYS, TOK), F32),
            pltpu.VMEM((HEAD, KEYS), BF),
            pltpu.VMEM((HEAD, KEYS), BF),
            pltpu.VMEM((KEYS, 2 * TOK), F32),
            pltpu.VMEM((KEYS, 2 * TOK), BF),
            pltpu.VMEM((KEYS, PER_GROUP * TOK), BF),
        ],
        compiler_params=pltpu.CompilerParams(
            vmem_limit_bytes=VMEM, dimension_semantics=("arbitrary",)
        ),
        cost_estimate=pl.CostEstimate(
            flops=5 * 2 * HQ * TOK * KEYS * HEAD, bytes_accessed=8 << 20, transcendentals=HQ * TOK * KEYS
        ),
        name="grads",
    )(here, docs_own, queries, grads, lse, *keys, *values)


def along_z(x, step):
    return lax.ppermute(x, "ctx", [(i, i // 4 * 4 + (i + step) % 4) for i in range(16)])


def along_x(x, step):
    return lax.ppermute(x, "ctx", [(i, (i + 4 * step) % 16) for i in range(16)])


def along_y(x, step):
    return lax.ppermute(x, "dp", [(i, (i + 2 * step) % 8) for i in range(8)])


def other_core(x):
    return lax.ppermute(x, "dp", [(i, i ^ 1) for i in range(8)])


def from_rows(x):
    return [x, along_x(x, 1), along_x(x, 2)]


def from_peers(own, z):
    late = jnp.stack(own[1:])
    early = jnp.stack(own[:2])
    return [along_z(jnp.where(z + e > 3, late, early), e) for e in (1, 2, 3)]


def sum_of_four(x, move):
    near = move(x, 1).astype(F32) + move(x, 3).astype(F32)
    return ((x.astype(F32) + move(x, 2).astype(F32)) + near).astype(BF)


def collect(own, to_peer, z):
    here_row = own[0].astype(F32)
    row_1 = own[1].astype(F32)
    row_2 = own[2].astype(F32)
    for e in (1, 2, 3):
        got = along_z(to_peer[e - 1], e)
        near, far = got[0].astype(F32), got[1].astype(F32)
        wrapped = e > z
        here_row = here_row + jnp.where(wrapped, near, 0.0)
        row_1 = row_1 + jnp.where(wrapped, far, near)
        row_2 = row_2 + jnp.where(wrapped, 0.0, far)
    from_1 = along_x(row_1.astype(BF), -1)
    from_2 = along_x(row_2.astype(BF), -2)
    return here_row + from_1.astype(F32) + from_2.astype(F32)


def local(
    normed,
    queries,
    rotated_keys,
    value_weight,
    adapter_down,
    adapter_up,
    attention_cotangent,
    document_index,
    owner_routing,
):
    ctx = lax.axis_index("ctx")
    dp = lax.axis_index("dp")
    z, y, core = ctx % 4, dp // 2, dp % 2
    rows = normed[0]
    low_rank = dot(rows, adapter_down).astype(BF)
    values = (dot(rows, value_weight) + ADAPTER_SCALE * dot(low_rank, adapter_up)).astype(BF)
    doc_rows = jnp.broadcast_to(
        jnp.tile(document_index.astype(BF), (1, KV // TOK)), (DOC_ROWS, KV)
    )
    key_own = from_rows(jnp.concatenate([rotated_keys[0], doc_rows], axis=0))
    value_own = from_rows(values)
    key_parts = key_own + from_peers(key_own, z)
    value_parts = value_own + from_peers(value_own, z)
    here = ctx.reshape(1)
    lse, send_lse, *dv_parts = run_scores(
        here,
        document_index,
        owner_routing.reshape(1, TOK),
        queries[0],
        attention_cotangent[0],
        key_parts,
    )
    value_grad = collect(dv_parts[0], dv_parts[1:], z).astype(BF)
    out, dq, *dk_parts = run_grads(
        here, document_index, queries[0], attention_cotangent[0], lse, key_parts, value_parts
    )

    peers = lax.axis_size("ctx")
    lse_rows = lax.all_to_all(
        send_lse.reshape(peers, 1, CAP * HQ), "ctx", split_axis=0, concat_axis=0, tiled=True
    ).reshape(peers * CAP, HQ)

    middle = (ADAPTER_SCALE * dot(value_grad, adapter_up, NT)).astype(BF)
    tn = (((0,), (0,)), ((), ()))
    down_part = dot(middle, rows, tn).astype(BF)
    up_part = (ADAPTER_SCALE * dot(low_rank, value_grad, tn)).astype(BF)
    both = jnp.concatenate([down_part, up_part], axis=1)
    width = both.shape[1]
    half = both.shape[0] // 2
    keep = lax.dynamic_slice(both, (core * half, 0), (half, width))
    send = lax.dynamic_slice(both, ((1 - core) * half, 0), (half, width))
    summed = (keep.astype(F32) + other_core(send).astype(F32)).astype(BF)
    part = width // 4

    def quarter(x, n):
        return lax.dynamic_slice(x, (0, (n % 4) * part), (half, part))

    mine = quarter(summed, y).astype(F32)
    for e in (1, 2, 3):
        mine = mine + along_y(quarter(summed, y + e), e).astype(F32)
    mine = sum_of_four(sum_of_four(mine.astype(BF), along_x), along_z)
    whole = jnp.zeros((half, width), BF)
    for e in range(4):
        got = along_y(mine, e) if e else mine
        whole = lax.dynamic_update_slice(whole, got, (0, ((y - e) % 4) * part))
    other = other_core(whole)
    total = jnp.concatenate(
        [jnp.where(core == 0, whole, other), jnp.where(core == 0, other, whole)], axis=0
    ).astype(F32)
    model = rows.shape[1]
    total_down = total[:, :model].T
    total_up = total[:, model:]

    normed_input_gradient = (dot(value_grad, value_weight, NT) + dot(middle, adapter_down, NT)).astype(BF)
    d_key = collect(dk_parts[0], dk_parts[1:], z).astype(BF)
    return (
        out[None],
        dq[None],
        d_key[None],
        normed_input_gradient[None],
        total_down,
        total_up,
        lse_rows[None],
    )


def solution(mesh):
    tokens = P("dp", "ctx", None)
    return jax.shard_map(
        local,
        mesh=mesh,
        in_specs=(tokens, tokens, tokens, P(), P(), P(), tokens, P("dp", "ctx"), tokens),
        out_specs=(tokens, tokens, tokens, tokens, P(), P(), tokens),
        check_vma=False,
    )
```

time: 648 us -> 186 us (0.29); the launches traced: 640 us -> 185 us
  waiting for transfers between devices: 252 us -> 57.6 us
  matrix products: 160 us -> 16.1 us
  local copies, waits for them, and re-layouts: 115 us -> 8.24 us
  blocking collectives: 34 us -> 0 us
  Pallas kernels: 0 us -> 31.3 us
  starting transfers between devices: 34.5 us -> 55.3 us
  between operations: 14.6 us -> 0.86 us
  other arithmetic: 29.3 us -> 15.8 us
    dot_general x36 -> x8, matrix products: 160 us -> 16.1 us  [dot(): return lax.dot_general(a, b, dims, preferred_element_type=F32)]
    psum x1 -> x0, waiting for transfers between devices: 128 us -> none  [local(): lax.psum((down_gradient_total, up_gradient_total), ('dp', 'ctx'))]
    reduce_scatter x1 -> x0, waiting for transfers between devices: 81.6 us -> none  [local(): lax.psum_scatter(key_grads, 'ctx', scatter_dimension=0, tiled=True)]
    ppermute x0 -> x34, waiting for transfers between devices: none -> 57.6 us  [the longest x15 36 us: along_z(): lax.ppermute(x, 'ctx', [(i, i // 4 * 4 + (i + step) % 4) for i in range(1...]
    ppermute x0 -> x34, starting transfers between devices: none -> 51 us  [the longest x15 17.2 us: along_z(): lax.ppermute(x, 'ctx', [(i, i // 4 * 4 + (i + step) % 4) for i in range(1...]
    all_to_all x5 -> x1, waiting for transfers between devices: 42.3 us -> 0.01 us  [local(): lax.all_to_all(send_lse.reshape(peers, 1, CAP * HQ), 'ctx', split_axis=0,...]
    all_gather x1 -> x0, blocking collectives: 34 us -> none  [local(): lax.all_gather(document_index, 'ctx', axis=1, tiled=True)]
    reshape x10 -> x1, local copies, waits for them, and re-layouts: 33.2 us -> 0.63 us  [local(): send_lse.reshape(peers, 1, CAP * HQ)]
  transfers between devices with their start and end apart: 8 -> 35, of which waited for: 4 -> 16; matrix products, arithmetic and copies ran while one was open for 11% -> 15% of each run, Pallas kernels for 0% -> 10%
where the time goes in v1:
time: 186 us; the launch traced here: 185 us
  waiting for transfers between devices  57.6 us (31%)
  starting transfers between devices  55.3 us (30%)
  Pallas kernels  31.3 us (17%)
  matrix products  16.1 us (9%)
  other arithmetic  15.8 us (8%)
  local copies, waits for them, and re-layouts  8.24 us (4%)
    ppermute x15, waiting for transfers between devices, along_z(): lax.ppermute(x, 'ctx', [(i, i // 4 * 4 + (i + step) % 4) for i in range(1...  36 us
    pallas_call x1, Pallas kernels, run_grads(): pl.pallas_call(grads_kernel, grid=(GROUPS,), in_specs=[smem(), pl.BlockSp...  17.8 us
    ppermute x11, waiting for transfers between devices, along_x(): return lax.ppermute(x, 'ctx', [(i, (i + 4 * step) % 16) for i in range(16)])  17.8 us
    ppermute x15, starting transfers between devices, along_z(): lax.ppermute(x, 'ctx', [(i, i // 4 * 4 + (i + step) % 4) for i in range(1...  17.2 us
    dot_general x8, matrix products, dot(): return lax.dot_general(a, b, dims, preferred_element_type=F32)  16.1 us
    ppermute x11, starting transfers between devices, along_x(): return lax.ppermute(x, 'ctx', [(i, (i + 4 * step) % 16) for i in range(16)])  14 us
    pallas_call x1, Pallas kernels, run_scores(): pl.pallas_call(scores_kernel, grid=(GROUPS,), in_specs=[smem(), line, lin...  13.5 us
    ppermute x2, starting transfers between devices, other_core(): return lax.ppermute(x, 'dp', [(i, i ^ 1) for i in range(8)])  10.4 us
  transfers between devices with their start and end apart: 35, of which 16 were waited for; matrix products, arithmetic and copies ran while one was open for 15% of the time, Pallas kernels for 10%

profile of v1, /device:TPU:1, one launch (start us, length us, event | category | flops | bytes accessed | tf_op | source)
XLA Modules:
  0.0 185.4 jit_solution(589243616933027137)
XLA Ops:
  0.6 0.8 convert_bitcast_fusion
  1.5 0.9 fusion.51
  2.4 2.1 %collective-permute-start = (bf16[144,512]{1,0:T(8,128)(2,1)S(1)}, bf16[144,512]{1,0:T(8,128)(2,1)S(1)}, u32[]{:S(2)}, u32[]{:S(2)}) collective-permute-start(bf16[144,512]{1,0:T(8,128)(2,1)S(1)} %get-tuple-element.70.rest_0_), channel_id=1, source_target_pairs={{0,4},{1,5},{2,6},{3,7},{4,8},{5,9},{6,10},{7,11},{8,12},{9,13},{1... | collective-permute-start | bytes 442376 | tf_op jit(solution)/shard_map/ppermute | solution.py:293
  4.5 2.5 %collective-permute-start.1 = (bf16[144,512]{1,0:T(8,128)(2,1)S(1)}, bf16[144,512]{1,0:T(8,128)(2,1)S(1)}, u32[]{:S(2)}, u32[]{:S(2)}) collective-permute-start(bf16[144,512]{1,0:T(8,128)(2,1)S(1)} %get-tuple-element.70.rest_0_), channel_id=1, source_target_pairs={{0,8},{1,9},{2,10},{3,11},{4,12},{5,13},{6,14},{7,15},{8,0},{9,1},... | collective-permute-start | bytes 442376 | tf_op jit(solution)/shard_map/ppermute | solution.py:293
  7.0 1.9 %collective-permute-done.rest_1_ = bf16[144,512]{1,0:T(8,128)(2,1)S(1)} collective-permute-done((bf16[144,512]{1,0:T(8,128)(2,1)S(1)}, bf16[144,512]{1,0:T(8,128)(2,1)S(1)}, u32[]{:S(2)}, u32[]{:S(2)}) %collective-permute-start) | collective-permute-done | bytes 147488 | tf_op jit(solution)/shard_map/ppermute | solution.py:293
  8.9 4.5 %collective-permute-done.1.rest_2_ = bf16[144,512]{1,0:T(8,128)(2,1)S(1)} collective-permute-done((bf16[144,512]{1,0:T(8,128)(2,1)S(1)}, bf16[144,512]{1,0:T(8,128)(2,1)S(1)}, u32[]{:S(2)}, u32[]{:S(2)}) %collective-permute-start.1) | collective-permute-done | bytes 147488 | tf_op jit(solution)/shard_map/ppermute | solution.py:293
  13.4 1.7 collective-permute-start.2
  15.2 3.3 %collective-permute-start.3 = (bf16[2,144,512]{2,1,0:T(8,128)(2,1)S(1)}, bf16[2,144,512]{2,1,0:T(8,128)(2,1)S(1)}, u32[]{:S(2)}, u32[]{:S(2)}) collective-permute-start(bf16[2,144,512]{2,1,0:T(8,128)(2,1)S(1)} %get-tuple-element.65), channel_id=1, source_target_pairs={{0,2},{1,3},{2,0},{3,1},{4,6},{5,7},{6,4},{7,5},{8,10},{9,11},{10,... | collective-permute-start | bytes 884744 | tf_op jit(solution)/shard_map/ppermute | solution.py:289
  18.5 0.7 collective-permute-start.4
  19.2 3.9 %collective-permute-done.2.rest_3_ = bf16[2,144,512]{2,1,0:T(8,128)(2,1)S(1)} collective-permute-done((bf16[2,144,512]{2,1,0:T(8,128)(2,1)S(1)}, bf16[2,144,512]{2,1,0:T(8,128)(2,1)S(1)}, u32[]{:S(2)}, u32[]{:S(2)}) %collective-permute-start.2) | collective-permute-done | bytes 294944 | tf_op jit(solution)/shard_map/ppermute | solution.py:289
  23.0 7.2 %collective-permute-done.3.rest_4_ = bf16[2,144,512]{2,1,0:T(8,128)(2,1)S(1)} collective-permute-done((bf16[2,144,512]{2,1,0:T(8,128)(2,1)S(1)}, bf16[2,144,512]{2,1,0:T(8,128)(2,1)S(1)}, u32[]{:S(2)}, u32[]{:S(2)}) %collective-permute-start.3) | collective-permute-done | bytes 294944 | tf_op jit(solution)/shard_map/ppermute | solution.py:289
  31.4 13.5 %scores.1 = (f32[4,8,128]{2,1,0:T(8,128)}, f32[16,384]{1,0:T(8,128)}, bf16[3,128,512]{2,1,0:T(8,128)(2,1)}, bf16[2,128,512]{2,1,0:T(8,128)(2,1)}, bf16[2,128,512...) custom-call(s32[1]{0:T(128)} %bitcast.here_ref, s32[1,128]{1,0:T(1,128)} %docs_ref.3, s32[1,128]{1,0:T(1,128)} %bitcast.82, ...), custom_call_target="tpu_custom_call" | custom-call | flops 2415919104 | bytes 6291456 | tf_op jit(solution)/shard_map/scores/pallas_call | solution.py:223
  44.9 3.5 %collective-permute-start.17 = (bf16[2,128,512]{2,1,0:T(8,128)(2,1)}, bf16[2,128,512]{2,1,0:T(8,128)(2,1)S(1)}, u32[]{:S(2)}, u32[]{:S(2)}) collective-permute-start(bf16[2,128,512]{2,1,0:T(8,128)(2,1)} %get-tuple-element.29), channel_id=1, source_target_pairs={{0,3},{1,0},{2,1},{3,2},{4,7},{5,4},{6,5},{7,6},{8,11},{9,8},{10,9... | collective-permute-start | bytes 786440 | tf_op jit(solution)/shard_map/ppermute | solution.py:289
  49.1 10.3 %collective-permute-done.17 = bf16[2,128,512]{2,1,0:T(8,128)(2,1)S(1)} collective-permute-done((bf16[2,128,512]{2,1,0:T(8,128)(2,1)}, bf16[2,128,512]{2,1,0:T(8,128)(2,1)S(1)}, u32[]{:S(2)}, u32[]{:S(2)}) %collective-permute-start.17) | collective-permute-done | bytes 262176 | tf_op jit(solution)/shard_map/ppermute | solution.py:289
  59.4 4.7 %collective-permute-done.15 = bf16[2,128,512]{2,1,0:T(8,128)(2,1)} collective-permute-done((bf16[2,128,512]{2,1,0:T(8,128)(2,1)}, bf16[2,128,512]{2,1,0:T(8,128)(2,1)}, u32[]{:S(2)}, u32[]{:S(2)}) %collective-permute-start.15) | collective-permute-done | bytes 262176 | tf_op jit(solution)/shard_map/ppermute | solution.py:289
  64.1 2.1 %fusion.47 = (bf16[128,512]{1,0:T(8,128)(2,1)}, bf16[128,512]{1,0:T(8,128)(2,1)}) fusion(bf16[3,128,512]{2,1,0:T(8,128)(2,1)} %get-tuple-element.26, pred[]{:T(512)S(6)} %lt.83, pred[]{:T(512)S(6)} %lt.82, pred[]{:T(512)S(6)} %lt.81, bf16[2,128,512]{2,1,0:T(8,128)(2,1)S(1)} %collective-permute-done.17, bf16[2,128,512]{2,1,0:T(8,128)(2,1)} %collective-permute-done.16, ...), kind=kLoop, calls=%fused_computation.91 | loop fusion | flops 1441792 | bytes 1310723 | tf_op jit(solution)/shard_map/convert_element_type | solution.py:330
  66.2 0.9 collective-permute-start.19
  67.1 1.5 fusion.11
  68.5 3.9 %collective-permute-done.19 = bf16[128,512]{1,0:T(8,128)(2,1)S(1)} collective-permute-done((bf16[128,512]{1,0:T(8,128)(2,1)}, bf16[128,512]{1,0:T(8,128)(2,1)S(1)}, u32[]{:S(2)}, u32[]{:S(2)}) %collective-permute-start.19) | collective-permute-done | bytes 131104 | tf_op jit(solution)/shard_map/ppermute | solution.py:293
  72.5 0.7 copy-done.10
  73.1 1.3 fusion.37
  74.4 1.0 fusion.10
  76.0 0.8 fusion.14
  76.9 1.3 collective-permute-start.20
  78.2 4.6 %fusion.5 = f32[128,512]{1,0:T(8,128)S(1)} fusion(bf16[8192,512]{1,0:T(8,128)(2,1)} %param.12, bf16[1,128,8192]{2,1,0:T(8,128)(2,1)S(1)} %copy-done), kind=kOutput, calls=%fused_computation.8 | convolution fusion | flops 1073741824 | bytes 10747904 | tf_op jit(solution)/shard_map/dot_general | solution.py:37
  83.5 1.4 collective-permute-start.6
  84.9 7.4 %collective-permute-done.5.rest_7_ = bf16[128,512]{1,0:T(8,128)(2,1)} collective-permute-done((bf16[128,512]{1,0:T(8,128)(2,1)S(1)}, bf16[128,512]{1,0:T(8,128)(2,1)}, u32[]{:S(2)}, u32[]{:S(2)}) %collective-permute-start.5) | collective-permute-done | bytes 131104 | tf_op jit(solution)/shard_map/ppermute | solution.py:293
  92.4 1.9 %broadcast_select_fusion.5 = (bf16[2,128,512]{2,1,0:T(8,128)(2,1)}, bf16[2,128,512]{2,1,0:T(8,128)(2,1)}, bf16[2,128,512]{2,1,0:T(8,128)(2,1)}) fusion(pred[]{:T(512)S(6)} %gt.14, bf16[1,128,512]{2,1,0:T(8,128)(2,1)} %bitcast.11, bf16[1,128,512]{2,1,0:T(8,128)(2,1)S(1)} %bitcast.73, bf16[1,128,512]{2,1,0:T(8,128)(2,1)} %bitcast.12, pred[]{:T(512)S(6)} %gt.12, ...), kind=kLoop, calls=%fused_computation.86 | loop fusion | flops 655360 | bytes 1179651 | tf_op jit(solution)/shard_map/jit(_where)/select_n | solution.py:311
  94.3 1.1 collective-permute-start.8
  95.4 1.6 collective-permute-start.9
  97.6 4.3 %all-to-all-start = ((f32[16,1,384]{2,1,0:T(1,128)}), f32[16,1,384]{2,1,0:T(1,128)}, u32[]{:S(2)}, u32[]{:S(2)}) async-start(f32[16,1,384]{2,1,0:T(1,128)} %copy.18), calls=%async_computation | async-start | bytes 49152 | tf_op jit(solution)/shard_map/all_to_all | solution.py:374
  102.0 1.2 add_convert_fusion
  103.2 0.8 copy-done.3
  104.0 0.8 constant_dynamic-slice_fusion.2
  104.8 2.7 %collective-permute-start.23 = (bf16[32,2176]{1,0:T(8,128)(2,1)}, bf16[32,2176]{1,0:T(8,128)(2,1)}, u32[]{:S(2)}, u32[]{:S(2)}) collective-permute-start(bf16[32,2176]{1,0:T(8,128)(2,1)} %get-tuple-element.61), channel_id=1, source_target_pairs={{0,96},{16,112},{32,0},{48,16},{64,32},{80,48},{96,64},{112,80},{1... | collective-permute-start | bytes 417800 | tf_op jit(solution)/shard_map/ppermute | solution.py:297
  107.9 0.7 collective-permute-done.7.rest_9_
  108.6 1.3 collective-permute-start.21
  109.9 17.8 %grads.1 = (bf16[128,4096]{1,0:T(8,128)(2,1)}, bf16[128,4096]{1,0:T(8,128)(2,1)}, bf16[3,128,512]{2,1,0:T(8,128)(2,1)}, bf16[2,128,512]{2,1,0:T(8,128)(2,1)}, bf...) custom-call(s32[1]{0:T(128)} %bitcast.here_ref, s32[1,128]{1,0:T(1,128)} %docs_ref.3, ...), custom_call_target="tpu_custom_call" | custom-call | flops 6039797760 | bytes 8388608 | tf_op jit(solution)/shard_map/grads/pallas_call | solution.py:256
  127.7 2.4 %collective-permute-start.12 = (bf16[2,128,512]{2,1,0:T(8,128)(2,1)}, bf16[2,128,512]{2,1,0:T(8,128)(2,1)S(1)}, u32[]{:S(2)}, u32[]{:S(2)}) collective-permute-start(bf16[2,128,512]{2,1,0:T(8,128)(2,1)} %get-tuple-element.25), channel_id=1, source_target_pairs={{0,3},{1,0},{2,1},{3,2},{4,7},{5,4},{6,5},{7,6},{8,11},{9,8},{10,9... | collective-permute-start | bytes 786440 | tf_op jit(solution)/shard_map/ppermute | solution.py:289
  130.1 1.4 reduce
  131.5 1.5 broadcast_in_dim_reshape.3
  133.0 1.6 copy.19
  134.6 0.7 collective-permute-start.10
  135.3 1.2 add_convert_fusion.3
  136.4 1.6 collective-permute-start.26
  138.1 1.7 collective-permute-start.24
  139.8 4.0 %collective-permute-done.10 = bf16[2,128,512]{2,1,0:T(8,128)(2,1)S(1)} collective-permute-done((bf16[2,128,512]{2,1,0:T(8,128)(2,1)}, bf16[2,128,512]{2,1,0:T(8,128)(2,1)S(1)}, u32[]{:S(2)}, u32[]{:S(2)}) %collective-permute-start.10) | collective-permute-done | bytes 262176 | tf_op jit(solution)/shard_map/ppermute | solution.py:289
  143.9 1.3 fusion.49
  145.1 2.4 %collective-permute-start.14 = (bf16[128,512]{1,0:T(8,128)(2,1)S(1)}, bf16[128,512]{1,0:T(8,128)(2,1)S(1)}, u32[]{:S(2)}, u32[]{:S(2)}) collective-permute-start(bf16[128,512]{1,0:T(8,128)(2,1)S(1)} %get-tuple-element.57), channel_id=1, source_target_pairs={{0,8},{1,9},{2,10},{3,11},{4,12},{5,13},{6,14},{7,15},{8,0},{9,1},... | collective-permute-start | bytes 393224 | tf_op jit(solution)/shard_map/ppermute | solution.py:293
  147.6 0.9 collective-permute-start.13
  148.6 1.4 collective-permute-start.28
  150.1 0.7 fusion.52
  150.8 2.0 %collective-permute-done.29 = bf16[32,2176]{1,0:T(8,128)(2,1)S(1)} collective-permute-done((bf16[32,2176]{1,0:T(8,128)(2,1)S(1)}, bf16[32,2176]{1,0:T(8,128)(2,1)S(1)}, u32[]{:S(2)}, u32[]{:S(2)}) %collective-permute-start.29) | collective-permute-done | bytes 139296 | tf_op jit(solution)/shard_map/ppermute | solution.py:289
  152.8 1.0 collective-permute-done.28
  153.8 1.7 collective-permute-done.27
  155.6 1.7 collective-permute-start.30
  157.3 1.8 fusion.50
  159.1 3.5 %collective-permute-start.31 = (bf16[32,2176]{1,0:T(8,128)(2,1)S(1)}, bf16[32,2176]{1,0:T(8,128)(2,1)S(1)}, u32[]{:S(2)}, u32[]{:S(2)}) collective-permute-start(bf16[32,2176]{1,0:T(8,128)(2,1)S(1)} %get-tuple-element.53), channel_id=1, source_target_pairs={{0,64},{16,80},{32,96},{48,112},{64,0},{80,16},{96,32},{112,48},{1... | collective-permute-start | bytes 417800 | tf_op jit(solution)/shard_map/ppermute | solution.py:297
  162.5 2.4 %collective-permute-done.31 = bf16[32,2176]{1,0:T(8,128)(2,1)S(1)} collective-permute-done((bf16[32,2176]{1,0:T(8,128)(2,1)S(1)}, bf16[32,2176]{1,0:T(8,128)(2,1)S(1)}, u32[]{:S(2)}, u32[]{:S(2)}) %collective-permute-start.31) | collective-permute-done | bytes 139296 | tf_op jit(solution)/shard_map/ppermute | solution.py:297
  165.0 1.4 collective-permute-done.32
  166.4 9.0 %collective-permute-start.33 = (bf16[32,8704]{1,0:T(8,128)(2,1)S(1)}, bf16[32,8704]{1,0:T(8,128)(2,1)S(1)}, u32[]{:S(2)}, u32[]{:S(2)}) collective-permute-start(bf16[32,8704]{1,0:T(8,128)(2,1)S(1)} %constant_dynamic-update-slice_fusion), channel_id=1, source_target_pairs={{0,16},{16,0},{32,48},{48,32},{64,80},{80,64},{96,112},{112,96},{1... | collective-permute-start | bytes 1671176 | tf_op jit(solution)/shard_map/ppermute | solution.py:301
  175.5 7.5 %fusion.1 = bf16[1,128,8192]{2,1,0:T(8,128)(2,1)} fusion(f32[128,8192]{1,0:T(8,128)S(1)} %fusion.52, bf16[128,512]{1,0:T(8,128)(2,1)S(1)} %fusion.37, bf16[8192,512]{1,0:T(8,128)(2,1)} %param.12), kind=kOutput, calls=%fused_computation.2 | convolution fusion | flops 1075838976 | bytes 14811136 | tf_op jit(solution)/shard_map/dot_general | solution.py:37
  183.2 0.7 maximum_convert_fusion.1
  183.9 1.5 slice_bitcast_fusion
  (74 shorter events, 4.8 us)
Async XLA Ops:
  0.6 66.4 %copy-start = (bf16[1,128,8192]{2,1,0:T(8,128)(2,1)S(1)}, bf16[1,128,8192]{2,1,0:T(8,128)(2,1)}, u32[]{:S(2)}) copy-start(bf16[1,128,8192]{2,1,0:T(8,128)(2,1)} %param.9) | copy-start | bytes 6291460
  2.4 28.3 %copy-start.6 = (bf16[144,512]{1,0:T(8,128)(2,1)}, bf16[144,512]{1,0:T(8,128)(2,1)S(1)}, u32[]{:S(2)}) copy-start(bf16[144,512]{1,0:T(8,128)(2,1)S(1)} %get-tuple-element.70.rest_0_) | copy-start | bytes 442372
  2.4 6.5 %collective-permute-start = (bf16[144,512]{1,0:T(8,128)(2,1)S(1)}, bf16[144,512]{1,0:T(8,128)(2,1)S(1)}, u32[]{:S(2)}, u32[]{:S(2)}) collective-permute-start(bf16[144,512]{1,0:T(8,128)(2,1)S(1)} %get-tuple-element.70.rest_0_), channel_id=1, source_target_pairs={{0,4},{1,5},{2,6},{3,7},{4,8},{5,9},{6,10},{7,11},{8,12},{9,13},{1... | collective-permute-start | bytes 442376 | tf_op jit(solution)/shard_map/ppermute | solution.py:293
  4.5 8.9 %collective-permute-start.1 = (bf16[144,512]{1,0:T(8,128)(2,1)S(1)}, bf16[144,512]{1,0:T(8,128)(2,1)S(1)}, u32[]{:S(2)}, u32[]{:S(2)}) collective-permute-start(bf16[144,512]{1,0:T(8,128)(2,1)S(1)} %get-tuple-element.70.rest_0_), channel_id=1, source_target_pairs={{0,8},{1,9},{2,10},{3,11},{4,12},{5,13},{6,14},{7,15},{8,0},{9,1},... | collective-permute-start | bytes 442376 | tf_op jit(solution)/shard_map/ppermute | solution.py:293
  8.9 21.8 %copy-start.8 = (bf16[144,512]{1,0:T(8,128)(2,1)}, bf16[144,512]{1,0:T(8,128)(2,1)S(1)}, u32[]{:S(2)}) copy-start(bf16[144,512]{1,0:T(8,128)(2,1)S(1)} %collective-permute-done.rest_1_) | copy-start | bytes 442372
  13.4 17.3 %copy-start.9 = (bf16[144,512]{1,0:T(8,128)(2,1)}, bf16[144,512]{1,0:T(8,128)(2,1)S(1)}, u32[]{:S(2)}) copy-start(bf16[144,512]{1,0:T(8,128)(2,1)S(1)} %collective-permute-done.1.rest_2_) | copy-start | bytes 442372
  13.4 9.6 %collective-permute-start.2 = (bf16[2,144,512]{2,1,0:T(8,128)(2,1)S(1)}, bf16[2,144,512]{2,1,0:T(8,128)(2,1)S(1)}, u32[]{:S(2)}, u32[]{:S(2)}) collective-permute-start(bf16[2,144,512]{2,1,0:T(8,128)(2,1)S(1)} %get-tuple-element.64), channel_id=1, source_target_pairs={{0,1},{1,2},{2,3},{3,0},{4,5},{5,6},{6,7},{7,4},{8,9},{9,10},{10,1... | collective-permute-start | bytes 884744 | tf_op jit(solution)/shard_map/ppermute | solution.py:289
  15.2 15.1 %collective-permute-start.3 = (bf16[2,144,512]{2,1,0:T(8,128)(2,1)S(1)}, bf16[2,144,512]{2,1,0:T(8,128)(2,1)S(1)}, u32[]{:S(2)}, u32[]{:S(2)}) collective-permute-start(bf16[2,144,512]{2,1,0:T(8,128)(2,1)S(1)} %get-tuple-element.65), channel_id=1, source_target_pairs={{0,2},{1,3},{2,0},{3,1},{4,6},{5,7},{6,4},{7,5},{8,10},{9,11},{10,... | collective-permute-start | bytes 884744 | tf_op jit(solution)/shard_map/ppermute | solution.py:289
  18.5 12.3 %collective-permute-start.4 = (bf16[2,144,512]{2,1,0:T(8,128)(2,1)S(1)}, bf16[2,144,512]{2,1,0:T(8,128)(2,1)S(1)}, u32[]{:S(2)}, u32[]{:S(2)}) collective-permute-start(bf16[2,144,512]{2,1,0:T(8,128)(2,1)S(1)} %get-tuple-element.63), channel_id=1, source_target_pairs={{0,3},{1,0},{2,1},{3,2},{4,7},{5,4},{6,5},{7,6},{8,11},{9,8},{10,9... | collective-permute-start | bytes 884744 | tf_op jit(solution)/shard_map/ppermute | solution.py:289
  23.0 7.7 %copy-start.12 = (bf16[2,144,512]{2,1,0:T(8,128)(2,1)}, bf16[2,144,512]{2,1,0:T(8,128)(2,1)S(1)}, u32[]{:S(2)}) copy-start(bf16[2,144,512]{2,1,0:T(8,128)(2,1)S(1)} %collective-permute-done.2.rest_3_) | copy-start | bytes 884740
  30.3 0.7 copy-start.13
  30.7 0.7 copy-start.14
  31.4 35.7 %copy-start.1 = (bf16[8192,64]{0,1:T(8,128)(2,1)S(1)}, bf16[8192,64]{0,1:T(8,128)(2,1)}, u32[]{:S(2)}) copy-start(bf16[8192,64]{0,1:T(8,128)(2,1)} %param.13) | copy-start | bytes 3145732
  44.9 14.5 %collective-permute-start.17 = (bf16[2,128,512]{2,1,0:T(8,128)(2,1)}, bf16[2,128,512]{2,1,0:T(8,128)(2,1)S(1)}, u32[]{:S(2)}, u32[]{:S(2)}) collective-permute-start(bf16[2,128,512]{2,1,0:T(8,128)(2,1)} %get-tuple-element.29), channel_id=1, source_target_pairs={{0,3},{1,0},{2,1},{3,2},{4,7},{5,4},{6,5},{7,6},{8,11},{9,8},{10,9... | collective-permute-start | bytes 786440 | tf_op jit(solution)/shard_map/ppermute | solution.py:289
  48.4 11.0 %collective-permute-start.16 = (bf16[2,128,512]{2,1,0:T(8,128)(2,1)}, bf16[2,128,512]{2,1,0:T(8,128)(2,1)}, u32[]{:S(2)}, u32[]{:S(2)}) collective-permute-start(bf16[2,128,512]{2,1,0:T(8,128)(2,1)} %get-tuple-element.28), channel_id=1, source_target_pairs={{0,2},{1,3},{2,0},{3,1},{4,6},{5,7},{6,4},{7,5},{8,10},{9,11},{10,... | collective-permute-start | bytes 786440 | tf_op jit(solution)/shard_map/ppermute | solution.py:289
  48.8 15.2 %collective-permute-start.15 = (bf16[2,128,512]{2,1,0:T(8,128)(2,1)}, bf16[2,128,512]{2,1,0:T(8,128)(2,1)}, u32[]{:S(2)}, u32[]{:S(2)}) collective-permute-start(bf16[2,128,512]{2,1,0:T(8,128)(2,1)} %get-tuple-element.27), channel_id=1, source_target_pairs={{0,1},{1,2},{2,3},{3,0},{4,5},{5,6},{6,7},{7,4},{8,9},{9,10},{10,1... | collective-permute-start | bytes 786440 | tf_op jit(solution)/shard_map/ppermute | solution.py:289
  66.2 6.3 %collective-permute-start.19 = (bf16[128,512]{1,0:T(8,128)(2,1)}, bf16[128,512]{1,0:T(8,128)(2,1)S(1)}, u32[]{:S(2)}, u32[]{:S(2)}) collective-permute-start(bf16[128,512]{1,0:T(8,128)(2,1)} %get-tuple-element.55), channel_id=1, source_target_pairs={{0,8},{1,9},{2,10},{3,11},{4,12},{5,13},{6,14},{7,15},{8,0},{9,1},... | collective-permute-start | bytes 393224 | tf_op jit(solution)/shard_map/ppermute | solution.py:293
  67.1 6.0 %collective-permute-start.18 = (bf16[128,512]{1,0:T(8,128)(2,1)}, bf16[128,512]{1,0:T(8,128)(2,1)}, u32[]{:S(2)}, u32[]{:S(2)}) collective-permute-start(bf16[128,512]{1,0:T(8,128)(2,1)} %get-tuple-element.54), channel_id=1, source_target_pairs={{0,12},{1,13},{2,14},{3,15},{4,0},{5,1},{6,2},{7,3},{8,4},{9,5},{1... | collective-permute-start | bytes 393224 | tf_op jit(solution)/shard_map/ppermute | solution.py:293
  68.5 7.3 %copy-start.7 = (bf16[128,64]{0,1:T(8,128)(2,1)S(1)}, bf16[128,64]{0,1:T(8,128)(2,1)}, u32[]{:S(2)}) copy-start(bf16[128,64]{0,1:T(8,128)(2,1)} %fusion.11) | copy-start | bytes 49156
  72.5 0.7 copy-start.10
  76.9 6.0 %copy-start.5 = (bf16[64,512]{1,0:T(8,128)(2,1)S(1)}, bf16[64,512]{1,0:T(8,128)(2,1)}, u32[]{:S(2)}) copy-start(bf16[64,512]{1,0:T(8,128)(2,1)} %param.14) | copy-start | bytes 196612
  76.9 20.1 %copy-start.11 = (f32[16,384]{1,0:T(8,128)S(1)}, f32[16,384]{1,0:T(8,128)}, u32[]{:S(2)}) copy-start(f32[16,384]{1,0:T(8,128)} %get-tuple-element.30) | copy-start | bytes 73732
  76.9 25.1 %collective-permute-start.20 = (bf16[32,8704]{1,0:T(8,128)(2,1)}, bf16[32,8704]{1,0:T(8,128)(2,1)}, u32[]{:S(2)}, u32[]{:S(2)}) collective-permute-start(bf16[32,8704]{1,0:T(8,128)(2,1)} %fusion.14), channel_id=1, source_target_pairs={{0,16},{16,0},{32,48},{48,32},{64,80},{80,64},{96,112},{112,96},{1... | collective-permute-start | bytes 1671176 | tf_op jit(solution)/shard_map/ppermute | solution.py:301
  83.1 21.7 %copy-start.4 = (bf16[128,512]{1,0:T(8,128)(2,1)}, bf16[128,512]{1,0:T(8,128)(2,1)S(1)}, u32[]{:S(2)}) copy-start(bf16[128,512]{1,0:T(8,128)(2,1)S(1)} %fusion.8.rest_6_) | copy-start | bytes 393220
  83.1 9.3 %collective-permute-start.5 = (bf16[128,512]{1,0:T(8,128)(2,1)S(1)}, bf16[128,512]{1,0:T(8,128)(2,1)}, u32[]{:S(2)}, u32[]{:S(2)}) collective-permute-start(bf16[128,512]{1,0:T(8,128)(2,1)S(1)} %fusion.8.rest_6_), channel_id=1, source_target_pairs={{0,4},{1,5},{2,6},{3,7},{4,8},{5,9},{6,10},{7,11},{8,12},{9,13},{1... | collective-permute-start | bytes 393224 | tf_op jit(solution)/shard_map/ppermute | solution.py:293
  83.5 8.9 %collective-permute-start.6 = (bf16[128,512]{1,0:T(8,128)(2,1)S(1)}, bf16[128,512]{1,0:T(8,128)(2,1)}, u32[]{:S(2)}, u32[]{:S(2)}) collective-permute-start(bf16[128,512]{1,0:T(8,128)(2,1)S(1)} %fusion.8.rest_6_), channel_id=1, source_target_pairs={{0,8},{1,9},{2,10},{3,11},{4,12},{5,13},{6,14},{7,15},{8,0},{9,1},... | collective-permute-start | bytes 393224 | tf_op jit(solution)/shard_map/ppermute | solution.py:293
  94.3 14.3 %collective-permute-start.7 = (bf16[2,128,512]{2,1,0:T(8,128)(2,1)}, bf16[2,128,512]{2,1,0:T(8,128)(2,1)}, u32[]{:S(2)}, u32[]{:S(2)}) collective-permute-start(bf16[2,128,512]{2,1,0:T(8,128)(2,1)} %get-tuple-element.67), channel_id=1, source_target_pairs={{0,1},{1,2},{2,3},{3,0},{4,5},{5,6},{6,7},{7,4},{8,9},{9,10},{10,1... | collective-permute-start | bytes 786440 | tf_op jit(solution)/shard_map/ppermute | solution.py:289
  94.3 15.5 %collective-permute-start.8 = (bf16[2,128,512]{2,1,0:T(8,128)(2,1)}, bf16[2,128,512]{2,1,0:T(8,128)(2,1)}, u32[]{:S(2)}, u32[]{:S(2)}) collective-permute-start(bf16[2,128,512]{2,1,0:T(8,128)(2,1)} %get-tuple-element.68), channel_id=1, source_target_pairs={{0,2},{1,3},{2,0},{3,1},{4,6},{5,7},{6,4},{7,5},{8,10},{9,11},{10,... | collective-permute-start | bytes 786440 | tf_op jit(solution)/shard_map/ppermute | solution.py:289
  95.4 14.5 %collective-permute-start.9 = (bf16[2,128,512]{2,1,0:T(8,128)(2,1)}, bf16[2,128,512]{2,1,0:T(8,128)(2,1)}, u32[]{:S(2)}, u32[]{:S(2)}) collective-permute-start(bf16[2,128,512]{2,1,0:T(8,128)(2,1)} %get-tuple-element.66), channel_id=1, source_target_pairs={{0,3},{1,0},{2,1},{3,2},{4,7},{5,4},{6,5},{7,6},{8,11},{9,8},{10,9... | collective-permute-start | bytes 786440 | tf_op jit(solution)/shard_map/ppermute | solution.py:289
  97.6 32.5 %all-to-all-start = ((f32[16,1,384]{2,1,0:T(1,128)}), f32[16,1,384]{2,1,0:T(1,128)}, u32[]{:S(2)}, u32[]{:S(2)}) async-start(f32[16,1,384]{2,1,0:T(1,128)} %copy.18), calls=%async_computation | async-start | bytes 49152 | tf_op jit(solution)/shard_map/all_to_all | solution.py:374
  103.2 0.8 copy-start.3
  104.8 29.8 %collective-permute-start.23 = (bf16[32,2176]{1,0:T(8,128)(2,1)}, bf16[32,2176]{1,0:T(8,128)(2,1)}, u32[]{:S(2)}, u32[]{:S(2)}) collective-permute-start(bf16[32,2176]{1,0:T(8,128)(2,1)} %get-tuple-element.61), channel_id=1, source_target_pairs={{0,96},{16,112},{32,0},{48,16},{64,32},{80,48},{96,64},{112,80},{1... | collective-permute-start | bytes 417800 | tf_op jit(solution)/shard_map/ppermute | solution.py:297
  107.5 27.8 %collective-permute-start.22 = (bf16[32,2176]{1,0:T(8,128)(2,1)}, bf16[32,2176]{1,0:T(8,128)(2,1)}, u32[]{:S(2)}, u32[]{:S(2)}) collective-permute-start(bf16[32,2176]{1,0:T(8,128)(2,1)} %get-tuple-element.62), channel_id=1, source_target_pairs={{0,64},{16,80},{32,96},{48,112},{64,0},{80,16},{96,32},{112,48},{1... | collective-permute-start | bytes 417800 | tf_op jit(solution)/shard_map/ppermute | solution.py:297
  108.6 26.7 %collective-permute-start.21 = (bf16[32,2176]{1,0:T(8,128)(2,1)}, bf16[32,2176]{1,0:T(8,128)(2,1)}, u32[]{:S(2)}, u32[]{:S(2)}) collective-permute-start(bf16[32,2176]{1,0:T(8,128)(2,1)} %get-tuple-element.60), channel_id=1, source_target_pairs={{0,32},{16,48},{32,64},{48,80},{64,96},{80,112},{96,0},{112,16},{1... | collective-permute-start | bytes 417800 | tf_op jit(solution)/shard_map/ppermute | solution.py:297
  127.7 22.4 %copy-start.2 = (bf16[8192,64]{0,1:T(8,128)(2,1)S(1)}, bf16[8192,64]{0,1:T(8,128)(2,1)}, u32[]{:S(2)}) copy-start(bf16[8192,64]{0,1:T(8,128)(2,1)} %param.13) | copy-start | bytes 3145732
  127.7 10.4 %collective-permute-start.12 = (bf16[2,128,512]{2,1,0:T(8,128)(2,1)}, bf16[2,128,512]{2,1,0:T(8,128)(2,1)S(1)}, u32[]{:S(2)}, u32[]{:S(2)}) collective-permute-start(bf16[2,128,512]{2,1,0:T(8,128)(2,1)} %get-tuple-element.25), channel_id=1, source_target_pairs={{0,3},{1,0},{2,1},{3,2},{4,7},{5,4},{6,5},{7,6},{8,11},{9,8},{10,9... | collective-permute-start | bytes 786440 | tf_op jit(solution)/shard_map/ppermute | solution.py:289
  130.1 9.7 %collective-permute-start.11 = (bf16[2,128,512]{2,1,0:T(8,128)(2,1)}, bf16[2,128,512]{2,1,0:T(8,128)(2,1)}, u32[]{:S(2)}, u32[]{:S(2)}) collective-permute-start(bf16[2,128,512]{2,1,0:T(8,128)(2,1)} %get-tuple-element.24), channel_id=1, source_target_pairs={{0,2},{1,3},{2,0},{3,1},{4,6},{5,7},{6,4},{7,5},{8,10},{9,11},{10,... | collective-permute-start | bytes 786440 | tf_op jit(solution)/shard_map/ppermute | solution.py:289
  134.6 9.3 %collective-permute-start.10 = (bf16[2,128,512]{2,1,0:T(8,128)(2,1)}, bf16[2,128,512]{2,1,0:T(8,128)(2,1)S(1)}, u32[]{:S(2)}, u32[]{:S(2)}) collective-permute-start(bf16[2,128,512]{2,1,0:T(8,128)(2,1)} %get-tuple-element.23), channel_id=1, source_target_pairs={{0,1},{1,2},{2,3},{3,0},{4,5},{5,6},{6,7},{7,4},{8,9},{9,10},{10,1... | collective-permute-start | bytes 786440 | tf_op jit(solution)/shard_map/ppermute | solution.py:289
  136.4 12.0 %collective-permute-start.26 = (bf16[32,2176]{1,0:T(8,128)(2,1)S(1)}, bf16[32,2176]{1,0:T(8,128)(2,1)S(1)}, u32[]{:S(2)}, u32[]{:S(2)}) collective-permute-start(bf16[32,2176]{1,0:T(8,128)(2,1)S(1)} %add_convert_fusion.3), channel_id=1, source_target_pairs={{0,12},{1,13},{2,14},{3,15},{4,0},{5,1},{6,2},{7,3},{8,4},{9,5},{1... | collective-permute-start | bytes 417800 | tf_op jit(solution)/shard_map/ppermute | solution.py:293
  138.1 10.4 %collective-permute-start.25 = (bf16[32,2176]{1,0:T(8,128)(2,1)S(1)}, bf16[32,2176]{1,0:T(8,128)(2,1)S(1)}, u32[]{:S(2)}, u32[]{:S(2)}) collective-permute-start(bf16[32,2176]{1,0:T(8,128)(2,1)S(1)} %add_convert_fusion.3), channel_id=1, source_target_pairs={{0,4},{1,5},{2,6},{3,7},{4,8},{5,9},{6,10},{7,11},{8,12},{9,13},{1... | collective-permute-start | bytes 417800 | tf_op jit(solution)/shard_map/ppermute | solution.py:293
  138.1 10.4 %collective-permute-start.24 = (bf16[32,2176]{1,0:T(8,128)(2,1)S(1)}, bf16[32,2176]{1,0:T(8,128)(2,1)S(1)}, u32[]{:S(2)}, u32[]{:S(2)}) collective-permute-start(bf16[32,2176]{1,0:T(8,128)(2,1)S(1)} %add_convert_fusion.3), channel_id=1, source_target_pairs={{0,8},{1,9},{2,10},{3,11},{4,12},{5,13},{6,14},{7,15},{8,0},{9,1},... | collective-permute-start | bytes 417800 | tf_op jit(solution)/shard_map/ppermute | solution.py:293
  145.1 12.2 %collective-permute-start.14 = (bf16[128,512]{1,0:T(8,128)(2,1)S(1)}, bf16[128,512]{1,0:T(8,128)(2,1)S(1)}, u32[]{:S(2)}, u32[]{:S(2)}) collective-permute-start(bf16[128,512]{1,0:T(8,128)(2,1)S(1)} %get-tuple-element.57), channel_id=1, source_target_pairs={{0,8},{1,9},{2,10},{3,11},{4,12},{5,13},{6,14},{7,15},{8,0},{9,1},... | collective-permute-start | bytes 393224 | tf_op jit(solution)/shard_map/ppermute | solution.py:293
  147.6 9.8 %collective-permute-start.13 = (bf16[128,512]{1,0:T(8,128)(2,1)S(1)}, bf16[128,512]{1,0:T(8,128)(2,1)S(1)}, u32[]{:S(2)}, u32[]{:S(2)}) collective-permute-start(bf16[128,512]{1,0:T(8,128)(2,1)S(1)} %get-tuple-element.56), channel_id=1, source_target_pairs={{0,12},{1,13},{2,14},{3,15},{4,0},{5,1},{6,2},{7,3},{8,4},{9,5},{1... | collective-permute-start | bytes 393224 | tf_op jit(solution)/shard_map/ppermute | solution.py:293
  148.6 4.3 %collective-permute-start.29 = (bf16[32,2176]{1,0:T(8,128)(2,1)S(1)}, bf16[32,2176]{1,0:T(8,128)(2,1)S(1)}, u32[]{:S(2)}, u32[]{:S(2)}) collective-permute-start(bf16[32,2176]{1,0:T(8,128)(2,1)S(1)} %add_convert_fusion.2), channel_id=1, source_target_pairs={{0,3},{1,0},{2,1},{3,2},{4,7},{5,4},{6,5},{7,6},{8,11},{9,8},{10,9... | collective-permute-start | bytes 417800 | tf_op jit(solution)/shard_map/ppermute | solution.py:289
  148.6 5.2 %collective-permute-start.28 = (bf16[32,2176]{1,0:T(8,128)(2,1)S(1)}, bf16[32,2176]{1,0:T(8,128)(2,1)S(1)}, u32[]{:S(2)}, u32[]{:S(2)}) collective-permute-start(bf16[32,2176]{1,0:T(8,128)(2,1)S(1)} %add_convert_fusion.2), channel_id=1, source_target_pairs={{0,1},{1,2},{2,3},{3,0},{4,5},{5,6},{6,7},{7,4},{8,9},{9,10},{10,1... | collective-permute-start | bytes 417800 | tf_op jit(solution)/shard_map/ppermute | solution.py:289
  150.1 5.4 %collective-permute-start.27 = (bf16[32,2176]{1,0:T(8,128)(2,1)S(1)}, bf16[32,2176]{1,0:T(8,128)(2,1)S(1)}, u32[]{:S(2)}, u32[]{:S(2)}) collective-permute-start(bf16[32,2176]{1,0:T(8,128)(2,1)S(1)} %add_convert_fusion.2), channel_id=1, source_target_pairs={{0,2},{1,3},{2,0},{3,1},{4,6},{5,7},{6,4},{7,5},{8,10},{9,11},{10,... | collective-permute-start | bytes 417800 | tf_op jit(solution)/shard_map/ppermute | solution.py:289
  155.6 6.9 %collective-permute-start.30 = (bf16[32,2176]{1,0:T(8,128)(2,1)S(1)}, bf16[32,2176]{1,0:T(8,128)(2,1)S(1)}, u32[]{:S(2)}, u32[]{:S(2)}) collective-permute-start(bf16[32,2176]{1,0:T(8,128)(2,1)S(1)} %get-tuple-element.53), channel_id=1, source_target_pairs={{0,32},{16,48},{32,64},{48,80},{64,96},{80,112},{96,0},{112,16},{1... | collective-permute-start | bytes 417800 | tf_op jit(solution)/shard_map/ppermute | solution.py:297
  159.1 5.9 %collective-permute-start.31 = (bf16[32,2176]{1,0:T(8,128)(2,1)S(1)}, bf16[32,2176]{1,0:T(8,128)(2,1)S(1)}, u32[]{:S(2)}, u32[]{:S(2)}) collective-permute-start(bf16[32,2176]{1,0:T(8,128)(2,1)S(1)} %get-tuple-element.53), channel_id=1, source_target_pairs={{0,64},{16,80},{32,96},{48,112},{64,0},{80,16},{96,32},{112,48},{1... | collective-permute-start | bytes 417800 | tf_op jit(solution)/shard_map/ppermute | solution.py:297
  162.5 3.9 %collective-permute-start.32 = (bf16[32,2176]{1,0:T(8,128)(2,1)S(1)}, bf16[32,2176]{1,0:T(8,128)(2,1)S(1)}, u32[]{:S(2)}, u32[]{:S(2)}) collective-permute-start(bf16[32,2176]{1,0:T(8,128)(2,1)S(1)} %get-tuple-element.53), channel_id=1, source_target_pairs={{0,96},{16,112},{32,0},{48,16},{64,32},{80,48},{96,64},{112,80},{1... | collective-permute-start | bytes 417800 | tf_op jit(solution)/shard_map/ppermute | solution.py:297
  166.4 16.6 %collective-permute-start.33 = (bf16[32,8704]{1,0:T(8,128)(2,1)S(1)}, bf16[32,8704]{1,0:T(8,128)(2,1)S(1)}, u32[]{:S(2)}, u32[]{:S(2)}) collective-permute-start(bf16[32,8704]{1,0:T(8,128)(2,1)S(1)} %constant_dynamic-update-slice_fusion), channel_id=1, source_target_pairs={{0,16},{16,0},{32,48},{48,32},{64,80},{80,64},{96,112},{112,96},{1... | collective-permute-start | bytes 1671176 | tf_op jit(solution)/shard_map/ppermute | solution.py:301

commit v2 on v1

--- a/solution.py
+++ b/solution.py
@@ -27,6 +27,7 @@
 LN2 = 0.6931471805599453
 MASKED = -1e30
 VMEM = 56 << 20
+SMALL_VMEM = 20 << 20
 BF = jnp.bfloat16
 F32 = jnp.float32
 NT = (((1,), (1,)), ((), ()))
@@ -41,6 +42,11 @@
     if distance % 4 == 0:
         return own[distance // 4]
     return pairs[distance % 4 - 1].at[distance // 4]
+
+
+def put_partials(outs, value_of):
+    for distance in range(BLOCKS):
+        outs[-distance % 4][distance // 4] = value_of(REACH - distance)
 
 
 def fill_bias(here, parts, docs_own, bias):
@@ -79,11 +85,11 @@
 
 def scores_kernel(here_ref, docs_ref, owners_ref, q_ref, g_ref, *rest):
     key_own, key_pairs = rest[:3], rest[3:6]
-    lse_ref, slots_ref, *outs = rest[6:12]
-    bias, scores, weights, lse_all = rest[12:]
+    lse_ref, slots_ref, *dv_refs = rest[7:13]
+    bias, scores, weights, lse_all = rest[13:]
+    parts = [window_part(key_own, key_pairs, REACH - k) for k in range(BLOCKS)]
     group = pl.program_id(0)
     here = here_ref[0]
-    parts = [window_part(key_own, key_pairs, REACH - k) for k in range(BLOCKS)]
 
     @pl.when(group == 0)
     def _():
@@ -114,8 +120,7 @@
                 scores[block(k), :] - lse2
             ).astype(BF)
     rows = jnp.concatenate([pair_rows(g_ref, pair) for pair in range(PAIRS)], axis=0)
-    for k in range(BLOCKS):
-        put_partial(outs, REACH - k, dot(weights[block(k), :], rows).astype(BF))
+    put_partials(dv_refs, lambda k: dot(weights[block(k), :], rows).astype(BF))
 
     @pl.when(group == GROUPS - 1)
     def _():
@@ -132,25 +137,18 @@
     earlier = dot(onehot.astype(BF), jnp.where(before, 1.0, 0.0).astype(BF))
     for slot in range(CAP):
         place = jnp.where(named & (earlier == slot), 1.0, 0.0)
-        slots_ref[:, slot * HQ : (slot + 1) * HQ] = lax.dot_general(
+        slots_ref[:, 0, slot * HQ : (slot + 1) * HQ] = lax.dot_general(
             place, lse, NT, precision=lax.Precision.HIGHEST, preferred_element_type=F32
         )
 
 
-def put_partial(outs, distance, value):
-    if distance % 4 == 0:
-        outs[0][distance // 4] = value
-    else:
-        outs[4 - distance % 4][distance // 4] = value
-
-
 def grads_kernel(here_ref, docs_ref, q_ref, g_ref, lse_ref, *rest):
     key_own, key_pairs, value_own, value_pairs = rest[:3], rest[3:6], rest[6:9], rest[9:12]
-    out_ref, dq_ref, *outs = rest[12:18]
+    out_ref, dq_ref, *dk_refs = rest[12:18]
     bias, keys_t, values_t, weights32, weights, d_scores = rest[18:]
+    parts = [window_part(key_own, key_pairs, REACH - k) for k in range(BLOCKS)]
     group = pl.program_id(0)
     here = here_ref[0]
-    parts = [window_part(key_own, key_pairs, REACH - k) for k in range(BLOCKS)]
 
     @pl.when(group == 0)
     def _():
@@ -194,44 +192,47 @@
             out_ref[:, head] = out_t[:, n * TOK : (n + 1) * TOK].T.astype(BF)
             dq_ref[:, head] = dq_t[:, n * TOK : (n + 1) * TOK].T.astype(BF)
     rows = jnp.concatenate([pair_rows(q_ref, pair) for pair in range(PAIRS)], axis=0)
-    for k in range(BLOCKS):
-        put_partial(
-            outs, REACH - k, (dot(d_scores[block(k), :], rows) * INV_ROOT).astype(BF)
-        )
+    put_partials(
+        dk_refs, lambda k: (dot(d_scores[block(k), :], rows) * INV_ROOT).astype(BF)
+    )
 
 
 def smem():
     return pl.BlockSpec(memory_space=pltpu.SMEM)
 
 
+def anywhere():
+    return pl.BlockSpec(memory_space=pl.ANY)
+
+
 def partial_outs():
-    shapes = [jax.ShapeDtypeStruct((n, TOK, KV), BF) for n in (3, 2, 2, 2)]
-    specs = [pl.BlockSpec((n, TOK, HEAD), lambda g: (0, 0, g)) for n in (3, 2, 2, 2)]
-    return shapes, specs
-
-
-def part_specs(rows):
+    counts = (3, 2, 2, 2)
+    shapes = [jax.ShapeDtypeStruct((n, TOK, KV), BF) for n in counts]
+    return shapes, [pl.BlockSpec((n, TOK, HEAD), lambda g: (0, 0, g)) for n in counts]
+
+
+def window_specs(rows):
     own = pl.BlockSpec((rows, HEAD), lambda g: (0, g))
     pair = pl.BlockSpec((2, rows, HEAD), lambda g: (0, 0, g))
     return [own] * 3 + [pair] * 3
 
 
-def run_scores(here, docs_own, owners, queries, grads, keys):
+def run_scores(here, docs_own, owners, queries, grads, keys, after):
     shapes, specs = partial_outs()
     wide = pl.BlockSpec((TOK, PER_GROUP * HEAD), lambda g: (0, g))
     line = pl.BlockSpec((1, TOK), lambda g: (0, 0))
     return pl.pallas_call(
         scores_kernel,
         grid=(GROUPS,),
-        in_specs=[smem(), line, line, wide, wide] + part_specs(PACK),
+        in_specs=[smem(), line, line, wide, wide] + window_specs(PACK) + [anywhere()],
         out_specs=[
             pl.BlockSpec((1, PER_GROUP, TOK), lambda g: (g, 0, 0)),
-            pl.BlockSpec((16, CAP * HQ), lambda g: (0, 0)),
+            pl.BlockSpec((16, 1, CAP * HQ), lambda g: (0, 0, 0)),
         ]
         + specs,
         out_shape=[
             jax.ShapeDtypeStruct((GROUPS, PER_GROUP, TOK), F32),
-            jax.ShapeDtypeStruct((16, CAP * HQ), F32),
+            jax.ShapeDtypeStruct((16, 1, CAP * HQ), F32),
         ]
         + shapes,
         scratch_shapes=[
@@ -244,10 +245,10 @@
             vmem_limit_bytes=VMEM, dimension_semantics=("arbitrary",)
         ),
         cost_estimate=pl.CostEstimate(
-            flops=2 * 2 * HQ * TOK * KEYS * HEAD, bytes_accessed=6 << 20, transcendentals=2 * HQ * TOK * KEYS
+            flops=32 << 30, bytes_accessed=6 << 20, transcendentals=2 * HQ * TOK * KEYS
         ),
         name="scores",
-    )(here, docs_own, owners, queries, grads, *keys)
+    )(here, docs_own, owners, queries, grads, *keys, after)
 
 
 def run_grads(here, docs_own, queries, grads, lse, keys, values):
@@ -263,8 +264,8 @@
             wide,
             pl.BlockSpec((1, PER_GROUP, TOK), lambda g: (g, 0, 0)),
         ]
-        + part_specs(PACK)
-        + part_specs(TOK),
+        + window_specs(PACK)
+        + window_specs(TOK),
         out_specs=[wide, wide] + specs,
         out_shape=[jax.ShapeDtypeStruct((TOK, HQ * HEAD), BF)] * 2 + shapes,
         scratch_shapes=[
@@ -279,7 +280,7 @@
             vmem_limit_bytes=VMEM, dimension_semantics=("arbitrary",)
         ),
         cost_estimate=pl.CostEstimate(
-            flops=5 * 2 * HQ * TOK * KEYS * HEAD, bytes_accessed=8 << 20, transcendentals=HQ * TOK * KEYS
+            flops=64 << 30, bytes_accessed=8 << 20, transcendentals=HQ * TOK * KEYS
         ),
         name="grads",
     )(here, docs_own, queries, grads, lse, *keys, *values)
@@ -301,35 +302,179 @@
     return lax.ppermute(x, "dp", [(i, i ^ 1) for i in range(8)])
 
 
-def from_rows(x):
-    return [x, along_x(x, 1), along_x(x, 2)]
-
-
-def from_peers(own, z):
-    late = jnp.stack(own[1:])
-    early = jnp.stack(own[:2])
-    return [along_z(jnp.where(z + e > 3, late, early), e) for e in (1, 2, 3)]
-
-
-def sum_of_four(x, move):
-    near = move(x, 1).astype(F32) + move(x, 3).astype(F32)
-    return ((x.astype(F32) + move(x, 2).astype(F32)) + near).astype(BF)
-
-
-def collect(own, to_peer, z):
-    here_row = own[0].astype(F32)
-    row_1 = own[1].astype(F32)
-    row_2 = own[2].astype(F32)
+def for_peers(own, z):
+    blocks = [own, along_x(own, 1), along_x(own, 2)]
+    own, row_1, row_2 = blocks
+    pairs = []
     for e in (1, 2, 3):
-        got = along_z(to_peer[e - 1], e)
-        near, far = got[0].astype(F32), got[1].astype(F32)
-        wrapped = e > z
-        here_row = here_row + jnp.where(wrapped, near, 0.0)
-        row_1 = row_1 + jnp.where(wrapped, far, near)
-        row_2 = row_2 + jnp.where(wrapped, 0.0, far)
-    from_1 = along_x(row_1.astype(BF), -1)
-    from_2 = along_x(row_2.astype(BF), -2)
-    return here_row + from_1.astype(F32) + from_2.astype(F32)
+        wrapped = z + e > 3
+        pairs.append(jnp.stack([jnp.where(wrapped, row_1, own), jnp.where(wrapped, row_2, row_1)]))
+    return blocks, pairs
+
+
+def to_peers(pairs):
+    return [along_z(pair, e) for e, pair in zip((1, 2, 3), pairs)]
+
+
+def across(x, axis_step):
+    return lax.ppermute(x, "ctx", [(i, i ^ axis_step) for i in range(16)])
+
+
+def swap_sum(x, axis_step, after=()):
+    (total,) = small_call(
+        swap_sum_kernel,
+        in_vmem(2) + [anywhere()] * len(after),
+        [(x.shape, BF)],
+        "swap_sum",
+        1,
+    )(x, across(x, axis_step), *after)
+    return total
+
+
+def swap_sum_kernel(own, got, *refs):
+    refs[-1][...] = (own[...].astype(F32) + got[...].astype(F32)).astype(BF)
+
+
+def in_vmem(count):
+    return [pl.BlockSpec(memory_space=pltpu.VMEM)] * count
+
+
+def small_call(kernel, specs, shapes, name, us, scratch=(), grid=()):
+    return pl.pallas_call(
+        kernel,
+        grid=grid,
+        in_specs=specs,
+        out_specs=in_vmem(len(shapes)),
+        out_shape=[jax.ShapeDtypeStruct(shape, dtype) for shape, dtype in shapes],
+        scratch_shapes=list(scratch),
+        compiler_params=pltpu.CompilerParams(vmem_limit_bytes=SMALL_VMEM),
+        cost_estimate=pl.CostEstimate(
+            flops=us << 30, bytes_accessed=us << 21, transcendentals=0
+        ),
+        name=name,
+    )
+
+
+def values_kernel(product, low_rank, up, _after, out):
+    out[...] = (product[...] + ADAPTER_SCALE * dot(low_rank[...], up[...])).astype(BF)
+
+
+def gate_kernel(*refs):
+    pass
+
+
+def gate(arrays, after):
+    return pl.pallas_call(
+        gate_kernel,
+        in_specs=[anywhere()] * (len(arrays) + 1),
+        out_specs=[anywhere()] * len(arrays),
+        out_shape=[jax.ShapeDtypeStruct(array.shape, array.dtype) for array in arrays],
+        input_output_aliases={n: n for n in range(len(arrays))},
+        name="gate",
+    )(*arrays, after)
+
+
+def sum_terms(terms):
+    total = terms[0][...].astype(F32)
+    for term in terms[1:]:
+        total = total + term[...].astype(F32)
+    return total.astype(BF)
+
+
+def key_grad_kernel(*refs):
+    refs[-1][...] = sum_terms(refs[:-1])
+
+
+def row_sums_kernel(z_ref, own, *refs):
+    *got, _after, here_out, near_out, far_out = refs
+    here_row, row_1, row_2 = (own[n].astype(F32) for n in range(3))
+    for n, pair in enumerate(got):
+        before = z_ref[0] + 1 + n > 3
+        near, far = pair[0].astype(F32), pair[1].astype(F32)
+        here_row = here_row + jnp.where(before, 0.0, near)
+        row_1 = row_1 + jnp.where(before, near, far)
+        row_2 = row_2 + jnp.where(before, far, 0.0)
+    here_out[...] = here_row
+    near_out[...] = row_1.astype(BF)
+    far_out[...] = row_2.astype(BF)
+
+
+def sum_kernel(*refs):
+    refs[-1][...] = sum_terms(refs[:4])
+
+
+def adapter_kernel(core_ref, *refs):
+    up, low_rank, rows, grad_out, middle_out, keep_out, send_out = refs[3:]
+    grad = sum_terms(refs[:3])
+    grad_out[...] = grad
+    middle = (ADAPTER_SCALE * dot(grad, up[...], NT)).astype(BF)
+    middle_out[...] = middle
+    middle_t = middle.astype(F32).T.astype(BF)
+    low_rank_t = low_rank[...].astype(F32).T.astype(BF)
+    half = keep_out.shape[0]
+    model = rows.shape[1]
+    first = core_ref[0] == 0
+
+    def split(part, columns):
+        low, high = part[:half].astype(BF), part[half:].astype(BF)
+        keep_out[:, columns] = jnp.where(first, low, high)
+        send_out[:, columns] = jnp.where(first, high, low)
+
+    step = 1024
+    for n in range(model // step):
+        columns = slice(n * step, (n + 1) * step)
+        split(dot(middle_t, rows[:, columns]), columns)
+    split(ADAPTER_SCALE * dot(low_rank_t, grad), slice(model, model + KV))
+
+
+def quarters_kernel(y_ref, keep, got, mine_out, *send_outs):
+    part = mine_out.shape[1]
+    for e, out in enumerate((mine_out,) + send_outs):
+        first = lax.rem(y_ref[0] + e, 4) * part
+        columns = pl.ds(pl.multiple_of(first, HEAD), part)
+        out[...] = (keep[:, columns].astype(F32) + got[:, columns].astype(F32)).astype(BF)
+
+
+def assemble_kernel(y_ref, *refs):
+    *parts, _d_key, _slots, out = refs
+    width = parts[0].shape[1]
+    for e, part in enumerate(parts):
+        first = lax.rem(y_ref[0] + 4 - e, 4) * width
+        out[:, pl.ds(pl.multiple_of(first, HEAD), width)] = part[...]
+
+
+def totals_kernel(core_ref, mine, other, down_out, up_out):
+    half = mine.shape[0]
+    model = down_out.shape[1]
+    first = core_ref[0] == 0
+    step = 512
+
+    def whole(columns):
+        a, b = mine[:, columns].astype(F32), other[:, columns].astype(F32)
+        return jnp.concatenate([jnp.where(first, a, b), jnp.where(first, b, a)], axis=0)
+
+    for n in range(model // step):
+        columns = slice(n * step, (n + 1) * step)
+        down_out[:, columns] = whole(columns)
+    up_out[...] = whole(slice(model, model + KV))
+
+
+def slots_kernel(got, out, rows):
+    for slot in range(CAP):
+        rows[pl.ds(slot, got.shape[0], stride=CAP), 0:HQ] = got[:, 0, slot * HQ : (slot + 1) * HQ]
+    out[...] = rows[...].T[:HQ]
+
+
+def sum_home(parts, z, after):
+    got = [along_z(part, -distance) for distance, part in zip((3, 2, 1), parts[1:])]
+    here_row, near, far = small_call(
+        row_sums_kernel,
+        [smem()] + in_vmem(4) + [anywhere()],
+        [((TOK, KV), F32), ((TOK, KV), BF), ((TOK, KV), BF)],
+        "row_sums",
+        1,
+    )(z, parts[0], *got[::-1], after)
+    return here_row, along_x(near, -1), along_x(far, -2)
 
 
 def local(
@@ -345,77 +490,89 @@
 ):
     ctx = lax.axis_index("ctx")
     dp = lax.axis_index("dp")
-    z, y, core = ctx % 4, dp // 2, dp % 2
+    y, core = dp // 2, dp % 2
     rows = normed[0]
     low_rank = dot(rows, adapter_down).astype(BF)
-    values = (dot(rows, value_weight) + ADAPTER_SCALE * dot(low_rank, adapter_up)).astype(BF)
     doc_rows = jnp.broadcast_to(
         jnp.tile(document_index.astype(BF), (1, KV // TOK)), (DOC_ROWS, KV)
     )
-    key_own = from_rows(jnp.concatenate([rotated_keys[0], doc_rows], axis=0))
-    value_own = from_rows(values)
-    key_parts = key_own + from_peers(key_own, z)
-    value_parts = value_own + from_peers(value_own, z)
-    here = ctx.reshape(1)
-    lse, send_lse, *dv_parts = run_scores(
+    z = ctx % 4
+    key_own, key_pairs = for_peers(jnp.concatenate([rotated_keys[0], doc_rows], axis=0), z)
+    (values,) = small_call(
+        values_kernel, in_vmem(3) + [anywhere()], [((TOK, KV), BF)], "values", 1
+    )(dot(rows, value_weight), low_rank, adapter_up, key_own[1])
+    value_own, value_pairs = for_peers(values, z)
+    key_parts = key_own + to_peers(key_pairs)
+    value_parts = value_own + to_peers(value_pairs)
+    here, z, y, core = (n.reshape(1) for n in (ctx, z, y, core))
+    lse, own_lse, *dv_parts = run_scores(
         here,
         document_index,
         owner_routing.reshape(1, TOK),
         queries[0],
         attention_cotangent[0],
         key_parts,
-    )
-    value_grad = collect(dv_parts[0], dv_parts[1:], z).astype(BF)
+        value_pairs[0],
+    )
     out, dq, *dk_parts = run_grads(
         here, document_index, queries[0], attention_cotangent[0], lse, key_parts, value_parts
     )
-
     peers = lax.axis_size("ctx")
-    lse_rows = lax.all_to_all(
-        send_lse.reshape(peers, 1, CAP * HQ), "ctx", split_axis=0, concat_axis=0, tiled=True
-    ).reshape(peers * CAP, HQ)
-
-    middle = (ADAPTER_SCALE * dot(value_grad, adapter_up, NT)).astype(BF)
-    tn = (((0,), (0,)), ((), ()))
-    down_part = dot(middle, rows, tn).astype(BF)
-    up_part = (ADAPTER_SCALE * dot(low_rank, value_grad, tn)).astype(BF)
-    both = jnp.concatenate([down_part, up_part], axis=1)
-    width = both.shape[1]
-    half = both.shape[0] // 2
-    keep = lax.dynamic_slice(both, (core * half, 0), (half, width))
-    send = lax.dynamic_slice(both, ((1 - core) * half, 0), (half, width))
-    summed = (keep.astype(F32) + other_core(send).astype(F32)).astype(BF)
+    got_lse = lax.all_to_all(own_lse, "ctx", split_axis=0, concat_axis=0, tiled=True)
+    (lse_rows,) = small_call(
+        slots_kernel,
+        in_vmem(1),
+        [((HQ, peers * CAP), F32)],
+        "slots",
+        1,
+        [pltpu.VMEM((peers * CAP, TOK), F32)],
+    )(got_lse)
+
+    dv_terms = sum_home(dv_parts, z, dq)
+
+    rank, model = adapter_up.shape[0], rows.shape[1]
+    half, width = rank // 2, model + KV
     part = width // 4
-
-    def quarter(x, n):
-        return lax.dynamic_slice(x, (0, (n % 4) * part), (half, part))
-
-    mine = quarter(summed, y).astype(F32)
-    for e in (1, 2, 3):
-        mine = mine + along_y(quarter(summed, y + e), e).astype(F32)
-    mine = sum_of_four(sum_of_four(mine.astype(BF), along_x), along_z)
-    whole = jnp.zeros((half, width), BF)
-    for e in range(4):
-        got = along_y(mine, e) if e else mine
-        whole = lax.dynamic_update_slice(whole, got, (0, ((y - e) % 4) * part))
-    other = other_core(whole)
-    total = jnp.concatenate(
-        [jnp.where(core == 0, whole, other), jnp.where(core == 0, other, whole)], axis=0
-    ).astype(F32)
-    model = rows.shape[1]
-    total_down = total[:, :model].T
-    total_up = total[:, model:]
-
-    normed_input_gradient = (dot(value_grad, value_weight, NT) + dot(middle, adapter_down, NT)).astype(BF)
-    d_key = collect(dk_parts[0], dk_parts[1:], z).astype(BF)
+    value_grad, middle, keep, send = small_call(
+        adapter_kernel,
+        [smem()] + in_vmem(6),
+        [((TOK, KV), BF), ((TOK, rank), BF), ((half, width), BF), ((half, width), BF)],
+        "adapter",
+        3,
+    )(core, *dv_terms, adapter_up, low_rank, rows)
+    mine, *sends = small_call(
+        quarters_kernel, [smem()] + in_vmem(2), [((half, part), BF)] * 4, "quarters", 1
+    )(y, keep, other_core(send))
+    normed_input_gradient = (
+        dot(value_grad, value_weight, NT) + dot(middle, adapter_down, NT)
+    ).astype(BF)
+    (mine,) = small_call(
+        sum_kernel, in_vmem(4) + [anywhere()], [((half, part), BF)], "y_sum", 1
+    )(mine, *[along_y(send, e) for e, send in zip((1, 2, 3), sends)], normed_input_gradient)
+    dk_parts[1:] = gate(dk_parts[1:], mine)
+    dk_terms = sum_home(dk_parts, z, here)
+    (d_key,) = small_call(key_grad_kernel, in_vmem(3), [((TOK, KV), BF)], "key_grad", 1)(*dk_terms)
+    for axis_step in (4, 8, 1, 2):
+        mine = swap_sum(mine, axis_step)
+    (whole,) = small_call(
+        assemble_kernel,
+        [smem()] + in_vmem(4) + [anywhere()] * 2,
+        [((half, width), BF)],
+        "assemble",
+        1,
+    )(y, mine, *[along_y(mine, e) for e in (1, 2, 3)], d_key, lse_rows)
+    total_down, total_up = small_call(
+        totals_kernel, [smem()] + in_vmem(2), [((rank, model), F32), ((rank, KV), F32)], "totals", 2
+    )(core, whole, other_core(whole))
+
     return (
         out[None],
         dq[None],
         d_key[None],
         normed_input_gradient[None],
-        total_down,
+        total_down.T,
         total_up,
-        lse_rows[None],
+        lse_rows.T[None],
     )
 
 

time: 186 us -> 157 us (0.84)
  waiting for transfers between devices: 57.6 us -> 25.7 us
  other arithmetic: 15.8 us -> 3.68 us
  Pallas kernels: 31.3 us -> 39.5 us
  starting transfers between devices: 55.3 us -> 62.5 us
  matrix products: 16.1 us -> 13.5 us
    ppermute x15 -> x12, waiting for transfers between devices: 36 us -> 10.3 us  [along_z(): lax.ppermute(x, 'ctx', [(i, i // 4 * 4 + (i + step) % 4) for i in range(1...]
    ppermute x11 -> x8, waiting for transfers between devices: 17.8 us -> 3.17 us  [along_x(): return lax.ppermute(x, 'ctx', [(i, (i + 4 * step) % 16) for i in range(16)])]
    pallas_call x0 -> x15, Pallas kernels: none -> 7.98 us  [the longest x1 2.43 us: local(): small_call(adapter_kernel, [smem()] + in_vmem(6), [((TOK, KV), BF), ((TOK...]
    ppermute x0 -> x4, starting transfers between devices: none -> 7.41 us  [across(): return lax.ppermute(x, 'ctx', [(i, i ^ axis_step) for i in range(16)])]
    convert_element_type x7 -> x0, other arithmetic: 7.25 us -> none  [the longest x2 3.36 us: collect(): from_1 = along_x(row_1.astype(BF), -1)]
    ppermute x0 -> x4, waiting for transfers between devices: none -> 6.7 us  [across(): return lax.ppermute(x, 'ctx', [(i, i ^ axis_step) for i in range(16)])]
    unnamed x31 -> x58, local copies, waits for them, and re-layouts: 3.78 us -> 10.1 us
    ppermute x2, waiting for transfers between devices: 0.01 us -> 2.69 us  [other_core(): return lax.ppermute(x, 'dp', [(i, i ^ 1) for i in range(8)])]
  transfers between devices with their start and end apart: 35 -> 33, of which waited for: 16 -> 13; matrix products, arithmetic and copies ran while one was open for 15% -> 10% of each run, Pallas kernels for 10% -> 22%
where the time goes in v2:
time: 157 us; the launch traced here: 156 us
  starting transfers between devices  62.5 us (40%)
  Pallas kernels  39.5 us (25%)
  waiting for transfers between devices  25.7 us (16%)
  matrix products  13.5 us (9%)
  local copies, waits for them, and re-layouts  10.1 us (6%)
  other arithmetic  3.68 us (2%)
    pallas_call x1, Pallas kernels, run_grads(): pl.pallas_call(grads_kernel, grid=(GROUPS,), in_specs=[smem(), pl.BlockSp...  17.9 us
    ppermute x12, starting transfers between devices, along_z(): lax.ppermute(x, 'ctx', [(i, i // 4 * 4 + (i + step) % 4) for i in range(1...  17.5 us
    pallas_call x1, Pallas kernels, run_scores(): pl.pallas_call(scores_kernel, grid=(GROUPS,), in_specs=[smem(), line, lin...  13.6 us
    dot_general x4, matrix products, dot(): return lax.dot_general(a, b, dims, preferred_element_type=F32)  13.5 us
    ppermute x8, starting transfers between devices, along_x(): return lax.ppermute(x, 'ctx', [(i, (i + 4 * step) % 16) for i in range(16)])  12.5 us
    ppermute x2, starting transfers between devices, other_core(): return lax.ppermute(x, 'dp', [(i, i ^ 1) for i in range(8)])  12.1 us
    ppermute x12, waiting for transfers between devices, along_z(): lax.ppermute(x, 'ctx', [(i, i // 4 * 4 + (i + step) % 4) for i in range(1...  10.3 us
    unnamed x58, local copies, waits for them, and re-layouts  10.1 us
  transfers between devices with their start and end apart: 33, of which 13 were waited for; matrix products, arithmetic and copies ran while one was open for 10% of the time, Pallas kernels for 22%

profile of v2, /device:TPU:1, one launch (start us, length us, event | category | flops | bytes accessed | tf_op | source)
XLA Modules:
  0.0 155.9 jit_solution(16198776506486555120)
XLA Ops:
  0.6 0.7 convert_bitcast_fusion
  1.4 0.6 copy-done.20
  2.0 1.6 %pad_maximum_fusion.6.rest_0_ = bf16[144,512]{1,0:T(8,128)(2,1)} fusion(bf16[16,512]{1,0:T(8,128)(2,1)S(1)} %broadcast_in_dim.20, bf16[128,512]{1,0:T(8,128)(2,1)} %bitcast.60), kind=kLoop, calls=%fused_computation.9 | loop fusion | flops 294912 | bytes 294912 | tf_op jit(solution)/shard_map/concatenate | solution.py:500
  3.6 2.0 %collective-permute-start = (bf16[144,512]{1,0:T(8,128)(2,1)}, bf16[144,512]{1,0:T(8,128)(2,1)S(1)}, u32[]{:S(2)}, u32[]{:S(2)}) collective-permute-start(bf16[144,512]{1,0:T(8,128)(2,1)} %pad_maximum_fusion.6.rest_0_), channel_id=1, source_target_pairs={{0,4},{1,5},{2,6},{3,7},{4,8},{5,9},{6,10},{7,11},{8,12},{9,13},{1... | collective-permute-start | bytes 442376 | tf_op jit(solution)/shard_map/ppermute | solution.py:294
  5.6 2.5 %collective-permute-start.1 = (bf16[144,512]{1,0:T(8,128)(2,1)}, bf16[144,512]{1,0:T(8,128)(2,1)}, u32[]{:S(2)}, u32[]{:S(2)}) collective-permute-start(bf16[144,512]{1,0:T(8,128)(2,1)} %pad_maximum_fusion.6.rest_0_), channel_id=1, source_target_pairs={{0,8},{1,9},{2,10},{3,11},{4,12},{5,13},{6,14},{7,15},{8,0},{9,1},... | collective-permute-start | bytes 442376 | tf_op jit(solution)/shard_map/ppermute | solution.py:294
  8.1 5.3 %fusion.2.product = f32[128,512]{1,0:T(8,128)S(1)} fusion(bf16[8192,512]{1,0:T(8,128)(2,1)} %param.12, bf16[1,128,8192]{2,1,0:T(8,128)(2,1)} %param.9), kind=kOutput, calls=%fused_computation.25 | convolution fusion | flops 1073741824 | bytes 10747904 | tf_op jit(solution)/shard_map/dot_general | solution.py:38
  13.4 1.3 convolution_convert_fusion.low_rank.refs_4_
  14.7 0.8 copy-done.6
  15.5 0.8 copy-done.8
  16.6 2.3 %collective-permute-start.6 = (bf16[128,512]{1,0:T(8,128)(2,1)S(1)}, bf16[128,512]{1,0:T(8,128)(2,1)S(1)}, u32[]{:S(2)}, u32[]{:S(2)}) collective-permute-start(bf16[128,512]{1,0:T(8,128)(2,1)S(1)} %values.1.rest_6_), channel_id=1, source_target_pairs={{0,8},{1,9},{2,10},{3,11},{4,12},{5,13},{6,14},{7,15},{8,0},{9,1},... | collective-permute-start | bytes 393224 | tf_op jit(solution)/shard_map/ppermute | solution.py:294
  18.9 1.1 select_bitcast_fusion.1
  20.1 1.7 %collective-permute-start.2 = (bf16[2,144,512]{2,1,0:T(8,128)(2,1)S(1)}, bf16[2,144,512]{2,1,0:T(8,128)(2,1)S(1)}, u32[]{:S(2)}, u32[]{:S(2)}) collective-permute-start(bf16[2,144,512]{2,1,0:T(8,128)(2,1)S(1)} %pad_maximum_fusion), channel_id=1, source_target_pairs={{0,1},{1,2},{2,3},{3,0},{4,5},{5,6},{6,7},{7,4},{8,9},{9,10},{10,1... | collective-permute-start | bytes 884744 | tf_op jit(solution)/shard_map/ppermute | solution.py:290
  21.8 3.4 %collective-permute-start.3 = (bf16[2,144,512]{2,1,0:T(8,128)(2,1)S(1)}, bf16[2,144,512]{2,1,0:T(8,128)(2,1)S(1)}, u32[]{:S(2)}, u32[]{:S(2)}) collective-permute-start(bf16[2,144,512]{2,1,0:T(8,128)(2,1)S(1)} %pad_maximum_fusion.1), channel_id=1, source_target_pairs={{0,2},{1,3},{2,0},{3,1},{4,6},{5,7},{6,4},{7,5},{8,10},{9,11},{10,... | collective-permute-start | bytes 884744 | tf_op jit(solution)/shard_map/ppermute | solution.py:290
  25.2 0.8 collective-permute-start.4
  26.2 0.8 collective-permute-start.7
  27.0 1.9 %collective-permute-start.8 = (bf16[2,128,512]{2,1,0:T(8,128)(2,1)S(1)}, bf16[2,128,512]{2,1,0:T(8,128)(2,1)S(1)}, u32[]{:S(2)}, u32[]{:S(2)}) collective-permute-start(bf16[2,128,512]{2,1,0:T(8,128)(2,1)S(1)} %pad_maximum_fusion.4), channel_id=1, source_target_pairs={{0,2},{1,3},{2,0},{3,1},{4,6},{5,7},{6,4},{7,5},{8,10},{9,11},{10,... | collective-permute-start | bytes 786440 | tf_op jit(solution)/shard_map/ppermute | solution.py:290
  29.4 1.2 collective-permute-start.9
  30.6 6.1 %collective-permute-done.3.rest_4_ = bf16[2,144,512]{2,1,0:T(8,128)(2,1)S(1)} collective-permute-done((bf16[2,144,512]{2,1,0:T(8,128)(2,1)S(1)}, bf16[2,144,512]{2,1,0:T(8,128)(2,1)S(1)}, u32[]{:S(2)}, u32[]{:S(2)}) %collective-permute-start.3) | collective-permute-done | bytes 294944 | tf_op jit(solution)/shard_map/ppermute | solution.py:290
  36.7 2.0 %collective-permute-done.4.rest_5_ = bf16[2,144,512]{2,1,0:T(8,128)(2,1)S(1)} collective-permute-done((bf16[2,144,512]{2,1,0:T(8,128)(2,1)S(1)}, bf16[2,144,512]{2,1,0:T(8,128)(2,1)S(1)}, u32[]{:S(2)}, u32[]{:S(2)}) %collective-permute-start.4) | collective-permute-done | bytes 294944 | tf_op jit(solution)/shard_map/ppermute | solution.py:290
  38.7 0.7 copy-done.25
  39.4 13.6 %scores.1 = (f32[4,8,128]{2,1,0:T(8,128)}, f32[16,1,384]{2,1,0:T(1,128)}, bf16[3,128,512]{2,1,0:T(8,128)(2,1)}, bf16[2,128,512]{2,1,0:T(8,128)(2,1)}, bf16[2,128...) custom-call(s32[1]{0:T(128)} %bitcast.here_ref.refs_3_, s32[1,128]{1,0:T(1,128)} %docs_ref.3, s32[1,128]{1,0:T(1,128)} %bitcast.66, ...), custom_call_target="tpu_custom_call" | custom-call | flops 34359738368 | bytes 6291456 | tf_op jit(solution)/shard_map/scores/pallas_call | solution.py:224
  53.0 4.0 %collective-permute-start.10 = (bf16[2,128,512]{2,1,0:T(8,128)(2,1)}, bf16[2,128,512]{2,1,0:T(8,128)(2,1)S(1)}, u32[]{:S(2)}, u32[]{:S(2)}) collective-permute-start(bf16[2,128,512]{2,1,0:T(8,128)(2,1)} %get-tuple-element.46), channel_id=1, source_target_pairs={{0,3},{1,0},{2,1},{3,2},{4,7},{5,4},{6,5},{7,6},{8,11},{9,8},{10,9... | collective-permute-start | bytes 786440 | tf_op jit(solution)/shard_map/ppermute | solution.py:290
  58.5 17.9 %grads.1 = (bf16[128,4096]{1,0:T(8,128)(2,1)}, bf16[128,4096]{1,0:T(8,128)(2,1)}, bf16[3,128,512]{2,1,0:T(8,128)(2,1)}, bf16[2,128,512]{2,1,0:T(8,128)(2,1)}, bf...) custom-call(s32[1]{0:T(128)} %bitcast.here_ref.refs_3_, s32[1,128]{1,0:T(1,128)} %docs_ref.3, ...), custom_call_target="tpu_custom_call" | custom-call | flops 68719476736 | bytes 8388608 | tf_op jit(solution)/shard_map/grads/pallas_call | solution.py:257
  76.5 1.2 copy-done.10
  77.7 0.8 row_sums.2
  78.5 0.7 copy-done.14
  79.6 2.3 %collective-permute-start.14 = (bf16[128,512]{1,0:T(8,128)(2,1)S(1)}, bf16[128,512]{1,0:T(8,128)(2,1)}, u32[]{:S(2)}, u32[]{:S(2)}) collective-permute-start(bf16[128,512]{1,0:T(8,128)(2,1)S(1)} %get-tuple-element.51), channel_id=1, source_target_pairs={{0,8},{1,9},{2,10},{3,11},{4,12},{5,13},{6,14},{7,15},{8,0},{9,1},... | collective-permute-start | bytes 393224 | tf_op jit(solution)/shard_map/ppermute | solution.py:294
  81.9 1.3 collective-permute-done.13.refs_1_
  83.2 1.8 %collective-permute-done.14.refs_2_ = bf16[128,512]{1,0:T(8,128)(2,1)} collective-permute-done((bf16[128,512]{1,0:T(8,128)(2,1)S(1)}, bf16[128,512]{1,0:T(8,128)(2,1)}, u32[]{:S(2)}, u32[]{:S(2)}) %collective-permute-start.14) | collective-permute-done | bytes 131104 | tf_op jit(solution)/shard_map/ppermute | solution.py:294
  85.1 0.9 copy-done.15
  86.0 2.4 %adapter.1 = (bf16[128,512]{1,0:T(8,128)(2,1)S(1)}, bf16[128,64]{1,0:T(8,128)(2,1)S(1)}, bf16[32,8704]{1,0:T(8,128)(2,1)S(1)}, bf16[32,8704]{1,0:T(8,128)(2,1)}) custom-call(s32[1]{0:T(128)} %bitcast.24.core_ref, f32[128,512]{1,0:T(8,128)S(1)} %copy-done.15, bf16[128,512]{1,0:T(8,128)(2,1)S(1)} %collective-permute-done.13.refs_1_, ...), custom_call_target="tpu_custom_call" | custom-call | flops 3221225472 | bytes 6291456 | tf_op jit(solution)/shard_map/adapter/pallas_call | solution.py:536
  88.4 0.8 copy-done.16
  89.2 4.7 %collective-permute-start.15 = (bf16[32,8704]{1,0:T(8,128)(2,1)}, bf16[32,8704]{1,0:T(8,128)(2,1)S(1)}, u32[]{:S(2)}, u32[]{:S(2)}) collective-permute-start(bf16[32,8704]{1,0:T(8,128)(2,1)} %get-tuple-element.53), channel_id=1, source_target_pairs={{0,16},{16,0},{32,48},{48,32},{64,80},{80,64},{96,112},{112,96},{1... | collective-permute-start | bytes 1671176 | tf_op jit(solution)/shard_map/ppermute | solution.py:302
  93.9 0.7 fusion.4
  94.6 1.1 collective-permute-done.15.got
  95.9 1.4 collective-permute-start.16
  97.2 2.6 %collective-permute-start.17 = (bf16[32,2176]{1,0:T(8,128)(2,1)S(1)}, bf16[32,2176]{1,0:T(8,128)(2,1)S(1)}, u32[]{:S(2)}, u32[]{:S(2)}) collective-permute-start(bf16[32,2176]{1,0:T(8,128)(2,1)S(1)} %get-tuple-element.56), channel_id=1, source_target_pairs={{0,64},{16,80},{32,96},{48,112},{64,0},{80,16},{96,32},{112,48},{1... | collective-permute-start | bytes 417800 | tf_op jit(solution)/shard_map/ppermute | solution.py:298
  99.8 1.1 collective-permute-start.18
  100.9 6.2 %fusion.refs_4_ = bf16[128,8192]{1,0:T(8,128)(2,1)S(1)} fusion(f32[128,8192]{1,0:T(8,128)S(1)} %fusion.4, bf16[128,512]{1,0:T(8,128)(2,1)S(1)} %get-tuple-element.58, bf16[8192,512]{1,0:T(8,128)(2,1)} %param.12), kind=kOutput, calls=%fused_computation.1 | convolution fusion | flops 1075838976 | bytes 14811136 | tf_op jit(solution)/shard_map/dot_general | solution.py:38
  107.2 1.1 collective-permute-start.24
  108.4 2.8 %collective-permute-done.24.got = bf16[32,2176]{1,0:T(8,128)(2,1)S(1)} collective-permute-done((bf16[32,2176]{1,0:T(8,128)(2,1)S(1)}, bf16[32,2176]{1,0:T(8,128)(2,1)S(1)}, u32[]{:S(2)}, u32[]{:S(2)}) %collective-permute-start.24) | collective-permute-done | bytes 139296 | tf_op jit(solution)/shard_map/ppermute | solution.py:320
  111.3 2.3 %collective-permute-start.25 = (bf16[32,2176]{1,0:T(8,128)(2,1)S(1)}, bf16[32,2176]{1,0:T(8,128)(2,1)S(1)}, u32[]{:S(2)}, u32[]{:S(2)}) collective-permute-start(bf16[32,2176]{1,0:T(8,128)(2,1)S(1)} %swap_sum.4.own), channel_id=1, source_target_pairs={{0,8},{1,9},{2,10},{3,11},{4,12},{5,13},{6,14},{7,15},{8,0},{9,1},... | collective-permute-start | bytes 417800 | tf_op jit(solution)/shard_map/ppermute | solution.py:320
  113.6 3.1 %collective-permute-done.25.got = bf16[32,2176]{1,0:T(8,128)(2,1)S(1)} collective-permute-done((bf16[32,2176]{1,0:T(8,128)(2,1)S(1)}, bf16[32,2176]{1,0:T(8,128)(2,1)S(1)}, u32[]{:S(2)}, u32[]{:S(2)}) %collective-permute-start.25) | collective-permute-done | bytes 139296 | tf_op jit(solution)/shard_map/ppermute | solution.py:320
  116.8 1.9 %collective-permute-start.26 = (bf16[32,2176]{1,0:T(8,128)(2,1)S(1)}, bf16[32,2176]{1,0:T(8,128)(2,1)}, u32[]{:S(2)}, u32[]{:S(2)}) collective-permute-start(bf16[32,2176]{1,0:T(8,128)(2,1)S(1)} %swap_sum.5.own), channel_id=1, source_target_pairs={{0,1},{1,0},{2,3},{3,2},{4,5},{5,4},{6,7},{7,6},{8,9},{9,8},{10,11... | collective-permute-start | bytes 417800 | tf_op jit(solution)/shard_map/ppermute | solution.py:320
  118.7 1.2 collective-permute-start.19
  119.9 1.1 collective-permute-start.20
  121.0 0.9 collective-permute-start.21
  121.8 0.9 swap_sum.6.own
  122.8 2.0 %collective-permute-start.27 = (bf16[32,2176]{1,0:T(8,128)(2,1)S(1)}, bf16[32,2176]{1,0:T(8,128)(2,1)S(1)}, u32[]{:S(2)}, u32[]{:S(2)}) collective-permute-start(bf16[32,2176]{1,0:T(8,128)(2,1)S(1)} %swap_sum.6.own), channel_id=1, source_target_pairs={{0,2},{1,3},{2,0},{3,1},{4,6},{5,7},{6,4},{7,5},{8,10},{9,11},{10,... | collective-permute-start | bytes 417800 | tf_op jit(solution)/shard_map/ppermute | solution.py:320
  124.8 4.9 %all-to-all-start = ((f32[16,1,384]{2,1,0:T(1,128)}), f32[16,1,384]{2,1,0:T(1,128)S(1)}, u32[]{:S(2)}, u32[]{:S(2)}) async-start(f32[16,1,384]{2,1,0:T(1,128)} %get-tuple-element.66), calls=%async_computation | async-start | bytes 49152 | tf_op jit(solution)/shard_map/all_to_all | solution.py:521
  129.7 1.7 %collective-permute-done.21.refs_2_ = bf16[2,128,512]{2,1,0:T(8,128)(2,1)S(1)} collective-permute-done((bf16[2,128,512]{2,1,0:T(8,128)(2,1)}, bf16[2,128,512]{2,1,0:T(8,128)(2,1)S(1)}, u32[]{:S(2)}, u32[]{:S(2)}) %collective-permute-start.21) | collective-permute-done | bytes 262176 | tf_op jit(solution)/shard_map/ppermute | solution.py:290
  131.5 1.0 copy-done.18
  132.8 1.9 %collective-permute-start.22 = (bf16[128,512]{1,0:T(8,128)(2,1)S(1)}, bf16[128,512]{1,0:T(8,128)(2,1)S(1)}, u32[]{:S(2)}, u32[]{:S(2)}) collective-permute-start(bf16[128,512]{1,0:T(8,128)(2,1)S(1)} %get-tuple-element.64), channel_id=1, source_target_pairs={{0,12},{1,13},{2,14},{3,15},{4,0},{5,1},{6,2},{7,3},{8,4},{9,5},{1... | collective-permute-start | bytes 393224 | tf_op jit(solution)/shard_map/ppermute | solution.py:294
  134.7 1.0 collective-permute-start.23
  135.7 0.7 collective-permute-done.27.got
  136.9 1.9 %collective-permute-start.29 = (bf16[32,2176]{1,0:T(8,128)(2,1)S(1)}, bf16[32,2176]{1,0:T(8,128)(2,1)S(1)}, u32[]{:S(2)}, u32[]{:S(2)}) collective-permute-start(bf16[32,2176]{1,0:T(8,128)(2,1)S(1)} %swap_sum.7.refs_0_), channel_id=1, source_target_pairs={{0,64},{16,80},{32,96},{48,112},{64,0},{80,16},{96,32},{112,48},{1... | collective-permute-start | bytes 417800 | tf_op jit(solution)/shard_map/ppermute | solution.py:298
  139.4 0.8 slots.1.refs_5_
  140.2 0.7 key_grad.1.refs_4_
  140.9 2.5 %collective-permute-done.28.refs_1_ = bf16[32,2176]{1,0:T(8,128)(2,1)S(1)} collective-permute-done((bf16[32,2176]{1,0:T(8,128)(2,1)S(1)}, bf16[32,2176]{1,0:T(8,128)(2,1)S(1)}, u32[]{:S(2)}, u32[]{:S(2)}) %collective-permute-start.28) | collective-permute-done | bytes 139296 | tf_op jit(solution)/shard_map/ppermute | solution.py:298
  143.8 0.9 copy-done.11
  144.7 0.8 copy-done.12
  145.5 7.4 %collective-permute-start.31 = (bf16[32,8704]{1,0:T(8,128)(2,1)S(1)}, bf16[32,8704]{1,0:T(8,128)(2,1)S(1)}, u32[]{:S(2)}, u32[]{:S(2)}) collective-permute-start(bf16[32,8704]{1,0:T(8,128)(2,1)S(1)} %assemble.1.mine), channel_id=1, source_target_pairs={{0,16},{16,0},{32,48},{48,32},{64,80},{80,64},{96,112},{112,96},{1... | collective-permute-start | bytes 1671176 | tf_op jit(solution)/shard_map/ppermute | solution.py:302
  152.9 1.6 %collective-permute-done.31.other = bf16[32,8704]{1,0:T(8,128)(2,1)S(1)} collective-permute-done((bf16[32,8704]{1,0:T(8,128)(2,1)S(1)}, bf16[32,8704]{1,0:T(8,128)(2,1)S(1)}, u32[]{:S(2)}, u32[]{:S(2)}) %collective-permute-start.31) | collective-permute-done | bytes 557088 | tf_op jit(solution)/shard_map/ppermute | solution.py:302
  154.4 1.5 totals.1
  (93 shorter events, 5.0 us)
Async XLA Ops:
  0.6 12.7 %copy-start = (bf16[8192,64]{0,1:T(8,128)(2,1)S(1)}, bf16[8192,64]{0,1:T(8,128)(2,1)}, u32[]{:S(2)}) copy-start(bf16[8192,64]{0,1:T(8,128)(2,1)} %param.13) | copy-start | bytes 3145732
  1.4 0.6 copy-start.20
  3.6 9.8 %copy-start.1 = (bf16[1,128,8192]{2,1,0:T(8,128)(2,1)S(1)}, bf16[1,128,8192]{2,1,0:T(8,128)(2,1)}, u32[]{:S(2)}) copy-start(bf16[1,128,8192]{2,1,0:T(8,128)(2,1)} %param.9) | copy-start | bytes 6291460
  3.6 11.1 %collective-permute-start = (bf16[144,512]{1,0:T(8,128)(2,1)}, bf16[144,512]{1,0:T(8,128)(2,1)S(1)}, u32[]{:S(2)}, u32[]{:S(2)}) collective-permute-start(bf16[144,512]{1,0:T(8,128)(2,1)} %pad_maximum_fusion.6.rest_0_), channel_id=1, source_target_pairs={{0,4},{1,5},{2,6},{3,7},{4,8},{5,9},{6,10},{7,11},{8,12},{9,13},{1... | collective-permute-start | bytes 442376 | tf_op jit(solution)/shard_map/ppermute | solution.py:294
  5.6 13.3 %collective-permute-start.1 = (bf16[144,512]{1,0:T(8,128)(2,1)}, bf16[144,512]{1,0:T(8,128)(2,1)}, u32[]{:S(2)}, u32[]{:S(2)}) collective-permute-start(bf16[144,512]{1,0:T(8,128)(2,1)} %pad_maximum_fusion.6.rest_0_), channel_id=1, source_target_pairs={{0,8},{1,9},{2,10},{3,11},{4,12},{5,13},{6,14},{7,15},{8,0},{9,1},... | collective-permute-start | bytes 442376 | tf_op jit(solution)/shard_map/ppermute | solution.py:294
  14.7 0.8 copy-start.6
  15.4 0.8 copy-start.8
  16.3 9.9 %copy-start.3 = (bf16[144,512]{1,0:T(8,128)(2,1)}, bf16[144,512]{1,0:T(8,128)(2,1)S(1)}, u32[]{:S(2)}) copy-start(bf16[144,512]{1,0:T(8,128)(2,1)S(1)} %collective-permute-done._after.rest_1_) | copy-start | bytes 442372
  16.5 36.5 %copy-start.5 = (bf16[128,512]{1,0:T(8,128)(2,1)}, bf16[128,512]{1,0:T(8,128)(2,1)S(1)}, u32[]{:S(2)}) copy-start(bf16[128,512]{1,0:T(8,128)(2,1)S(1)} %values.1.rest_6_) | copy-start | bytes 393220
  16.5 9.6 %collective-permute-start.5 = (bf16[128,512]{1,0:T(8,128)(2,1)S(1)}, bf16[128,512]{1,0:T(8,128)(2,1)S(1)}, u32[]{:S(2)}, u32[]{:S(2)}) collective-permute-start(bf16[128,512]{1,0:T(8,128)(2,1)S(1)} %values.1.rest_6_), channel_id=1, source_target_pairs={{0,4},{1,5},{2,6},{3,7},{4,8},{5,9},{6,10},{7,11},{8,12},{9,13},{1... | collective-permute-start | bytes 393224 | tf_op jit(solution)/shard_map/ppermute | solution.py:294
  16.6 9.5 %collective-permute-start.6 = (bf16[128,512]{1,0:T(8,128)(2,1)S(1)}, bf16[128,512]{1,0:T(8,128)(2,1)S(1)}, u32[]{:S(2)}, u32[]{:S(2)}) collective-permute-start(bf16[128,512]{1,0:T(8,128)(2,1)S(1)} %values.1.rest_6_), channel_id=1, source_target_pairs={{0,8},{1,9},{2,10},{3,11},{4,12},{5,13},{6,14},{7,15},{8,0},{9,1},... | collective-permute-start | bytes 393224 | tf_op jit(solution)/shard_map/ppermute | solution.py:294
  20.1 9.3 %collective-permute-start.2 = (bf16[2,144,512]{2,1,0:T(8,128)(2,1)S(1)}, bf16[2,144,512]{2,1,0:T(8,128)(2,1)S(1)}, u32[]{:S(2)}, u32[]{:S(2)}) collective-permute-start(bf16[2,144,512]{2,1,0:T(8,128)(2,1)S(1)} %pad_maximum_fusion), channel_id=1, source_target_pairs={{0,1},{1,2},{2,3},{3,0},{4,5},{5,6},{6,7},{7,4},{8,9},{9,10},{10,1... | collective-permute-start | bytes 884744 | tf_op jit(solution)/shard_map/ppermute | solution.py:290
  21.8 14.9 %collective-permute-start.3 = (bf16[2,144,512]{2,1,0:T(8,128)(2,1)S(1)}, bf16[2,144,512]{2,1,0:T(8,128)(2,1)S(1)}, u32[]{:S(2)}, u32[]{:S(2)}) collective-permute-start(bf16[2,144,512]{2,1,0:T(8,128)(2,1)S(1)} %pad_maximum_fusion.1), channel_id=1, source_target_pairs={{0,2},{1,3},{2,0},{3,1},{4,6},{5,7},{6,4},{7,5},{8,10},{9,11},{10,... | collective-permute-start | bytes 884744 | tf_op jit(solution)/shard_map/ppermute | solution.py:290
  25.2 13.5 %collective-permute-start.4 = (bf16[2,144,512]{2,1,0:T(8,128)(2,1)S(1)}, bf16[2,144,512]{2,1,0:T(8,128)(2,1)S(1)}, u32[]{:S(2)}, u32[]{:S(2)}) collective-permute-start(bf16[2,144,512]{2,1,0:T(8,128)(2,1)S(1)} %pad_maximum_fusion.2), channel_id=1, source_target_pairs={{0,3},{1,0},{2,1},{3,2},{4,7},{5,4},{6,5},{7,6},{8,11},{9,8},{10,9... | collective-permute-start | bytes 884744 | tf_op jit(solution)/shard_map/ppermute | solution.py:290
  26.0 27.0 %copy-start.21 = (bf16[128,512]{1,0:T(8,128)(2,1)}, bf16[128,512]{1,0:T(8,128)(2,1)S(1)}, u32[]{:S(2)}) copy-start(bf16[128,512]{1,0:T(8,128)(2,1)S(1)} %collective-permute-done.5.rest_7_) | copy-start | bytes 393220
  26.0 27.0 %copy-start.22 = (bf16[128,512]{1,0:T(8,128)(2,1)}, bf16[128,512]{1,0:T(8,128)(2,1)S(1)}, u32[]{:S(2)}) copy-start(bf16[128,512]{1,0:T(8,128)(2,1)S(1)} %collective-permute-done.6.rest_8_) | copy-start | bytes 393220
  26.2 12.5 %copy-start.19 = (bf16[2,128,512]{2,1,0:T(8,128)(2,1)}, bf16[2,128,512]{2,1,0:T(8,128)(2,1)S(1)}, u32[]{:S(2)}) copy-start(bf16[2,128,512]{2,1,0:T(8,128)(2,1)S(1)} %pad_maximum_fusion.3.rest_6_) | copy-start | bytes 786436
  26.2 31.2 %collective-permute-start.7 = (bf16[2,128,512]{2,1,0:T(8,128)(2,1)S(1)}, bf16[2,128,512]{2,1,0:T(8,128)(2,1)S(1)}, u32[]{:S(2)}, u32[]{:S(2)}) collective-permute-start(bf16[2,128,512]{2,1,0:T(8,128)(2,1)S(1)} %pad_maximum_fusion.3.rest_6_), channel_id=1, source_target_pairs={{0,1},{1,2},{2,3},{3,0},{4,5},{5,6},{6,7},{7,4},{8,9},{9,10},{10,1... | collective-permute-start | bytes 786440 | tf_op jit(solution)/shard_map/ppermute | solution.py:290
  27.0 30.7 %collective-permute-start.8 = (bf16[2,128,512]{2,1,0:T(8,128)(2,1)S(1)}, bf16[2,128,512]{2,1,0:T(8,128)(2,1)S(1)}, u32[]{:S(2)}, u32[]{:S(2)}) collective-permute-start(bf16[2,128,512]{2,1,0:T(8,128)(2,1)S(1)} %pad_maximum_fusion.4), channel_id=1, source_target_pairs={{0,2},{1,3},{2,0},{3,1},{4,6},{5,7},{6,4},{7,5},{8,10},{9,11},{10,... | collective-permute-start | bytes 786440 | tf_op jit(solution)/shard_map/ppermute | solution.py:290
  29.4 9.3 %copy-start.23 = (bf16[2,144,512]{2,1,0:T(8,128)(2,1)}, bf16[2,144,512]{2,1,0:T(8,128)(2,1)S(1)}, u32[]{:S(2)}) copy-start(bf16[2,144,512]{2,1,0:T(8,128)(2,1)S(1)} %collective-permute-done.2.rest_3_) | copy-start | bytes 884740
  29.4 28.3 %collective-permute-start.9 = (bf16[2,128,512]{2,1,0:T(8,128)(2,1)S(1)}, bf16[2,128,512]{2,1,0:T(8,128)(2,1)S(1)}, u32[]{:S(2)}, u32[]{:S(2)}) collective-permute-start(bf16[2,128,512]{2,1,0:T(8,128)(2,1)S(1)} %pad_maximum_fusion.5), channel_id=1, source_target_pairs={{0,3},{1,0},{2,1},{3,2},{4,7},{5,4},{6,5},{7,6},{8,11},{9,8},{10,9... | collective-permute-start | bytes 786440 | tf_op jit(solution)/shard_map/ppermute | solution.py:290
  36.7 2.0 %copy-start.24 = (bf16[2,144,512]{2,1,0:T(8,128)(2,1)}, bf16[2,144,512]{2,1,0:T(8,128)(2,1)S(1)}, u32[]{:S(2)}) copy-start(bf16[2,144,512]{2,1,0:T(8,128)(2,1)S(1)} %collective-permute-done.3.rest_4_) | copy-start | bytes 884740
  38.7 0.7 copy-start.25
  53.0 23.4 %collective-permute-start.10 = (bf16[2,128,512]{2,1,0:T(8,128)(2,1)}, bf16[2,128,512]{2,1,0:T(8,128)(2,1)S(1)}, u32[]{:S(2)}, u32[]{:S(2)}) collective-permute-start(bf16[2,128,512]{2,1,0:T(8,128)(2,1)} %get-tuple-element.46), channel_id=1, source_target_pairs={{0,3},{1,0},{2,1},{3,2},{4,7},{5,4},{6,5},{7,6},{8,11},{9,8},{10,9... | collective-permute-start | bytes 786440 | tf_op jit(solution)/shard_map/ppermute | solution.py:290
  57.0 19.4 %collective-permute-start.11 = (bf16[2,128,512]{2,1,0:T(8,128)(2,1)}, bf16[2,128,512]{2,1,0:T(8,128)(2,1)S(1)}, u32[]{:S(2)}, u32[]{:S(2)}) collective-permute-start(bf16[2,128,512]{2,1,0:T(8,128)(2,1)} %get-tuple-element.47), channel_id=1, source_target_pairs={{0,2},{1,3},{2,0},{3,1},{4,6},{5,7},{6,4},{7,5},{8,10},{9,11},{10,... | collective-permute-start | bytes 786440 | tf_op jit(solution)/shard_map/ppermute | solution.py:290
  57.4 0.7 copy-start.26
  57.4 19.0 %collective-permute-start.12 = (bf16[2,128,512]{2,1,0:T(8,128)(2,1)}, bf16[2,128,512]{2,1,0:T(8,128)(2,1)S(1)}, u32[]{:S(2)}, u32[]{:S(2)}) collective-permute-start(bf16[2,128,512]{2,1,0:T(8,128)(2,1)} %get-tuple-element.48), channel_id=1, source_target_pairs={{0,1},{1,2},{2,3},{3,0},{4,5},{5,6},{6,7},{7,4},{8,9},{9,10},{10,1... | collective-permute-start | bytes 786440 | tf_op jit(solution)/shard_map/ppermute | solution.py:290
  57.7 0.7 copy-start.27
  57.7 0.8 copy-start.28
  58.5 18.0 %copy-start.13 = (bf16[3,128,512]{2,1,0:T(8,128)(2,1)S(1)}, bf16[3,128,512]{2,1,0:T(8,128)(2,1)}, u32[]{:S(2)}) copy-start(bf16[3,128,512]{2,1,0:T(8,128)(2,1)} %get-tuple-element.45.own) | copy-start | bytes 1179652
  58.5 26.6 %copy-start.7 = (bf16[128,64]{1,0:T(8,128)(2,1)S(1)}, bf16[128,64]{1,0:T(8,128)(2,1)}, u32[]{:S(2)}) copy-start(bf16[128,64]{1,0:T(8,128)(2,1)} %convolution_convert_fusion.low_rank.refs_4_) | copy-start | bytes 49156
  58.5 26.6 %copy-start.9 = (bf16[64,512]{1,0:T(8,128)(2,1)S(1)}, bf16[64,512]{1,0:T(8,128)(2,1)}, u32[]{:S(2)}) copy-start(bf16[64,512]{1,0:T(8,128)(2,1)} %refs_3_.1) | copy-start | bytes 196612
  76.5 1.2 copy-start.10
  78.5 0.7 copy-start.14
  79.2 4.0 %collective-permute-start.13 = (bf16[128,512]{1,0:T(8,128)(2,1)}, bf16[128,512]{1,0:T(8,128)(2,1)S(1)}, u32[]{:S(2)}, u32[]{:S(2)}) collective-permute-start(bf16[128,512]{1,0:T(8,128)(2,1)} %get-tuple-element.50), channel_id=1, source_target_pairs={{0,12},{1,13},{2,14},{3,15},{4,0},{5,1},{6,2},{7,3},{8,4},{9,5},{1... | collective-permute-start | bytes 393224 | tf_op jit(solution)/shard_map/ppermute | solution.py:294
  79.6 5.4 %collective-permute-start.14 = (bf16[128,512]{1,0:T(8,128)(2,1)S(1)}, bf16[128,512]{1,0:T(8,128)(2,1)}, u32[]{:S(2)}, u32[]{:S(2)}) collective-permute-start(bf16[128,512]{1,0:T(8,128)(2,1)S(1)} %get-tuple-element.51), channel_id=1, source_target_pairs={{0,8},{1,9},{2,10},{3,11},{4,12},{5,13},{6,14},{7,15},{8,0},{9,1},... | collective-permute-start | bytes 393224 | tf_op jit(solution)/shard_map/ppermute | solution.py:294
  85.1 1.0 copy-start.15
  88.4 0.8 copy-start.16
  89.2 6.5 %copy-start.17 = (bf16[32,8704]{1,0:T(8,128)(2,1)S(1)}, bf16[32,8704]{1,0:T(8,128)(2,1)}, u32[]{:S(2)}) copy-start(bf16[32,8704]{1,0:T(8,128)(2,1)} %copy-done.16) | copy-start | bytes 1671172
  89.2 6.5 %collective-permute-start.15 = (bf16[32,8704]{1,0:T(8,128)(2,1)}, bf16[32,8704]{1,0:T(8,128)(2,1)S(1)}, u32[]{:S(2)}, u32[]{:S(2)}) collective-permute-start(bf16[32,8704]{1,0:T(8,128)(2,1)} %get-tuple-element.53), channel_id=1, source_target_pairs={{0,16},{16,0},{32,48},{48,32},{64,80},{80,64},{96,112},{112,96},{1... | collective-permute-start | bytes 1671176 | tf_op jit(solution)/shard_map/ppermute | solution.py:302
  95.9 11.3 %collective-permute-start.16 = (bf16[32,2176]{1,0:T(8,128)(2,1)S(1)}, bf16[32,2176]{1,0:T(8,128)(2,1)S(1)}, u32[]{:S(2)}, u32[]{:S(2)}) collective-permute-start(bf16[32,2176]{1,0:T(8,128)(2,1)S(1)} %get-tuple-element.55), channel_id=1, source_target_pairs={{0,32},{16,48},{32,64},{48,80},{64,96},{80,112},{96,0},{112,16},{1... | collective-permute-start | bytes 417800 | tf_op jit(solution)/shard_map/ppermute | solution.py:298
  97.2 9.9 %collective-permute-start.17 = (bf16[32,2176]{1,0:T(8,128)(2,1)S(1)}, bf16[32,2176]{1,0:T(8,128)(2,1)S(1)}, u32[]{:S(2)}, u32[]{:S(2)}) collective-permute-start(bf16[32,2176]{1,0:T(8,128)(2,1)S(1)} %get-tuple-element.56), channel_id=1, source_target_pairs={{0,64},{16,80},{32,96},{48,112},{64,0},{80,16},{96,32},{112,48},{1... | collective-permute-start | bytes 417800 | tf_op jit(solution)/shard_map/ppermute | solution.py:298
  99.8 7.3 %collective-permute-start.18 = (bf16[32,2176]{1,0:T(8,128)(2,1)S(1)}, bf16[32,2176]{1,0:T(8,128)(2,1)S(1)}, u32[]{:S(2)}, u32[]{:S(2)}) collective-permute-start(bf16[32,2176]{1,0:T(8,128)(2,1)S(1)} %get-tuple-element.57), channel_id=1, source_target_pairs={{0,96},{16,112},{32,0},{48,16},{64,32},{80,48},{96,64},{112,80},{1... | collective-permute-start | bytes 417800 | tf_op jit(solution)/shard_map/ppermute | solution.py:298
  107.1 9.7 %copy-start.2 = (bf16[128,8192]{1,0:T(8,128)(2,1)}, bf16[128,8192]{1,0:T(8,128)(2,1)S(1)}, u32[]{:S(2)}) copy-start(bf16[128,8192]{1,0:T(8,128)(2,1)S(1)} %fusion.refs_4_) | copy-start | bytes 6291460
  107.2 11.5 %copy-start.4 = (bf16[32,2176]{1,0:T(8,128)(2,1)}, bf16[32,2176]{1,0:T(8,128)(2,1)S(1)}, u32[]{:S(2)}) copy-start(bf16[32,2176]{1,0:T(8,128)(2,1)S(1)} %y_sum.1.refs_3_.own) | copy-start | bytes 417796
  107.2 4.0 %collective-permute-start.24 = (bf16[32,2176]{1,0:T(8,128)(2,1)S(1)}, bf16[32,2176]{1,0:T(8,128)(2,1)S(1)}, u32[]{:S(2)}, u32[]{:S(2)}) collective-permute-start(bf16[32,2176]{1,0:T(8,128)(2,1)S(1)} %y_sum.1.refs_3_.own), channel_id=1, source_target_pairs={{0,4},{1,5},{2,6},{3,7},{4,0},{5,1},{6,2},{7,3},{8,12},{9,13},{10,... | collective-permute-start | bytes 417800 | tf_op jit(solution)/shard_map/ppermute | solution.py:320
  111.3 5.5 %collective-permute-start.25 = (bf16[32,2176]{1,0:T(8,128)(2,1)S(1)}, bf16[32,2176]{1,0:T(8,128)(2,1)S(1)}, u32[]{:S(2)}, u32[]{:S(2)}) collective-permute-start(bf16[32,2176]{1,0:T(8,128)(2,1)S(1)} %swap_sum.4.own), channel_id=1, source_target_pairs={{0,8},{1,9},{2,10},{3,11},{4,12},{5,13},{6,14},{7,15},{8,0},{9,1},... | collective-permute-start | bytes 417800 | tf_op jit(solution)/shard_map/ppermute | solution.py:320
  116.8 5.0 %collective-permute-start.26 = (bf16[32,2176]{1,0:T(8,128)(2,1)S(1)}, bf16[32,2176]{1,0:T(8,128)(2,1)}, u32[]{:S(2)}, u32[]{:S(2)}) collective-permute-start(bf16[32,2176]{1,0:T(8,128)(2,1)S(1)} %swap_sum.5.own), channel_id=1, source_target_pairs={{0,1},{1,0},{2,3},{3,2},{4,5},{5,4},{6,7},{7,6},{8,9},{9,8},{10,11... | collective-permute-start | bytes 417800 | tf_op jit(solution)/shard_map/ppermute | solution.py:320
  118.7 11.0 %collective-permute-start.19 = (bf16[2,128,512]{2,1,0:T(8,128)(2,1)}, bf16[2,128,512]{2,1,0:T(8,128)(2,1)S(1)}, u32[]{:S(2)}, u32[]{:S(2)}) collective-permute-start(bf16[2,128,512]{2,1,0:T(8,128)(2,1)} %get-tuple-element.60), channel_id=1, source_target_pairs={{0,3},{1,0},{2,1},{3,2},{4,7},{5,4},{6,5},{7,6},{8,11},{9,8},{10,9... | collective-permute-start | bytes 786440 | tf_op jit(solution)/shard_map/ppermute | solution.py:290
  119.9 9.9 %collective-permute-start.20 = (bf16[2,128,512]{2,1,0:T(8,128)(2,1)}, bf16[2,128,512]{2,1,0:T(8,128)(2,1)S(1)}, u32[]{:S(2)}, u32[]{:S(2)}) collective-permute-start(bf16[2,128,512]{2,1,0:T(8,128)(2,1)} %get-tuple-element.61), channel_id=1, source_target_pairs={{0,2},{1,3},{2,0},{3,1},{4,6},{5,7},{6,4},{7,5},{8,10},{9,11},{10,... | collective-permute-start | bytes 786440 | tf_op jit(solution)/shard_map/ppermute | solution.py:290
  121.0 10.5 %collective-permute-start.21 = (bf16[2,128,512]{2,1,0:T(8,128)(2,1)}, bf16[2,128,512]{2,1,0:T(8,128)(2,1)S(1)}, u32[]{:S(2)}, u32[]{:S(2)}) collective-permute-start(bf16[2,128,512]{2,1,0:T(8,128)(2,1)} %get-tuple-element.62), channel_id=1, source_target_pairs={{0,1},{1,2},{2,3},{3,0},{4,5},{5,6},{6,7},{7,4},{8,9},{9,10},{10,1... | collective-permute-start | bytes 786440 | tf_op jit(solution)/shard_map/ppermute | solution.py:290
  122.8 13.7 %collective-permute-start.27 = (bf16[32,2176]{1,0:T(8,128)(2,1)S(1)}, bf16[32,2176]{1,0:T(8,128)(2,1)S(1)}, u32[]{:S(2)}, u32[]{:S(2)}) collective-permute-start(bf16[32,2176]{1,0:T(8,128)(2,1)S(1)} %swap_sum.6.own), channel_id=1, source_target_pairs={{0,2},{1,3},{2,0},{3,1},{4,6},{5,7},{6,4},{7,5},{8,10},{9,11},{10,... | collective-permute-start | bytes 417800 | tf_op jit(solution)/shard_map/ppermute | solution.py:320
  124.8 14.6 %all-to-all-start = ((f32[16,1,384]{2,1,0:T(1,128)}), f32[16,1,384]{2,1,0:T(1,128)S(1)}, u32[]{:S(2)}, u32[]{:S(2)}) async-start(f32[16,1,384]{2,1,0:T(1,128)} %get-tuple-element.66), calls=%async_computation | async-start | bytes 49152 | tf_op jit(solution)/shard_map/all_to_all | solution.py:521
  131.5 1.0 copy-start.18
  132.8 7.4 %collective-permute-start.22 = (bf16[128,512]{1,0:T(8,128)(2,1)S(1)}, bf16[128,512]{1,0:T(8,128)(2,1)S(1)}, u32[]{:S(2)}, u32[]{:S(2)}) collective-permute-start(bf16[128,512]{1,0:T(8,128)(2,1)S(1)} %get-tuple-element.64), channel_id=1, source_target_pairs={{0,12},{1,13},{2,14},{3,15},{4,0},{5,1},{6,2},{7,3},{8,4},{9,5},{1... | collective-permute-start | bytes 393224 | tf_op jit(solution)/shard_map/ppermute | solution.py:294
  134.7 5.5 %collective-permute-start.23 = (bf16[128,512]{1,0:T(8,128)(2,1)S(1)}, bf16[128,512]{1,0:T(8,128)(2,1)S(1)}, u32[]{:S(2)}, u32[]{:S(2)}) collective-permute-start(bf16[128,512]{1,0:T(8,128)(2,1)S(1)} %get-tuple-element.65), channel_id=1, source_target_pairs={{0,8},{1,9},{2,10},{3,11},{4,12},{5,13},{6,14},{7,15},{8,0},{9,1},... | collective-permute-start | bytes 393224 | tf_op jit(solution)/shard_map/ppermute | solution.py:294
  136.5 7.0 %collective-permute-start.28 = (bf16[32,2176]{1,0:T(8,128)(2,1)S(1)}, bf16[32,2176]{1,0:T(8,128)(2,1)S(1)}, u32[]{:S(2)}, u32[]{:S(2)}) collective-permute-start(bf16[32,2176]{1,0:T(8,128)(2,1)S(1)} %swap_sum.7.refs_0_), channel_id=1, source_target_pairs={{0,32},{16,48},{32,64},{48,80},{64,96},{80,112},{96,0},{112,16},{1... | collective-permute-start | bytes 417800 | tf_op jit(solution)/shard_map/ppermute | solution.py:298
  136.9 6.5 %collective-permute-start.29 = (bf16[32,2176]{1,0:T(8,128)(2,1)S(1)}, bf16[32,2176]{1,0:T(8,128)(2,1)S(1)}, u32[]{:S(2)}, u32[]{:S(2)}) collective-permute-start(bf16[32,2176]{1,0:T(8,128)(2,1)S(1)} %swap_sum.7.refs_0_), channel_id=1, source_target_pairs={{0,64},{16,80},{32,96},{48,112},{64,0},{80,16},{96,32},{112,48},{1... | collective-permute-start | bytes 417800 | tf_op jit(solution)/shard_map/ppermute | solution.py:298
  138.9 4.9 %collective-permute-start.30 = (bf16[32,2176]{1,0:T(8,128)(2,1)S(1)}, bf16[32,2176]{1,0:T(8,128)(2,1)S(1)}, u32[]{:S(2)}, u32[]{:S(2)}) collective-permute-start(bf16[32,2176]{1,0:T(8,128)(2,1)S(1)} %swap_sum.7.refs_0_), channel_id=1, source_target_pairs={{0,96},{16,112},{32,0},{48,16},{64,32},{80,48},{96,64},{112,80},{1... | collective-permute-start | bytes 417800 | tf_op jit(solution)/shard_map/ppermute | solution.py:298
  143.8 0.9 copy-start.11
  144.7 0.8 copy-start.12
  145.5 9.0 %collective-permute-start.31 = (bf16[32,8704]{1,0:T(8,128)(2,1)S(1)}, bf16[32,8704]{1,0:T(8,128)(2,1)S(1)}, u32[]{:S(2)}, u32[]{:S(2)}) collective-permute-start(bf16[32,8704]{1,0:T(8,128)(2,1)S(1)} %assemble.1.mine), channel_id=1, source_target_pairs={{0,16},{16,0},{32,48},{48,32},{64,80},{80,64},{96,112},{112,96},{1... | collective-permute-start | bytes 1671176 | tf_op jit(solution)/shard_map/ppermute | solution.py:302

commit v3 on v2

--- a/solution.py
+++ b/solution.py
@@ -96,6 +96,7 @@
         fill_bias(here, parts, docs_ref[...], bias)
 
     keys = [part[pl.ds(0, TOK), :] for part in parts]
+    rows = []
     for pair in range(PAIRS):
         q2 = pair_rows(q_ref, pair)
         peak = jnp.full((8, 2 * TOK), MASKED, F32)
@@ -109,17 +110,20 @@
         peak = jnp.max(peak, axis=0, keepdims=True)
         total = jnp.zeros((8, 2 * TOK), F32)
         for k in range(BLOCKS):
-            total = total + fold(jnp.exp2(scores[block(k), :] - peak), jnp.sum)
-        lse2 = peak + jnp.log2(jnp.sum(total, axis=0, keepdims=True))
+            p = jnp.exp2(scores[block(k), :] - peak)
+            total = total + fold(p, jnp.sum)
+            weights[block(k), pl.ds(pair * 2 * TOK, 2 * TOK)] = p.astype(BF)
+        total = jnp.sum(total, axis=0, keepdims=True)
+        lse2 = peak + jnp.log2(total)
+        share = 1.0 / total
         for n in range(2):
             lse = lse2[:, n * TOK : (n + 1) * TOK] * LN2
             lse_ref[0, 2 * pair + n : 2 * pair + n + 1, :] = lse
             lse_all[pl.ds(group * PER_GROUP + 2 * pair + n, 1), :] = lse
-        for k in range(BLOCKS):
-            weights[block(k), pl.ds(pair * 2 * TOK, 2 * TOK)] = jnp.exp2(
-                scores[block(k), :] - lse2
-            ).astype(BF)
-    rows = jnp.concatenate([pair_rows(g_ref, pair) for pair in range(PAIRS)], axis=0)
+            column = jnp.broadcast_to(share[:, n * TOK : (n + 1) * TOK], (TOK, TOK)).T
+            head = slice((2 * pair + n) * HEAD, (2 * pair + n + 1) * HEAD)
+            rows.append((g_ref[:, head].astype(F32) * column).astype(BF))
+    rows = jnp.concatenate(rows, axis=0)
     put_partials(dv_refs, lambda k: dot(weights[block(k), :], rows).astype(BF))
 
     @pl.when(group == GROUPS - 1)
@@ -144,8 +148,8 @@
 
 def grads_kernel(here_ref, docs_ref, q_ref, g_ref, lse_ref, *rest):
     key_own, key_pairs, value_own, value_pairs = rest[:3], rest[3:6], rest[6:9], rest[9:12]
-    out_ref, dq_ref, *dk_refs = rest[12:18]
-    bias, keys_t, values_t, weights32, weights, d_scores = rest[18:]
+    out_ref, dq_ref, *dk_refs = rest[-12:-6]
+    bias, keys_t, values_t, weights32, weights, d_scores = rest[-6:]
     parts = [window_part(key_own, key_pairs, REACH - k) for k in range(BLOCKS)]
     group = pl.program_id(0)
     here = here_ref[0]
@@ -205,15 +209,15 @@
     return pl.BlockSpec(memory_space=pl.ANY)
 
 
-def partial_outs():
+def partial_outs(first=0):
     counts = (3, 2, 2, 2)
     shapes = [jax.ShapeDtypeStruct((n, TOK, KV), BF) for n in counts]
-    return shapes, [pl.BlockSpec((n, TOK, HEAD), lambda g: (0, 0, g)) for n in counts]
-
-
-def window_specs(rows):
-    own = pl.BlockSpec((rows, HEAD), lambda g: (0, g))
-    pair = pl.BlockSpec((2, rows, HEAD), lambda g: (0, 0, g))
+    return shapes, [pl.BlockSpec((n, TOK, HEAD), lambda g: (0, 0, g + first)) for n in counts]
+
+
+def window_specs(rows, first=0):
+    own = pl.BlockSpec((rows, HEAD), lambda g: (0, g + first))
+    pair = pl.BlockSpec((2, rows, HEAD), lambda g: (0, 0, g + first))
     return [own] * 3 + [pair] * 3
 
 
@@ -251,21 +255,22 @@
     )(here, docs_own, owners, queries, grads, *keys, after)
 
 
-def run_grads(here, docs_own, queries, grads, lse, keys, values):
-    shapes, specs = partial_outs()
-    wide = pl.BlockSpec((TOK, PER_GROUP * HEAD), lambda g: (0, g))
+def run_grads(here, docs_own, queries, grads, lse, keys, values, first, count, begun=()):
+    shapes, specs = partial_outs(first)
+    wide = pl.BlockSpec((TOK, PER_GROUP * HEAD), lambda g: (0, g + first))
     return pl.pallas_call(
         grads_kernel,
-        grid=(GROUPS,),
+        grid=(count,),
         in_specs=[
             smem(),
             pl.BlockSpec((1, TOK), lambda g: (0, 0)),
             wide,
             wide,
-            pl.BlockSpec((1, PER_GROUP, TOK), lambda g: (g, 0, 0)),
+            pl.BlockSpec((1, PER_GROUP, TOK), lambda g: (g + first, 0, 0)),
         ]
-        + window_specs(PACK)
-        + window_specs(TOK),
+        + window_specs(PACK, first)
+        + window_specs(TOK, first)
+        + [anywhere()] * len(begun),
         out_specs=[wide, wide] + specs,
         out_shape=[jax.ShapeDtypeStruct((TOK, HQ * HEAD), BF)] * 2 + shapes,
         scratch_shapes=[
@@ -276,14 +281,15 @@
             pltpu.VMEM((KEYS, 2 * TOK), BF),
             pltpu.VMEM((KEYS, PER_GROUP * TOK), BF),
         ],
+        input_output_aliases={17 + n: n for n in range(len(begun))},
         compiler_params=pltpu.CompilerParams(
             vmem_limit_bytes=VMEM, dimension_semantics=("arbitrary",)
         ),
         cost_estimate=pl.CostEstimate(
-            flops=64 << 30, bytes_accessed=8 << 20, transcendentals=HQ * TOK * KEYS
+            flops=32 << 30, bytes_accessed=8 << 20, transcendentals=HQ * TOK * KEYS
         ),
-        name="grads",
-    )(here, docs_own, queries, grads, lse, *keys, *values)
+        name="grads_%d" % first,
+    )(here, docs_own, queries, grads, lse, *keys, *values, *begun)
 
 
 def along_z(x, step):
@@ -302,14 +308,19 @@
     return lax.ppermute(x, "dp", [(i, i ^ 1) for i in range(8)])
 
 
+def pick_kernel(z_ref, own, row_1, row_2, *outs):
+    for e, out in zip((1, 2, 3), outs):
+        wrapped = z_ref[0] + e > 3
+        out[0] = jnp.where(wrapped, row_1[...], own[...])
+        out[1] = jnp.where(wrapped, row_2[...], row_1[...])
+
+
 def for_peers(own, z):
     blocks = [own, along_x(own, 1), along_x(own, 2)]
-    own, row_1, row_2 = blocks
-    pairs = []
-    for e in (1, 2, 3):
-        wrapped = z + e > 3
-        pairs.append(jnp.stack([jnp.where(wrapped, row_1, own), jnp.where(wrapped, row_2, row_1)]))
-    return blocks, pairs
+    pairs = small_call(
+        pick_kernel, [smem()] + in_vmem(3), [((2, *own.shape), BF)] * 3, "pick", 1
+    )(z, *blocks)
+    return blocks, list(pairs)
 
 
 def to_peers(pairs):
@@ -355,8 +366,11 @@
     )
 
 
-def values_kernel(product, low_rank, up, _after, out):
-    out[...] = (product[...] + ADAPTER_SCALE * dot(low_rank[...], up[...])).astype(BF)
+def pack_kernel(keys, docs, out):
+    out[0:TOK, :] = keys[...]
+    rows = jnp.broadcast_to(docs[...].astype(F32), (DOC_ROWS, TOK)).astype(BF)
+    for group in range(GROUPS):
+        out[TOK:PACK, group * HEAD : (group + 1) * HEAD] = rows
 
 
 def gate_kernel(*refs):
@@ -404,7 +418,7 @@
 
 
 def adapter_kernel(core_ref, *refs):
-    up, low_rank, rows, grad_out, middle_out, keep_out, send_out = refs[3:]
+    up, low_rank, rows, _after, grad_out, middle_out, keep_out, send_out = refs[3:]
     grad = sum_terms(refs[:3])
     grad_out[...] = grad
     middle = (ADAPTER_SCALE * dot(grad, up[...], NT)).astype(BF)
@@ -493,18 +507,17 @@
     y, core = dp // 2, dp % 2
     rows = normed[0]
     low_rank = dot(rows, adapter_down).astype(BF)
-    doc_rows = jnp.broadcast_to(
-        jnp.tile(document_index.astype(BF), (1, KV // TOK)), (DOC_ROWS, KV)
-    )
-    z = ctx % 4
-    key_own, key_pairs = for_peers(jnp.concatenate([rotated_keys[0], doc_rows], axis=0), z)
-    (values,) = small_call(
-        values_kernel, in_vmem(3) + [anywhere()], [((TOK, KV), BF)], "values", 1
-    )(dot(rows, value_weight), low_rank, adapter_up, key_own[1])
+    values = (dot(rows, value_weight) + ADAPTER_SCALE * dot(low_rank, adapter_up)).astype(BF)
+    z = (ctx % 4).reshape(1)
+    (packed,) = small_call(pack_kernel, in_vmem(2), [((PACK, KV), BF)], "pack", 1)(
+        rotated_keys[0], document_index
+    )
+    key_own, key_pairs = for_peers(packed, z)
+    key_parts = key_own + to_peers(key_pairs)
+    (values,) = gate([values], key_own[1])
     value_own, value_pairs = for_peers(values, z)
-    key_parts = key_own + to_peers(key_pairs)
     value_parts = value_own + to_peers(value_pairs)
-    here, z, y, core = (n.reshape(1) for n in (ctx, z, y, core))
+    here, y, core = (n.reshape(1) for n in (ctx, y, core))
     lse, own_lse, *dv_parts = run_scores(
         here,
         document_index,
@@ -514,9 +527,10 @@
         key_parts,
         value_pairs[0],
     )
-    out, dq, *dk_parts = run_grads(
-        here, document_index, queries[0], attention_cotangent[0], lse, key_parts, value_parts
-    )
+    args = (here, document_index, queries[0], attention_cotangent[0], lse, key_parts, value_parts)
+    half_done = run_grads(*args, 0, GROUPS // 2)
+    out, dq, *dk_parts = run_grads(*args, GROUPS // 2, GROUPS - GROUPS // 2, half_done)
+
     peers = lax.axis_size("ctx")
     got_lse = lax.all_to_all(own_lse, "ctx", split_axis=0, concat_axis=0, tiled=True)
     (lse_rows,) = small_call(
@@ -528,18 +542,18 @@
         [pltpu.VMEM((peers * CAP, TOK), F32)],
     )(got_lse)
 
-    dv_terms = sum_home(dv_parts, z, dq)
+    dv_terms = sum_home(dv_parts, z, half_done[1])
 
     rank, model = adapter_up.shape[0], rows.shape[1]
     half, width = rank // 2, model + KV
     part = width // 4
     value_grad, middle, keep, send = small_call(
         adapter_kernel,
-        [smem()] + in_vmem(6),
+        [smem()] + in_vmem(6) + [anywhere()],
         [((TOK, KV), BF), ((TOK, rank), BF), ((half, width), BF), ((half, width), BF)],
         "adapter",
         3,
-    )(core, *dv_terms, adapter_up, low_rank, rows)
+    )(core, *dv_terms, adapter_up, low_rank, rows, dq)
     mine, *sends = small_call(
         quarters_kernel, [smem()] + in_vmem(2), [((half, part), BF)] * 4, "quarters", 1
     )(y, keep, other_core(send))
@@ -552,8 +566,8 @@
     dk_parts[1:] = gate(dk_parts[1:], mine)
     dk_terms = sum_home(dk_parts, z, here)
     (d_key,) = small_call(key_grad_kernel, in_vmem(3), [((TOK, KV), BF)], "key_grad", 1)(*dk_terms)
-    for axis_step in (4, 8, 1, 2):
-        mine = swap_sum(mine, axis_step)
+    for axis_step, after in ((4, ()), (8, ()), (1, (dk_terms[0],)), (2, ())):
+        mine = swap_sum(mine, axis_step, after)
     (whole,) = small_call(
         assemble_kernel,
         [smem()] + in_vmem(4) + [anywhere()] * 2,

time: 157 us -> 148 us (0.943)
  starting transfers between devices: 62.5 us -> 51.3 us
  other arithmetic: 3.68 us -> 0 us
  waiting for transfers between devices: 25.7 us -> 28 us
    ppermute x2, starting transfers between devices: 12.1 us -> 7.41 us  [other_core(): return lax.ppermute(x, 'dp', [(i, i ^ 1) for i in range(8)])]
    ppermute x12, waiting for transfers between devices: 10.3 us -> 13.8 us  [along_z(): lax.ppermute(x, 'ctx', [(i, i // 4 * 4 + (i + step) % 4) for i in range(1...]
    ppermute x4, waiting for transfers between devices: 6.7 us -> 3.25 us  [across(): return lax.ppermute(x, 'ctx', [(i, i ^ axis_step) for i in range(16)])]
    pallas_call x3 -> x6, Pallas kernels: 20.5 us -> 23.6 us  [the longest x2 20.1 us: run_grads(): pl.pallas_call(grads_kernel, grid=(count,), in_specs=[smem(), pl.BlockSpe...]
    ppermute x8, waiting for transfers between devices: 3.17 us -> 6.2 us  [along_x(): return lax.ppermute(x, 'ctx', [(i, (i + 4 * step) % 16) for i in range(16)])]
    ppermute x12, starting transfers between devices: 17.5 us -> 15 us  [along_z(): lax.ppermute(x, 'ctx', [(i, i // 4 * 4 + (i + step) % 4) for i in range(1...]
    another operation x9 -> x0, other arithmetic: 2.11 us -> none  [the longest x8 1.36 us: for_peers(): jnp.stack([jnp.where(wrapped, row_1, own), jnp.where(wrapped, row_2, row_...]
    ppermute x8, starting transfers between devices: 12.5 us -> 10.9 us  [along_x(): return lax.ppermute(x, 'ctx', [(i, (i + 4 * step) % 16) for i in range(16)])]
  transfers between devices with their start and end apart: 33 -> 33, of which waited for: 13 -> 13; matrix products, arithmetic and copies ran while one was open for 10% -> 10% of each run, Pallas kernels for 22% -> 24%
where the time goes in v3:
time: 148 us; the launch traced here: 147 us
  starting transfers between devices  51.3 us (35%)
  Pallas kernels  40.8 us (28%)
  waiting for transfers between devices  28 us (19%)
  matrix products  14.7 us (10%)
  local copies, waits for them, and re-layouts  11.2 us (8%)
    pallas_call x2, Pallas kernels, run_grads(): pl.pallas_call(grads_kernel, grid=(count,), in_specs=[smem(), pl.BlockSpe...  20.1 us
    ppermute x12, starting transfers between devices, along_z(): lax.ppermute(x, 'ctx', [(i, i // 4 * 4 + (i + step) % 4) for i in range(1...  15 us
    dot_general x5, matrix products, dot(): return lax.dot_general(a, b, dims, preferred_element_type=F32)  14.7 us
    ppermute x12, waiting for transfers between devices, along_z(): lax.ppermute(x, 'ctx', [(i, i // 4 * 4 + (i + step) % 4) for i in range(1...  13.8 us
    pallas_call x1, Pallas kernels, run_scores(): pl.pallas_call(scores_kernel, grid=(GROUPS,), in_specs=[smem(), line, lin...  12.4 us
    unnamed x52, local copies, waits for them, and re-layouts  11.2 us
    ppermute x8, starting transfers between devices, along_x(): return lax.ppermute(x, 'ctx', [(i, (i + 4 * step) % 16) for i in range(16)])  10.9 us
    ppermute x6, starting transfers between devices, along_y(): return lax.ppermute(x, 'dp', [(i, (i + 2 * step) % 8) for i in range(8)])  8.03 us
  transfers between devices with their start and end apart: 33, of which 13 were waited for; matrix products, arithmetic and copies ran while one was open for 10% of the time, Pallas kernels for 24%

profile of v3, /device:TPU:1, one launch (start us, length us, event | category | flops | bytes accessed | tf_op | source)
XLA Modules:
  0.0 147.1 jit_solution(1337528193813553772)
XLA Ops:
  0.7 1.0 copy-done.11
  1.7 0.7 copy-done.14
  2.4 2.1 %collective-permute-start = (bf16[144,512]{1,0:T(8,128)(2,1)S(1)}, bf16[144,512]{1,0:T(8,128)(2,1)S(1)}, u32[]{:S(2)}, u32[]{:S(2)}) collective-permute-start(bf16[144,512]{1,0:T(8,128)(2,1)S(1)} %pack.1.own.rest_0_), channel_id=1, source_target_pairs={{0,4},{1,5},{2,6},{3,7},{4,8},{5,9},{6,10},{7,11},{8,12},{9,13},{1... | collective-permute-start | bytes 442376 | tf_op jit(solution)/shard_map/ppermute | solution.py:300
  4.5 2.5 %collective-permute-start.1 = (bf16[144,512]{1,0:T(8,128)(2,1)S(1)}, bf16[144,512]{1,0:T(8,128)(2,1)}, u32[]{:S(2)}, u32[]{:S(2)}) collective-permute-start(bf16[144,512]{1,0:T(8,128)(2,1)S(1)} %pack.1.own.rest_0_), channel_id=1, source_target_pairs={{0,8},{1,9},{2,10},{3,11},{4,12},{5,13},{6,14},{7,15},{8,0},{9,1},... | collective-permute-start | bytes 442376 | tf_op jit(solution)/shard_map/ppermute | solution.py:300
  7.0 5.3 %fusion.4 = f32[128,512]{1,0:T(8,128)} fusion(bf16[8192,512]{1,0:T(8,128)(2,1)} %param.12, bf16[1,128,8192]{2,1,0:T(8,128)(2,1)S(1)} %copy-done.1), kind=kOutput, calls=%fused_computation.7 | convolution fusion | flops 1073741824 | bytes 10747904 | tf_op jit(solution)/shard_map/dot_general | solution.py:38
  12.3 0.7 convolution_convert_fusion.refs_4_
  13.5 1.9 %pick.2 = (bf16[2,144,512]{2,1,0:T(8,128)(2,1)}, bf16[2,144,512]{2,1,0:T(8,128)(2,1)}, bf16[2,144,512]{2,1,0:T(8,128)(2,1)}) custom-call(s32[1]{0:T(128)} %bitcast.5.z_ref, bf16[144,512]{1,0:T(8,128)(2,1)S(1)} %pack.1.own.rest_0_, bf16[144,512]{1,0:T(8,128)(2,1)S(1)} %collective-permute-done.row_1.refs_1_.rest_1_, ...), custom_call_target="tpu_custom_call" | custom-call | flops 1073741824 | bytes 2097152 | tf_op jit(solution)/shard_map/pick/pallas_call | solution.py:320
  15.3 1.6 %collective-permute-start.2 = (bf16[2,144,512]{2,1,0:T(8,128)(2,1)}, bf16[2,144,512]{2,1,0:T(8,128)(2,1)}, u32[]{:S(2)}, u32[]{:S(2)}) collective-permute-start(bf16[2,144,512]{2,1,0:T(8,128)(2,1)} %get-tuple-element.50), channel_id=1, source_target_pairs={{0,1},{1,2},{2,3},{3,0},{4,5},{5,6},{6,7},{7,4},{8,9},{9,10},{10,1... | collective-permute-start | bytes 884744 | tf_op jit(solution)/shard_map/ppermute | solution.py:296
  17.0 3.3 %collective-permute-start.3 = (bf16[2,144,512]{2,1,0:T(8,128)(2,1)}, bf16[2,144,512]{2,1,0:T(8,128)(2,1)}, u32[]{:S(2)}, u32[]{:S(2)}) collective-permute-start(bf16[2,144,512]{2,1,0:T(8,128)(2,1)} %get-tuple-element.51), channel_id=1, source_target_pairs={{0,2},{1,3},{2,0},{3,1},{4,6},{5,7},{6,4},{7,5},{8,10},{9,11},{10,... | collective-permute-start | bytes 884744 | tf_op jit(solution)/shard_map/ppermute | solution.py:296
  20.3 0.7 collective-permute-start.4
  21.0 1.8 %fusion.2.refs_0_ = bf16[128,512]{1,0:T(8,128)(2,1)} fusion(f32[128,512]{1,0:T(8,128)} %fusion.4, bf16[128,64]{1,0:T(8,128)(2,1)S(1)} %convolution_convert_fusion.refs_4_, bf16[64,512]{1,0:T(8,128)(2,1)S(1)} %copy-done.6), kind=kOutput, calls=%fused_computation.4 | convolution fusion | flops 8585216 | bytes 475136 | tf_op jit(solution)/shard_map/dot_general | solution.py:38
  22.8 2.0 %collective-permute-start.6 = (bf16[128,512]{1,0:T(8,128)(2,1)}, bf16[128,512]{1,0:T(8,128)(2,1)S(1)}, u32[]{:S(2)}, u32[]{:S(2)}) collective-permute-start(bf16[128,512]{1,0:T(8,128)(2,1)} %gate.2.own.rest_6_), channel_id=1, source_target_pairs={{0,8},{1,9},{2,10},{3,11},{4,12},{5,13},{6,14},{7,15},{8,0},{9,1},... | collective-permute-start | bytes 393224 | tf_op jit(solution)/shard_map/ppermute | solution.py:300
  24.8 4.7 %collective-permute-done.5.row_1.rest_7_ = bf16[128,512]{1,0:T(8,128)(2,1)S(1)} collective-permute-done((bf16[128,512]{1,0:T(8,128)(2,1)}, bf16[128,512]{1,0:T(8,128)(2,1)S(1)}, u32[]{:S(2)}, u32[]{:S(2)}) %collective-permute-start.5) | collective-permute-done | bytes 131104 | tf_op jit(solution)/shard_map/ppermute | solution.py:300
  29.4 1.0 copy-done.3
  30.5 1.0 collective-permute-start.7
  31.5 0.8 collective-permute-start.8
  32.3 1.7 %collective-permute-start.9 = (bf16[2,128,512]{2,1,0:T(8,128)(2,1)S(1)}, bf16[2,128,512]{2,1,0:T(8,128)(2,1)S(1)}, u32[]{:S(2)}, u32[]{:S(2)}) collective-permute-start(bf16[2,128,512]{2,1,0:T(8,128)(2,1)S(1)} %get-tuple-element.56), channel_id=1, source_target_pairs={{0,3},{1,0},{2,1},{3,2},{4,7},{5,4},{6,5},{7,6},{8,11},{9,8},{10,9... | collective-permute-start | bytes 786440 | tf_op jit(solution)/shard_map/ppermute | solution.py:296
  34.0 12.4 %scores.1 = (f32[4,8,128]{2,1,0:T(8,128)}, f32[16,1,384]{2,1,0:T(1,128)}, bf16[3,128,512]{2,1,0:T(8,128)(2,1)}, bf16[2,128,512]{2,1,0:T(8,128)(2,1)}, bf16[2,128...) custom-call(s32[1]{0:T(128)} %bitcast.here_ref.refs_3_, s32[1,128]{1,0:T(1,128)} %docs_ref.5, s32[1,128]{1,0:T(1,128)} %bitcast.41, ...), custom_call_target="tpu_custom_call" | custom-call | flops 34359738368 | bytes 6291456 | tf_op jit(solution)/shard_map/scores/pallas_call | solution.py:228
  46.4 2.2 %collective-permute-start.10 = (bf16[2,128,512]{2,1,0:T(8,128)(2,1)}, bf16[2,128,512]{2,1,0:T(8,128)(2,1)S(1)}, u32[]{:S(2)}, u32[]{:S(2)}) collective-permute-start(bf16[2,128,512]{2,1,0:T(8,128)(2,1)} %get-tuple-element.70), channel_id=1, source_target_pairs={{0,3},{1,0},{2,1},{3,2},{4,7},{5,4},{6,5},{7,6},{8,11},{9,8},{10,9... | collective-permute-start | bytes 786440 | tf_op jit(solution)/shard_map/ppermute | solution.py:296
  50.1 10.1 %grads_0.1 = (bf16[128,4096]{1,0:T(8,128)(2,1)}, bf16[128,4096]{1,0:T(8,128)(2,1)}, bf16[3,128,512]{2,1,0:T(8,128)(2,1)}, bf16[2,128,512]{2,1,0:T(8,128)(2,1)}, ...) custom-call(s32[1]{0:T(128)} %bitcast.here_ref.refs_3_, s32[1,128]{1,0:T(1,128)} %docs_ref.5, ...), custom_call_target="tpu_custom_call" | custom-call | flops 34359738368 | bytes 8388608 | tf_op jit(solution)/shard_map/grads_0/pallas_call | solution.py:261
  60.2 2.9 %collective-permute-done.12.refs_2_ = bf16[2,128,512]{2,1,0:T(8,128)(2,1)S(1)} collective-permute-done((bf16[2,128,512]{2,1,0:T(8,128)(2,1)}, bf16[2,128,512]{2,1,0:T(8,128)(2,1)S(1)}, u32[]{:S(2)}, u32[]{:S(2)}) %collective-permute-start.12) | collective-permute-done | bytes 262176 | tf_op jit(solution)/shard_map/ppermute | solution.py:296
  63.1 1.2 copy-done.15
  64.7 1.1 collective-permute-start.14
  65.8 10.0 %grads_2.1 = (bf16[128,4096]{1,0:T(8,128)(2,1)}, bf16[128,4096]{1,0:T(8,128)(2,1)}, bf16[3,128,512]{2,1,0:T(8,128)(2,1)}, bf16[2,128,512]{2,1,0:T(8,128)(2,1)}, ...) custom-call(s32[1]{0:T(128)} %bitcast.here_ref.refs_3_, ...), custom_call_target="tpu_custom_call", output_to_operand_aliasing={{0}: (17, {}), {1}: (18, {}), {2}: (19, {}), {3}: (20, {}),... | custom-call | flops 34359738368 | bytes 8388608 | tf_op jit(solution)/shard_map/grads_2/pallas_call | solution.py:261
  75.9 1.2 copy-done.16
  77.1 1.5 %adapter.1 = (bf16[128,512]{1,0:T(8,128)(2,1)S(1)}, bf16[128,64]{1,0:T(8,128)(2,1)S(1)}, bf16[32,8704]{1,0:T(8,128)(2,1)S(1)}, bf16[32,8704]{1,0:T(8,128)(2,1)}) custom-call(s32[1]{0:T(128)} %bitcast.10.core_ref, f32[128,512]{1,0:T(8,128)S(1)} %get-tuple-element.73.refs_0_, bf16[128,512]{1,0:T(8,128)(2,1)S(1)} %collective-permute-done.13.refs_1_, ...), custom_call_target="tpu_custom_call" | custom-call | flops 3221225472 | bytes 6291456 | tf_op jit(solution)/shard_map/adapter/pallas_call | solution.py:550
  78.6 0.8 copy-done.20
  79.4 2.9 %collective-permute-start.15 = (bf16[32,8704]{1,0:T(8,128)(2,1)}, bf16[32,8704]{1,0:T(8,128)(2,1)S(1)}, u32[]{:S(2)}, u32[]{:S(2)}) collective-permute-start(bf16[32,8704]{1,0:T(8,128)(2,1)} %get-tuple-element.77), channel_id=1, source_target_pairs={{0,16},{16,0},{32,48},{48,32},{64,80},{80,64},{96,112},{112,96},{1... | collective-permute-start | bytes 1671176 | tf_op jit(solution)/shard_map/ppermute | solution.py:308
  82.4 0.7 fusion.6
  83.1 1.1 collective-permute-done.15.got
  84.2 0.8 copy-done.7
  85.0 1.1 copy-done.8
  86.2 1.4 collective-permute-start.16
  87.5 2.6 %collective-permute-start.17 = (bf16[32,2176]{1,0:T(8,128)(2,1)S(1)}, bf16[32,2176]{1,0:T(8,128)(2,1)S(1)}, u32[]{:S(2)}, u32[]{:S(2)}) collective-permute-start(bf16[32,2176]{1,0:T(8,128)(2,1)S(1)} %get-tuple-element.80), channel_id=1, source_target_pairs={{0,64},{16,80},{32,96},{48,112},{64,0},{80,16},{96,32},{112,48},{1... | collective-permute-start | bytes 417800 | tf_op jit(solution)/shard_map/ppermute | solution.py:304
  90.2 1.1 collective-permute-start.18
  91.2 6.2 %fusion.refs_4_ = bf16[128,8192]{1,0:T(8,128)(2,1)S(1)} fusion(f32[128,8192]{1,0:T(8,128)S(1)} %fusion.6, bf16[128,512]{1,0:T(8,128)(2,1)S(1)} %get-tuple-element.82, bf16[8192,512]{1,0:T(8,128)(2,1)} %param.12), kind=kOutput, calls=%fused_computation.1 | convolution fusion | flops 1075838976 | bytes 14811136 | tf_op jit(solution)/shard_map/dot_general | solution.py:38
  97.6 0.7 collective-permute-start.24
  98.3 3.2 %collective-permute-done.24.got = bf16[32,2176]{1,0:T(8,128)(2,1)S(1)} collective-permute-done((bf16[32,2176]{1,0:T(8,128)(2,1)S(1)}, bf16[32,2176]{1,0:T(8,128)(2,1)S(1)}, u32[]{:S(2)}, u32[]{:S(2)}) %collective-permute-start.24) | collective-permute-done | bytes 139296 | tf_op jit(solution)/shard_map/ppermute | solution.py:331
  101.6 3.3 %collective-permute-start.25 = (bf16[32,2176]{1,0:T(8,128)(2,1)S(1)}, bf16[32,2176]{1,0:T(8,128)(2,1)}, u32[]{:S(2)}, u32[]{:S(2)}) collective-permute-start(bf16[32,2176]{1,0:T(8,128)(2,1)S(1)} %swap_sum.4.own), channel_id=1, source_target_pairs={{0,8},{1,9},{2,10},{3,11},{4,12},{5,13},{6,14},{7,15},{8,0},{9,1},... | collective-permute-start | bytes 417800 | tf_op jit(solution)/shard_map/ppermute | solution.py:331
  104.9 1.6 %collective-permute-start.19 = (bf16[2,128,512]{2,1,0:T(8,128)(2,1)}, bf16[2,128,512]{2,1,0:T(8,128)(2,1)S(1)}, u32[]{:S(2)}, u32[]{:S(2)}) collective-permute-start(bf16[2,128,512]{2,1,0:T(8,128)(2,1)} %get-tuple-element.84), channel_id=1, source_target_pairs={{0,3},{1,0},{2,1},{3,2},{4,7},{5,4},{6,5},{7,6},{8,11},{9,8},{10,9... | collective-permute-start | bytes 786440 | tf_op jit(solution)/shard_map/ppermute | solution.py:296
  106.6 0.9 collective-permute-start.20
  107.9 0.9 swap_sum.5.own
  108.8 1.4 collective-permute-start.26
  110.2 0.6 collective-permute-done.19.refs_0_
  110.9 2.7 %collective-permute-done.20.refs_1_ = bf16[2,128,512]{2,1,0:T(8,128)(2,1)S(1)} collective-permute-done((bf16[2,128,512]{2,1,0:T(8,128)(2,1)}, bf16[2,128,512]{2,1,0:T(8,128)(2,1)S(1)}, u32[]{:S(2)}, u32[]{:S(2)}) %collective-permute-start.20) | collective-permute-done | bytes 262176 | tf_op jit(solution)/shard_map/ppermute | solution.py:296
  113.6 7.5 %collective-permute-done.21.refs_2_ = bf16[2,128,512]{2,1,0:T(8,128)(2,1)S(1)} collective-permute-done((bf16[2,128,512]{2,1,0:T(8,128)(2,1)}, bf16[2,128,512]{2,1,0:T(8,128)(2,1)S(1)}, u32[]{:S(2)}, u32[]{:S(2)}) %collective-permute-start.21) | collective-permute-done | bytes 262176 | tf_op jit(solution)/shard_map/ppermute | solution.py:296
  121.1 1.0 copy-done.22
  122.5 0.9 collective-permute-start.27
  123.4 3.6 %all-to-all-start = ((f32[16,1,384]{2,1,0:T(1,128)}), f32[16,1,384]{2,1,0:T(1,128)S(1)}, u32[]{:S(2)}, u32[]{:S(2)}) async-start(f32[16,1,384]{2,1,0:T(1,128)} %get-tuple-element.90), calls=%async_computation | async-start | bytes 49152 | tf_op jit(solution)/shard_map/all_to_all | solution.py:535
  127.0 2.6 %collective-permute-start.22 = (bf16[128,512]{1,0:T(8,128)(2,1)S(1)}, bf16[128,512]{1,0:T(8,128)(2,1)S(1)}, u32[]{:S(2)}, u32[]{:S(2)}) collective-permute-start(bf16[128,512]{1,0:T(8,128)(2,1)S(1)} %get-tuple-element.88), channel_id=1, source_target_pairs={{0,12},{1,13},{2,14},{3,15},{4,0},{5,1},{6,2},{7,3},{8,4},{9,5},{1... | collective-permute-start | bytes 393224 | tf_op jit(solution)/shard_map/ppermute | solution.py:300
  129.6 0.6 collective-permute-start.23
  130.2 0.5 collective-permute-start.28
  130.7 2.0 %collective-permute-start.29 = (bf16[32,2176]{1,0:T(8,128)(2,1)S(1)}, bf16[32,2176]{1,0:T(8,128)(2,1)S(1)}, u32[]{:S(2)}, u32[]{:S(2)}) collective-permute-start(bf16[32,2176]{1,0:T(8,128)(2,1)S(1)} %swap_sum.7.refs_0_), channel_id=1, source_target_pairs={{0,64},{16,80},{32,96},{48,112},{64,0},{80,16},{96,32},{112,48},{1... | collective-permute-start | bytes 417800 | tf_op jit(solution)/shard_map/ppermute | solution.py:304
  132.7 0.5 collective-permute-start.30
  133.5 0.8 slots.1.refs_5_
  134.3 1.1 collective-permute-done.23.refs_2_
  135.3 0.7 key_grad.1.refs_4_
  136.1 0.8 collective-permute-done.28.refs_1_
  136.9 0.9 collective-permute-done.30.refs_3_
  137.8 0.9 copy-done.17
  138.7 0.8 copy-done.18
  139.5 4.5 %collective-permute-start.31 = (bf16[32,8704]{1,0:T(8,128)(2,1)S(1)}, bf16[32,8704]{1,0:T(8,128)(2,1)S(1)}, u32[]{:S(2)}, u32[]{:S(2)}) collective-permute-start(bf16[32,8704]{1,0:T(8,128)(2,1)S(1)} %assemble.1.mine), channel_id=1, source_target_pairs={{0,16},{16,0},{32,48},{48,32},{64,80},{80,64},{96,112},{112,96},{1... | collective-permute-start | bytes 1671176 | tf_op jit(solution)/shard_map/ppermute | solution.py:308
  144.0 1.6 %collective-permute-done.31.other = bf16[32,8704]{1,0:T(8,128)(2,1)S(1)} collective-permute-done((bf16[32,8704]{1,0:T(8,128)(2,1)S(1)}, bf16[32,8704]{1,0:T(8,128)(2,1)S(1)}, u32[]{:S(2)}, u32[]{:S(2)}) %collective-permute-start.31) | collective-permute-done | bytes 557088 | tf_op jit(solution)/shard_map/ppermute | solution.py:308
  145.6 1.5 %totals.1 = (f32[64,8192]{1,0:T(8,128)}, f32[64,512]{1,0:T(8,128)}) custom-call(s32[1]{0:T(128)} %bitcast.10.core_ref, bf16[32,8704]{1,0:T(8,128)(2,1)S(1)} %assemble.1.mine, bf16[32,8704]{1,0:T(8,128)(2,1)S(1)} %collective-permute-done.31.other), custom_call_target="tpu_custom_call" | custom-call | flops 2147483648 | bytes 4194304 | tf_op jit(solution)/shard_map/totals/pallas_call | solution.py:578
  (80 shorter events, 3.9 us)
Async XLA Ops:
  0.6 11.7 %copy-start = (bf16[8192,64]{0,1:T(8,128)(2,1)S(1)}, bf16[8192,64]{0,1:T(8,128)(2,1)}, u32[]{:S(2)}) copy-start(bf16[8192,64]{0,1:T(8,128)(2,1)} %param.13) | copy-start | bytes 3145732
  0.6 6.3 %copy-start.1 = (bf16[1,128,8192]{2,1,0:T(8,128)(2,1)S(1)}, bf16[1,128,8192]{2,1,0:T(8,128)(2,1)}, u32[]{:S(2)}) copy-start(bf16[1,128,8192]{2,1,0:T(8,128)(2,1)} %param.9) | copy-start | bytes 6291460
  0.7 1.1 copy-start.11
  1.7 0.7 copy-start.14
  2.4 11.1 %copy-start.10 = (bf16[144,512]{1,0:T(8,128)(2,1)}, bf16[144,512]{1,0:T(8,128)(2,1)S(1)}, u32[]{:S(2)}) copy-start(bf16[144,512]{1,0:T(8,128)(2,1)S(1)} %pack.1.own.rest_0_) | copy-start | bytes 442372
  2.4 10.6 %collective-permute-start = (bf16[144,512]{1,0:T(8,128)(2,1)S(1)}, bf16[144,512]{1,0:T(8,128)(2,1)S(1)}, u32[]{:S(2)}, u32[]{:S(2)}) collective-permute-start(bf16[144,512]{1,0:T(8,128)(2,1)S(1)} %pack.1.own.rest_0_), channel_id=1, source_target_pairs={{0,4},{1,5},{2,6},{3,7},{4,8},{5,9},{6,10},{7,11},{8,12},{9,13},{1... | collective-permute-start | bytes 442376 | tf_op jit(solution)/shard_map/ppermute | solution.py:300
  4.5 9.0 %collective-permute-start.1 = (bf16[144,512]{1,0:T(8,128)(2,1)S(1)}, bf16[144,512]{1,0:T(8,128)(2,1)}, u32[]{:S(2)}, u32[]{:S(2)}) collective-permute-start(bf16[144,512]{1,0:T(8,128)(2,1)S(1)} %pack.1.own.rest_0_), channel_id=1, source_target_pairs={{0,8},{1,9},{2,10},{3,11},{4,12},{5,13},{6,14},{7,15},{8,0},{9,1},... | collective-permute-start | bytes 442376 | tf_op jit(solution)/shard_map/ppermute | solution.py:300
  12.3 8.7 %copy-start.6 = (bf16[64,512]{1,0:T(8,128)(2,1)S(1)}, bf16[64,512]{1,0:T(8,128)(2,1)}, u32[]{:S(2)}) copy-start(bf16[64,512]{1,0:T(8,128)(2,1)} %refs_3_.1) | copy-start | bytes 196612
  13.0 9.8 %copy-start.4 = (bf16[144,512]{1,0:T(8,128)(2,1)}, bf16[144,512]{1,0:T(8,128)(2,1)S(1)}, u32[]{:S(2)}) copy-start(bf16[144,512]{1,0:T(8,128)(2,1)S(1)} %collective-permute-done.row_1.refs_1_.rest_1_) | copy-start | bytes 442372
  15.3 16.9 %collective-permute-start.2 = (bf16[2,144,512]{2,1,0:T(8,128)(2,1)}, bf16[2,144,512]{2,1,0:T(8,128)(2,1)}, u32[]{:S(2)}, u32[]{:S(2)}) collective-permute-start(bf16[2,144,512]{2,1,0:T(8,128)(2,1)} %get-tuple-element.50), channel_id=1, source_target_pairs={{0,1},{1,2},{2,3},{3,0},{4,5},{5,6},{6,7},{7,4},{8,9},{9,10},{10,1... | collective-permute-start | bytes 884744 | tf_op jit(solution)/shard_map/ppermute | solution.py:296
  17.0 17.0 %collective-permute-start.3 = (bf16[2,144,512]{2,1,0:T(8,128)(2,1)}, bf16[2,144,512]{2,1,0:T(8,128)(2,1)}, u32[]{:S(2)}, u32[]{:S(2)}) collective-permute-start(bf16[2,144,512]{2,1,0:T(8,128)(2,1)} %get-tuple-element.51), channel_id=1, source_target_pairs={{0,2},{1,3},{2,0},{3,1},{4,6},{5,7},{6,4},{7,5},{8,10},{9,11},{10,... | collective-permute-start | bytes 884744 | tf_op jit(solution)/shard_map/ppermute | solution.py:296
  20.3 13.7 %collective-permute-start.4 = (bf16[2,144,512]{2,1,0:T(8,128)(2,1)}, bf16[2,144,512]{2,1,0:T(8,128)(2,1)}, u32[]{:S(2)}, u32[]{:S(2)}) collective-permute-start(bf16[2,144,512]{2,1,0:T(8,128)(2,1)} %get-tuple-element.52), channel_id=1, source_target_pairs={{0,3},{1,0},{2,1},{3,2},{4,7},{5,4},{6,5},{7,6},{8,11},{9,8},{10,9... | collective-permute-start | bytes 884744 | tf_op jit(solution)/shard_map/ppermute | solution.py:296
  22.8 6.6 %collective-permute-start.5 = (bf16[128,512]{1,0:T(8,128)(2,1)}, bf16[128,512]{1,0:T(8,128)(2,1)S(1)}, u32[]{:S(2)}, u32[]{:S(2)}) collective-permute-start(bf16[128,512]{1,0:T(8,128)(2,1)} %gate.2.own.rest_6_), channel_id=1, source_target_pairs={{0,4},{1,5},{2,6},{3,7},{4,8},{5,9},{6,10},{7,11},{8,12},{9,13},{1... | collective-permute-start | bytes 393224 | tf_op jit(solution)/shard_map/ppermute | solution.py:300
  22.8 6.6 %collective-permute-start.6 = (bf16[128,512]{1,0:T(8,128)(2,1)}, bf16[128,512]{1,0:T(8,128)(2,1)S(1)}, u32[]{:S(2)}, u32[]{:S(2)}) collective-permute-start(bf16[128,512]{1,0:T(8,128)(2,1)} %gate.2.own.rest_6_), channel_id=1, source_target_pairs={{0,8},{1,9},{2,10},{3,11},{4,12},{5,13},{6,14},{7,15},{8,0},{9,1},... | collective-permute-start | bytes 393224 | tf_op jit(solution)/shard_map/ppermute | solution.py:300
  29.4 17.0 %copy-start.12 = (bf16[128,512]{1,0:T(8,128)(2,1)}, bf16[128,512]{1,0:T(8,128)(2,1)S(1)}, u32[]{:S(2)}) copy-start(bf16[128,512]{1,0:T(8,128)(2,1)S(1)} %collective-permute-done.5.row_1.rest_7_) | copy-start | bytes 393220
  29.4 1.0 copy-start.3
  30.4 16.0 %copy-start.13 = (bf16[128,512]{1,0:T(8,128)(2,1)}, bf16[128,512]{1,0:T(8,128)(2,1)S(1)}, u32[]{:S(2)}) copy-start(bf16[128,512]{1,0:T(8,128)(2,1)S(1)} %collective-permute-done.6.row_2.rest_8_) | copy-start | bytes 393220
  30.5 3.6 %copy-start.9 = (bf16[2,128,512]{2,1,0:T(8,128)(2,1)}, bf16[2,128,512]{2,1,0:T(8,128)(2,1)S(1)}, u32[]{:S(2)}) copy-start(bf16[2,128,512]{2,1,0:T(8,128)(2,1)S(1)} %get-tuple-element.53.rest_6_) | copy-start | bytes 786436
  30.5 18.5 %collective-permute-start.7 = (bf16[2,128,512]{2,1,0:T(8,128)(2,1)S(1)}, bf16[2,128,512]{2,1,0:T(8,128)(2,1)S(1)}, u32[]{:S(2)}, u32[]{:S(2)}) collective-permute-start(bf16[2,128,512]{2,1,0:T(8,128)(2,1)S(1)} %get-tuple-element.53.rest_6_), channel_id=1, source_target_pairs={{0,1},{1,2},{2,3},{3,0},{4,5},{5,6},{6,7},{7,4},{8,9},{9,10},{10,1... | collective-permute-start | bytes 786440 | tf_op jit(solution)/shard_map/ppermute | solution.py:296
  31.5 17.8 %collective-permute-start.8 = (bf16[2,128,512]{2,1,0:T(8,128)(2,1)S(1)}, bf16[2,128,512]{2,1,0:T(8,128)(2,1)S(1)}, u32[]{:S(2)}, u32[]{:S(2)}) collective-permute-start(bf16[2,128,512]{2,1,0:T(8,128)(2,1)S(1)} %get-tuple-element.55), channel_id=1, source_target_pairs={{0,2},{1,3},{2,0},{3,1},{4,6},{5,7},{6,4},{7,5},{8,10},{9,11},{10,... | collective-permute-start | bytes 786440 | tf_op jit(solution)/shard_map/ppermute | solution.py:296
  32.3 17.0 %collective-permute-start.9 = (bf16[2,128,512]{2,1,0:T(8,128)(2,1)S(1)}, bf16[2,128,512]{2,1,0:T(8,128)(2,1)S(1)}, u32[]{:S(2)}, u32[]{:S(2)}) collective-permute-start(bf16[2,128,512]{2,1,0:T(8,128)(2,1)S(1)} %get-tuple-element.56), channel_id=1, source_target_pairs={{0,3},{1,0},{2,1},{3,2},{4,7},{5,4},{6,5},{7,6},{8,11},{9,8},{10,9... | collective-permute-start | bytes 786440 | tf_op jit(solution)/shard_map/ppermute | solution.py:296
  46.4 13.8 %collective-permute-start.10 = (bf16[2,128,512]{2,1,0:T(8,128)(2,1)}, bf16[2,128,512]{2,1,0:T(8,128)(2,1)S(1)}, u32[]{:S(2)}, u32[]{:S(2)}) collective-permute-start(bf16[2,128,512]{2,1,0:T(8,128)(2,1)} %get-tuple-element.70), channel_id=1, source_target_pairs={{0,3},{1,0},{2,1},{3,2},{4,7},{5,4},{6,5},{7,6},{8,11},{9,8},{10,9... | collective-permute-start | bytes 786440 | tf_op jit(solution)/shard_map/ppermute | solution.py:296
  48.6 11.6 %collective-permute-start.11 = (bf16[2,128,512]{2,1,0:T(8,128)(2,1)}, bf16[2,128,512]{2,1,0:T(8,128)(2,1)S(1)}, u32[]{:S(2)}, u32[]{:S(2)}) collective-permute-start(bf16[2,128,512]{2,1,0:T(8,128)(2,1)} %get-tuple-element.71), channel_id=1, source_target_pairs={{0,2},{1,3},{2,0},{3,1},{4,6},{5,7},{6,4},{7,5},{8,10},{9,11},{10,... | collective-permute-start | bytes 786440 | tf_op jit(solution)/shard_map/ppermute | solution.py:296
  49.0 0.7 copy-start.23
  49.0 14.1 %collective-permute-start.12 = (bf16[2,128,512]{2,1,0:T(8,128)(2,1)}, bf16[2,128,512]{2,1,0:T(8,128)(2,1)S(1)}, u32[]{:S(2)}, u32[]{:S(2)}) collective-permute-start(bf16[2,128,512]{2,1,0:T(8,128)(2,1)} %get-tuple-element.72), channel_id=1, source_target_pairs={{0,1},{1,2},{2,3},{3,0},{4,5},{5,6},{6,7},{7,4},{8,9},{9,10},{10,1... | collective-permute-start | bytes 786440 | tf_op jit(solution)/shard_map/ppermute | solution.py:296
  49.3 0.7 copy-start.24
  49.3 0.8 copy-start.25
  50.1 13.0 %copy-start.19 = (bf16[3,128,512]{2,1,0:T(8,128)(2,1)S(1)}, bf16[3,128,512]{2,1,0:T(8,128)(2,1)}, u32[]{:S(2)}) copy-start(bf16[3,128,512]{2,1,0:T(8,128)(2,1)} %get-tuple-element.69.own) | copy-start | bytes 1179652
  63.1 1.2 copy-start.15
  64.6 11.2 %collective-permute-start.13 = (bf16[128,512]{1,0:T(8,128)(2,1)S(1)}, bf16[128,512]{1,0:T(8,128)(2,1)S(1)}, u32[]{:S(2)}, u32[]{:S(2)}) collective-permute-start(bf16[128,512]{1,0:T(8,128)(2,1)S(1)} %get-tuple-element.74), channel_id=1, source_target_pairs={{0,12},{1,13},{2,14},{3,15},{4,0},{5,1},{6,2},{7,3},{8,4},{9,5},{1... | collective-permute-start | bytes 393224 | tf_op jit(solution)/shard_map/ppermute | solution.py:300
  64.7 11.2 %collective-permute-start.14 = (bf16[128,512]{1,0:T(8,128)(2,1)S(1)}, bf16[128,512]{1,0:T(8,128)(2,1)S(1)}, u32[]{:S(2)}, u32[]{:S(2)}) collective-permute-start(bf16[128,512]{1,0:T(8,128)(2,1)S(1)} %get-tuple-element.75), channel_id=1, source_target_pairs={{0,8},{1,9},{2,10},{3,11},{4,12},{5,13},{6,14},{7,15},{8,0},{9,1},... | collective-permute-start | bytes 393224 | tf_op jit(solution)/shard_map/ppermute | solution.py:300
  75.9 1.2 copy-start.16
  78.6 0.8 copy-start.20
  79.4 5.6 %copy-start.21 = (bf16[32,8704]{1,0:T(8,128)(2,1)S(1)}, bf16[32,8704]{1,0:T(8,128)(2,1)}, u32[]{:S(2)}) copy-start(bf16[32,8704]{1,0:T(8,128)(2,1)} %copy-done.20) | copy-start | bytes 1671172
  79.4 4.7 %collective-permute-start.15 = (bf16[32,8704]{1,0:T(8,128)(2,1)}, bf16[32,8704]{1,0:T(8,128)(2,1)S(1)}, u32[]{:S(2)}, u32[]{:S(2)}) collective-permute-start(bf16[32,8704]{1,0:T(8,128)(2,1)} %get-tuple-element.77), channel_id=1, source_target_pairs={{0,16},{16,0},{32,48},{48,32},{64,80},{80,64},{96,112},{112,96},{1... | collective-permute-start | bytes 1671176 | tf_op jit(solution)/shard_map/ppermute | solution.py:308
  84.2 0.8 copy-start.7
  85.0 1.1 copy-start.8
  86.2 11.3 %collective-permute-start.16 = (bf16[32,2176]{1,0:T(8,128)(2,1)S(1)}, bf16[32,2176]{1,0:T(8,128)(2,1)S(1)}, u32[]{:S(2)}, u32[]{:S(2)}) collective-permute-start(bf16[32,2176]{1,0:T(8,128)(2,1)S(1)} %get-tuple-element.79), channel_id=1, source_target_pairs={{0,32},{16,48},{32,64},{48,80},{64,96},{80,112},{96,0},{112,16},{1... | collective-permute-start | bytes 417800 | tf_op jit(solution)/shard_map/ppermute | solution.py:304
  87.5 9.9 %collective-permute-start.17 = (bf16[32,2176]{1,0:T(8,128)(2,1)S(1)}, bf16[32,2176]{1,0:T(8,128)(2,1)S(1)}, u32[]{:S(2)}, u32[]{:S(2)}) collective-permute-start(bf16[32,2176]{1,0:T(8,128)(2,1)S(1)} %get-tuple-element.80), channel_id=1, source_target_pairs={{0,64},{16,80},{32,96},{48,112},{64,0},{80,16},{96,32},{112,48},{1... | collective-permute-start | bytes 417800 | tf_op jit(solution)/shard_map/ppermute | solution.py:304
  90.2 7.3 %collective-permute-start.18 = (bf16[32,2176]{1,0:T(8,128)(2,1)S(1)}, bf16[32,2176]{1,0:T(8,128)(2,1)S(1)}, u32[]{:S(2)}, u32[]{:S(2)}) collective-permute-start(bf16[32,2176]{1,0:T(8,128)(2,1)S(1)} %get-tuple-element.81), channel_id=1, source_target_pairs={{0,96},{16,112},{32,0},{48,16},{64,32},{80,48},{96,64},{112,80},{1... | collective-permute-start | bytes 417800 | tf_op jit(solution)/shard_map/ppermute | solution.py:304
  97.4 7.5 %copy-start.2 = (bf16[128,8192]{1,0:T(8,128)(2,1)}, bf16[128,8192]{1,0:T(8,128)(2,1)S(1)}, u32[]{:S(2)}) copy-start(bf16[128,8192]{1,0:T(8,128)(2,1)S(1)} %fusion.refs_4_) | copy-start | bytes 6291460
  97.6 7.4 %copy-start.5 = (bf16[32,2176]{1,0:T(8,128)(2,1)}, bf16[32,2176]{1,0:T(8,128)(2,1)S(1)}, u32[]{:S(2)}) copy-start(bf16[32,2176]{1,0:T(8,128)(2,1)S(1)} %y_sum.1.refs_3_.own) | copy-start | bytes 417796
  97.6 4.0 %collective-permute-start.24 = (bf16[32,2176]{1,0:T(8,128)(2,1)S(1)}, bf16[32,2176]{1,0:T(8,128)(2,1)S(1)}, u32[]{:S(2)}, u32[]{:S(2)}) collective-permute-start(bf16[32,2176]{1,0:T(8,128)(2,1)S(1)} %y_sum.1.refs_3_.own), channel_id=1, source_target_pairs={{0,4},{1,5},{2,6},{3,7},{4,0},{5,1},{6,2},{7,3},{8,12},{9,13},{10,... | collective-permute-start | bytes 417800 | tf_op jit(solution)/shard_map/ppermute | solution.py:331
  101.6 6.3 %collective-permute-start.25 = (bf16[32,2176]{1,0:T(8,128)(2,1)S(1)}, bf16[32,2176]{1,0:T(8,128)(2,1)}, u32[]{:S(2)}, u32[]{:S(2)}) collective-permute-start(bf16[32,2176]{1,0:T(8,128)(2,1)S(1)} %swap_sum.4.own), channel_id=1, source_target_pairs={{0,8},{1,9},{2,10},{3,11},{4,12},{5,13},{6,14},{7,15},{8,0},{9,1},... | collective-permute-start | bytes 417800 | tf_op jit(solution)/shard_map/ppermute | solution.py:331
  104.9 5.9 %collective-permute-start.19 = (bf16[2,128,512]{2,1,0:T(8,128)(2,1)}, bf16[2,128,512]{2,1,0:T(8,128)(2,1)S(1)}, u32[]{:S(2)}, u32[]{:S(2)}) collective-permute-start(bf16[2,128,512]{2,1,0:T(8,128)(2,1)} %get-tuple-element.84), channel_id=1, source_target_pairs={{0,3},{1,0},{2,1},{3,2},{4,7},{5,4},{6,5},{7,6},{8,11},{9,8},{10,9... | collective-permute-start | bytes 786440 | tf_op jit(solution)/shard_map/ppermute | solution.py:296
  106.6 7.0 %collective-permute-start.20 = (bf16[2,128,512]{2,1,0:T(8,128)(2,1)}, bf16[2,128,512]{2,1,0:T(8,128)(2,1)S(1)}, u32[]{:S(2)}, u32[]{:S(2)}) collective-permute-start(bf16[2,128,512]{2,1,0:T(8,128)(2,1)} %get-tuple-element.85), channel_id=1, source_target_pairs={{0,2},{1,3},{2,0},{3,1},{4,6},{5,7},{6,4},{7,5},{8,10},{9,11},{10,... | collective-permute-start | bytes 786440 | tf_op jit(solution)/shard_map/ppermute | solution.py:296
  107.4 13.7 %collective-permute-start.21 = (bf16[2,128,512]{2,1,0:T(8,128)(2,1)}, bf16[2,128,512]{2,1,0:T(8,128)(2,1)S(1)}, u32[]{:S(2)}, u32[]{:S(2)}) collective-permute-start(bf16[2,128,512]{2,1,0:T(8,128)(2,1)} %get-tuple-element.86), channel_id=1, source_target_pairs={{0,1},{1,2},{2,3},{3,0},{4,5},{5,6},{6,7},{7,4},{8,9},{9,10},{10,1... | collective-permute-start | bytes 786440 | tf_op jit(solution)/shard_map/ppermute | solution.py:296
  108.8 13.6 %collective-permute-start.26 = (bf16[32,2176]{1,0:T(8,128)(2,1)S(1)}, bf16[32,2176]{1,0:T(8,128)(2,1)S(1)}, u32[]{:S(2)}, u32[]{:S(2)}) collective-permute-start(bf16[32,2176]{1,0:T(8,128)(2,1)S(1)} %swap_sum.5.own), channel_id=1, source_target_pairs={{0,1},{1,0},{2,3},{3,2},{4,5},{5,4},{6,7},{7,6},{8,9},{9,8},{10,11... | collective-permute-start | bytes 417800 | tf_op jit(solution)/shard_map/ppermute | solution.py:331
  121.1 1.0 copy-start.22
  122.5 7.7 %collective-permute-start.27 = (bf16[32,2176]{1,0:T(8,128)(2,1)S(1)}, bf16[32,2176]{1,0:T(8,128)(2,1)S(1)}, u32[]{:S(2)}, u32[]{:S(2)}) collective-permute-start(bf16[32,2176]{1,0:T(8,128)(2,1)S(1)} %swap_sum.6.own), channel_id=1, source_target_pairs={{0,2},{1,3},{2,0},{3,1},{4,6},{5,7},{6,4},{7,5},{8,10},{9,11},{10,... | collective-permute-start | bytes 417800 | tf_op jit(solution)/shard_map/ppermute | solution.py:331
  123.4 10.1 %all-to-all-start = ((f32[16,1,384]{2,1,0:T(1,128)}), f32[16,1,384]{2,1,0:T(1,128)S(1)}, u32[]{:S(2)}, u32[]{:S(2)}) async-start(f32[16,1,384]{2,1,0:T(1,128)} %get-tuple-element.90), calls=%async_computation | async-start | bytes 49152 | tf_op jit(solution)/shard_map/all_to_all | solution.py:535
  127.0 7.3 %collective-permute-start.22 = (bf16[128,512]{1,0:T(8,128)(2,1)S(1)}, bf16[128,512]{1,0:T(8,128)(2,1)S(1)}, u32[]{:S(2)}, u32[]{:S(2)}) collective-permute-start(bf16[128,512]{1,0:T(8,128)(2,1)S(1)} %get-tuple-element.88), channel_id=1, source_target_pairs={{0,12},{1,13},{2,14},{3,15},{4,0},{5,1},{6,2},{7,3},{8,4},{9,5},{1... | collective-permute-start | bytes 393224 | tf_op jit(solution)/shard_map/ppermute | solution.py:300
  129.6 5.7 %collective-permute-start.23 = (bf16[128,512]{1,0:T(8,128)(2,1)S(1)}, bf16[128,512]{1,0:T(8,128)(2,1)S(1)}, u32[]{:S(2)}, u32[]{:S(2)}) collective-permute-start(bf16[128,512]{1,0:T(8,128)(2,1)S(1)} %get-tuple-element.89), channel_id=1, source_target_pairs={{0,8},{1,9},{2,10},{3,11},{4,12},{5,13},{6,14},{7,15},{8,0},{9,1},... | collective-permute-start | bytes 393224 | tf_op jit(solution)/shard_map/ppermute | solution.py:300
  130.2 6.7 %collective-permute-start.28 = (bf16[32,2176]{1,0:T(8,128)(2,1)S(1)}, bf16[32,2176]{1,0:T(8,128)(2,1)S(1)}, u32[]{:S(2)}, u32[]{:S(2)}) collective-permute-start(bf16[32,2176]{1,0:T(8,128)(2,1)S(1)} %swap_sum.7.refs_0_), channel_id=1, source_target_pairs={{0,32},{16,48},{32,64},{48,80},{64,96},{80,112},{96,0},{112,16},{1... | collective-permute-start | bytes 417800 | tf_op jit(solution)/shard_map/ppermute | solution.py:304
  130.7 6.2 %collective-permute-start.29 = (bf16[32,2176]{1,0:T(8,128)(2,1)S(1)}, bf16[32,2176]{1,0:T(8,128)(2,1)S(1)}, u32[]{:S(2)}, u32[]{:S(2)}) collective-permute-start(bf16[32,2176]{1,0:T(8,128)(2,1)S(1)} %swap_sum.7.refs_0_), channel_id=1, source_target_pairs={{0,64},{16,80},{32,96},{48,112},{64,0},{80,16},{96,32},{112,48},{1... | collective-permute-start | bytes 417800 | tf_op jit(solution)/shard_map/ppermute | solution.py:304
  132.7 5.1 %collective-permute-start.30 = (bf16[32,2176]{1,0:T(8,128)(2,1)S(1)}, bf16[32,2176]{1,0:T(8,128)(2,1)S(1)}, u32[]{:S(2)}, u32[]{:S(2)}) collective-permute-start(bf16[32,2176]{1,0:T(8,128)(2,1)S(1)} %swap_sum.7.refs_0_), channel_id=1, source_target_pairs={{0,96},{16,112},{32,0},{48,16},{64,32},{80,48},{96,64},{112,80},{1... | collective-permute-start | bytes 417800 | tf_op jit(solution)/shard_map/ppermute | solution.py:304
  137.8 0.9 copy-start.17
  138.7 0.8 copy-start.18
  139.5 6.0 %collective-permute-start.31 = (bf16[32,8704]{1,0:T(8,128)(2,1)S(1)}, bf16[32,8704]{1,0:T(8,128)(2,1)S(1)}, u32[]{:S(2)}, u32[]{:S(2)}) collective-permute-start(bf16[32,8704]{1,0:T(8,128)(2,1)S(1)} %assemble.1.mine), channel_id=1, source_target_pairs={{0,16},{16,0},{32,48},{48,32},{64,80},{80,64},{96,112},{112,96},{1... | collective-permute-start | bytes 1671176 | tf_op jit(solution)/shard_map/ppermute | solution.py:308

commit v4 on v3

--- a/solution.py
+++ b/solution.py
@@ -566,7 +566,7 @@
     dk_parts[1:] = gate(dk_parts[1:], mine)
     dk_terms = sum_home(dk_parts, z, here)
     (d_key,) = small_call(key_grad_kernel, in_vmem(3), [((TOK, KV), BF)], "key_grad", 1)(*dk_terms)
-    for axis_step, after in ((4, ()), (8, ()), (1, (dk_terms[0],)), (2, ())):
+    for axis_step, after in ((4, ()), (8, ()), (1, (dk_terms[0],)), (2, (lse_rows,))):
         mine = swap_sum(mine, axis_step, after)
     (whole,) = small_call(
         assemble_kernel,

time: 148 us -> 153 us (1.034)
  blocking collectives: 0 us -> 9.81 us
  starting transfers between devices: 51.3 us -> 47.6 us
  local copies, waits for them, and re-layouts: 11.2 us -> 9.41 us
    all_to_all x0 -> x1, blocking collectives: none -> 9.81 us  [local(): lax.all_to_all(own_lse, 'ctx', split_axis=0, concat_axis=0, tiled=True)]
    all_to_all x1 -> x0, starting transfers between devices: 3.59 us -> none  [local(): lax.all_to_all(own_lse, 'ctx', split_axis=0, concat_axis=0, tiled=True)]
    unnamed x52 -> x50, local copies, waits for them, and re-layouts: 11.2 us -> 9.41 us
    ppermute x6, waiting for transfers between devices: 1.76 us -> 3.57 us  [along_y(): return lax.ppermute(x, 'dp', [(i, (i + 2 * step) % 8) for i in range(8)])]
  transfers between devices with their start and end apart: 33 -> 32, of which waited for: 13 -> 12; matrix products, arithmetic and copies ran while one was open for 10% -> 10% of each run, Pallas kernels for 24% -> 23%
where the time goes in v4:
time: 153 us; the launch traced here: 152 us
  starting transfers between devices  47.6 us (31%)
  Pallas kernels  40.9 us (27%)
  waiting for transfers between devices  28.7 us (19%)
  matrix products  14.7 us (10%)
  blocking collectives  9.81 us (6%)
  local copies, waits for them, and re-layouts  9.41 us (6%)
    pallas_call x2, Pallas kernels, run_grads(): pl.pallas_call(grads_kernel, grid=(count,), in_specs=[smem(), pl.BlockSpe...  20.1 us
    ppermute x12, starting transfers between devices, along_z(): lax.ppermute(x, 'ctx', [(i, i // 4 * 4 + (i + step) % 4) for i in range(1...  15 us
    dot_general x5, matrix products, dot(): return lax.dot_general(a, b, dims, preferred_element_type=F32)  14.7 us
    ppermute x12, waiting for transfers between devices, along_z(): lax.ppermute(x, 'ctx', [(i, i // 4 * 4 + (i + step) % 4) for i in range(1...  13.7 us
    pallas_call x1, Pallas kernels, run_scores(): pl.pallas_call(scores_kernel, grid=(GROUPS,), in_specs=[smem(), line, lin...  12.4 us
    all_to_all x1, blocking collectives, local(): lax.all_to_all(own_lse, 'ctx', split_axis=0, concat_axis=0, tiled=True)  9.81 us
    ppermute x8, starting transfers between devices, along_x(): return lax.ppermute(x, 'ctx', [(i, (i + 4 * step) % 16) for i in range(16)])  9.78 us
    unnamed x50, local copies, waits for them, and re-layouts  9.41 us
  transfers between devices with their start and end apart: 32, of which 12 were waited for; matrix products, arithmetic and copies ran while one was open for 10% of the time, Pallas kernels for 23%

profile of v4, /device:TPU:1, one launch (start us, length us, event | category | flops | bytes accessed | tf_op | source)
XLA Modules:
  0.0 152.0 jit_solution(10782334575724195931)
XLA Ops:
  0.7 1.0 copy-done.9
  1.7 0.7 copy-done.12
  2.4 2.1 %collective-permute-start = (bf16[144,512]{1,0:T(8,128)(2,1)S(1)}, bf16[144,512]{1,0:T(8,128)(2,1)S(1)}, u32[]{:S(2)}, u32[]{:S(2)}) collective-permute-start(bf16[144,512]{1,0:T(8,128)(2,1)S(1)} %pack.1.own.rest_0_), channel_id=1, source_target_pairs={{0,4},{1,5},{2,6},{3,7},{4,8},{5,9},{6,10},{7,11},{8,12},{9,13},{1... | collective-permute-start | bytes 442376 | tf_op jit(solution)/shard_map/ppermute | solution.py:300
  4.5 2.5 %collective-permute-start.1 = (bf16[144,512]{1,0:T(8,128)(2,1)S(1)}, bf16[144,512]{1,0:T(8,128)(2,1)}, u32[]{:S(2)}, u32[]{:S(2)}) collective-permute-start(bf16[144,512]{1,0:T(8,128)(2,1)S(1)} %pack.1.own.rest_0_), channel_id=1, source_target_pairs={{0,8},{1,9},{2,10},{3,11},{4,12},{5,13},{6,14},{7,15},{8,0},{9,1},... | collective-permute-start | bytes 442376 | tf_op jit(solution)/shard_map/ppermute | solution.py:300
  7.0 5.3 %fusion.4 = f32[128,512]{1,0:T(8,128)} fusion(bf16[8192,512]{1,0:T(8,128)(2,1)} %param.12, bf16[1,128,8192]{2,1,0:T(8,128)(2,1)S(1)} %copy-done.1), kind=kOutput, calls=%fused_computation.7 | convolution fusion | flops 1073741824 | bytes 10747904 | tf_op jit(solution)/shard_map/dot_general | solution.py:38
  12.3 0.7 convolution_convert_fusion.refs_4_
  13.0 0.4 collective-permute-done.1.row_2.rest_2_
  13.5 1.9 %pick.2 = (bf16[2,144,512]{2,1,0:T(8,128)(2,1)}, bf16[2,144,512]{2,1,0:T(8,128)(2,1)}, bf16[2,144,512]{2,1,0:T(8,128)(2,1)}) custom-call(s32[1]{0:T(128)} %bitcast.5.z_ref, bf16[144,512]{1,0:T(8,128)(2,1)S(1)} %pack.1.own.rest_0_, bf16[144,512]{1,0:T(8,128)(2,1)S(1)} %collective-permute-done.row_1.refs_1_.rest_1_, ...), custom_call_target="tpu_custom_call" | custom-call | flops 1073741824 | bytes 2097152 | tf_op jit(solution)/shard_map/pick/pallas_call | solution.py:320
  15.3 1.6 %collective-permute-start.2 = (bf16[2,144,512]{2,1,0:T(8,128)(2,1)}, bf16[2,144,512]{2,1,0:T(8,128)(2,1)}, u32[]{:S(2)}, u32[]{:S(2)}) collective-permute-start(bf16[2,144,512]{2,1,0:T(8,128)(2,1)} %get-tuple-element.50), channel_id=1, source_target_pairs={{0,1},{1,2},{2,3},{3,0},{4,5},{5,6},{6,7},{7,4},{8,9},{9,10},{10,1... | collective-permute-start | bytes 884744 | tf_op jit(solution)/shard_map/ppermute | solution.py:296
  17.0 3.3 %collective-permute-start.3 = (bf16[2,144,512]{2,1,0:T(8,128)(2,1)}, bf16[2,144,512]{2,1,0:T(8,128)(2,1)}, u32[]{:S(2)}, u32[]{:S(2)}) collective-permute-start(bf16[2,144,512]{2,1,0:T(8,128)(2,1)} %get-tuple-element.51), channel_id=1, source_target_pairs={{0,2},{1,3},{2,0},{3,1},{4,6},{5,7},{6,4},{7,5},{8,10},{9,11},{10,... | collective-permute-start | bytes 884744 | tf_op jit(solution)/shard_map/ppermute | solution.py:296
  20.3 0.7 collective-permute-start.4
  21.0 1.8 %fusion.2.refs_0_ = bf16[128,512]{1,0:T(8,128)(2,1)} fusion(f32[128,512]{1,0:T(8,128)} %fusion.4, bf16[128,64]{1,0:T(8,128)(2,1)S(1)} %convolution_convert_fusion.refs_4_, bf16[64,512]{1,0:T(8,128)(2,1)S(1)} %copy-done.6), kind=kOutput, calls=%fused_computation.4 | convolution fusion | flops 8585216 | bytes 475136 | tf_op jit(solution)/shard_map/dot_general | solution.py:38
  22.8 2.0 %collective-permute-start.6 = (bf16[128,512]{1,0:T(8,128)(2,1)}, bf16[128,512]{1,0:T(8,128)(2,1)S(1)}, u32[]{:S(2)}, u32[]{:S(2)}) collective-permute-start(bf16[128,512]{1,0:T(8,128)(2,1)} %gate.2.own.rest_6_), channel_id=1, source_target_pairs={{0,8},{1,9},{2,10},{3,11},{4,12},{5,13},{6,14},{7,15},{8,0},{9,1},... | collective-permute-start | bytes 393224 | tf_op jit(solution)/shard_map/ppermute | solution.py:300
  24.8 4.7 %collective-permute-done.5.row_1.rest_7_ = bf16[128,512]{1,0:T(8,128)(2,1)S(1)} collective-permute-done((bf16[128,512]{1,0:T(8,128)(2,1)}, bf16[128,512]{1,0:T(8,128)(2,1)S(1)}, u32[]{:S(2)}, u32[]{:S(2)}) %collective-permute-start.5) | collective-permute-done | bytes 131104 | tf_op jit(solution)/shard_map/ppermute | solution.py:300
  29.4 1.0 copy-done.3
  30.5 1.0 collective-permute-start.7
  31.5 0.8 collective-permute-start.8
  32.3 1.7 %collective-permute-start.9 = (bf16[2,128,512]{2,1,0:T(8,128)(2,1)S(1)}, bf16[2,128,512]{2,1,0:T(8,128)(2,1)S(1)}, u32[]{:S(2)}, u32[]{:S(2)}) collective-permute-start(bf16[2,128,512]{2,1,0:T(8,128)(2,1)S(1)} %get-tuple-element.56), channel_id=1, source_target_pairs={{0,3},{1,0},{2,1},{3,2},{4,7},{5,4},{6,5},{7,6},{8,11},{9,8},{10,9... | collective-permute-start | bytes 786440 | tf_op jit(solution)/shard_map/ppermute | solution.py:296
  34.0 12.4 %scores.1 = (f32[4,8,128]{2,1,0:T(8,128)}, f32[16,1,384]{2,1,0:T(1,128)}, bf16[3,128,512]{2,1,0:T(8,128)(2,1)}, bf16[2,128,512]{2,1,0:T(8,128)(2,1)}, bf16[2,128...) custom-call(s32[1]{0:T(128)} %bitcast.here_ref.refs_3_, s32[1,128]{1,0:T(1,128)} %docs_ref.5, s32[1,128]{1,0:T(1,128)} %bitcast.41, ...), custom_call_target="tpu_custom_call" | custom-call | flops 34359738368 | bytes 6291456 | tf_op jit(solution)/shard_map/scores/pallas_call | solution.py:228
  46.4 2.2 %collective-permute-start.10 = (bf16[2,128,512]{2,1,0:T(8,128)(2,1)}, bf16[2,128,512]{2,1,0:T(8,128)(2,1)S(1)}, u32[]{:S(2)}, u32[]{:S(2)}) collective-permute-start(bf16[2,128,512]{2,1,0:T(8,128)(2,1)} %get-tuple-element.70), channel_id=1, source_target_pairs={{0,3},{1,0},{2,1},{3,2},{4,7},{5,4},{6,5},{7,6},{8,11},{9,8},{10,9... | collective-permute-start | bytes 786440 | tf_op jit(solution)/shard_map/ppermute | solution.py:296
  49.3 0.4 copy-done.22
  50.1 10.1 %grads_0.1 = (bf16[128,4096]{1,0:T(8,128)(2,1)}, bf16[128,4096]{1,0:T(8,128)(2,1)}, bf16[3,128,512]{2,1,0:T(8,128)(2,1)}, bf16[2,128,512]{2,1,0:T(8,128)(2,1)}, ...) custom-call(s32[1]{0:T(128)} %bitcast.here_ref.refs_3_, s32[1,128]{1,0:T(1,128)} %docs_ref.5, ...), custom_call_target="tpu_custom_call" | custom-call | flops 34359738368 | bytes 8388608 | tf_op jit(solution)/shard_map/grads_0/pallas_call | solution.py:261
  60.2 2.9 %collective-permute-done.12.refs_2_ = bf16[2,128,512]{2,1,0:T(8,128)(2,1)S(1)} collective-permute-done((bf16[2,128,512]{2,1,0:T(8,128)(2,1)}, bf16[2,128,512]{2,1,0:T(8,128)(2,1)S(1)}, u32[]{:S(2)}, u32[]{:S(2)}) %collective-permute-start.12) | collective-permute-done | bytes 262176 | tf_op jit(solution)/shard_map/ppermute | solution.py:296
  63.1 1.2 copy-done.13
  64.7 1.1 collective-permute-start.14
  65.8 10.0 %grads_2.1 = (bf16[128,4096]{1,0:T(8,128)(2,1)}, bf16[128,4096]{1,0:T(8,128)(2,1)}, bf16[3,128,512]{2,1,0:T(8,128)(2,1)}, bf16[2,128,512]{2,1,0:T(8,128)(2,1)}, ...) custom-call(s32[1]{0:T(128)} %bitcast.here_ref.refs_3_, ...), custom_call_target="tpu_custom_call", output_to_operand_aliasing={{0}: (17, {}), {1}: (18, {}), {2}: (19, {}), {3}: (20, {}),... | custom-call | flops 34359738368 | bytes 8388608 | tf_op jit(solution)/shard_map/grads_2/pallas_call | solution.py:261
  75.9 1.2 copy-done.14
  77.1 1.5 adapter.1
  78.6 0.8 copy-done.18
  79.4 3.0 %collective-permute-start.15 = (bf16[32,8704]{1,0:T(8,128)(2,1)}, bf16[32,8704]{1,0:T(8,128)(2,1)S(1)}, u32[]{:S(2)}, u32[]{:S(2)}) collective-permute-start(bf16[32,8704]{1,0:T(8,128)(2,1)} %get-tuple-element.77), channel_id=1, source_target_pairs={{0,16},{16,0},{32,48},{48,32},{64,80},{80,64},{96,112},{112,96},{1... | collective-permute-start | bytes 1671176 | tf_op jit(solution)/shard_map/ppermute | solution.py:308
  82.4 0.7 fusion.6
  83.1 1.1 collective-permute-done.15.got
  84.3 1.4 collective-permute-start.16
  85.7 2.6 %collective-permute-start.17 = (bf16[32,2176]{1,0:T(8,128)(2,1)S(1)}, bf16[32,2176]{1,0:T(8,128)(2,1)S(1)}, u32[]{:S(2)}, u32[]{:S(2)}) collective-permute-start(bf16[32,2176]{1,0:T(8,128)(2,1)S(1)} %get-tuple-element.80), channel_id=1, source_target_pairs={{0,64},{16,80},{32,96},{48,112},{64,0},{80,16},{96,32},{112,48},{1... | collective-permute-start | bytes 417800 | tf_op jit(solution)/shard_map/ppermute | solution.py:304
  88.3 1.1 collective-permute-start.18
  89.4 6.2 %fusion.refs_4_ = bf16[128,8192]{1,0:T(8,128)(2,1)S(1)} fusion(f32[128,8192]{1,0:T(8,128)S(1)} %fusion.6, bf16[128,512]{1,0:T(8,128)(2,1)S(1)} %get-tuple-element.82, bf16[8192,512]{1,0:T(8,128)(2,1)} %param.12), kind=kOutput, calls=%fused_computation.1 | convolution fusion | flops 1075838976 | bytes 14811136 | tf_op jit(solution)/shard_map/dot_general | solution.py:38
  95.8 0.8 collective-permute-start.24
  96.5 3.2 %collective-permute-done.24.got = bf16[32,2176]{1,0:T(8,128)(2,1)S(1)} collective-permute-done((bf16[32,2176]{1,0:T(8,128)(2,1)S(1)}, bf16[32,2176]{1,0:T(8,128)(2,1)S(1)}, u32[]{:S(2)}, u32[]{:S(2)}) %collective-permute-start.24) | collective-permute-done | bytes 139296 | tf_op jit(solution)/shard_map/ppermute | solution.py:331
  99.8 3.3 %collective-permute-start.25 = (bf16[32,2176]{1,0:T(8,128)(2,1)S(1)}, bf16[32,2176]{1,0:T(8,128)(2,1)}, u32[]{:S(2)}, u32[]{:S(2)}) collective-permute-start(bf16[32,2176]{1,0:T(8,128)(2,1)S(1)} %swap_sum.4.own), channel_id=1, source_target_pairs={{0,8},{1,9},{2,10},{3,11},{4,12},{5,13},{6,14},{7,15},{8,0},{9,1},... | collective-permute-start | bytes 417800 | tf_op jit(solution)/shard_map/ppermute | solution.py:331
  103.1 1.6 %collective-permute-start.19 = (bf16[2,128,512]{2,1,0:T(8,128)(2,1)}, bf16[2,128,512]{2,1,0:T(8,128)(2,1)S(1)}, u32[]{:S(2)}, u32[]{:S(2)}) collective-permute-start(bf16[2,128,512]{2,1,0:T(8,128)(2,1)} %get-tuple-element.84), channel_id=1, source_target_pairs={{0,3},{1,0},{2,1},{3,2},{4,7},{5,4},{6,5},{7,6},{8,11},{9,8},{10,9... | collective-permute-start | bytes 786440 | tf_op jit(solution)/shard_map/ppermute | solution.py:296
  104.7 0.9 collective-permute-start.20
  105.6 0.4 collective-permute-start.21
  106.0 0.9 swap_sum.5.own
  107.0 1.4 collective-permute-start.26
  108.4 0.6 collective-permute-done.19.refs_0_
  109.0 2.8 %collective-permute-done.20.refs_1_ = bf16[2,128,512]{2,1,0:T(8,128)(2,1)S(1)} collective-permute-done((bf16[2,128,512]{2,1,0:T(8,128)(2,1)}, bf16[2,128,512]{2,1,0:T(8,128)(2,1)S(1)}, u32[]{:S(2)}, u32[]{:S(2)}) %collective-permute-start.20) | collective-permute-done | bytes 262176 | tf_op jit(solution)/shard_map/ppermute | solution.py:296
  111.8 7.5 %collective-permute-done.21.refs_2_ = bf16[2,128,512]{2,1,0:T(8,128)(2,1)S(1)} collective-permute-done((bf16[2,128,512]{2,1,0:T(8,128)(2,1)}, bf16[2,128,512]{2,1,0:T(8,128)(2,1)S(1)}, u32[]{:S(2)}, u32[]{:S(2)}) %collective-permute-start.21) | collective-permute-done | bytes 262176 | tf_op jit(solution)/shard_map/ppermute | solution.py:296
  119.3 1.0 copy-done.20
  120.6 1.0 collective-permute-start.27
  121.6 9.8 %all_to_all.5.got = f32[16,1,384]{2,1,0:T(1,128)S(1)} all-to-all(f32[16,1,384]{2,1,0:T(1,128)S(1)} %copy-done.21), channel_id=1, replica_groups=mesh['dp'=8,'ctx'=16] {'ctx'}, dimensions={0} | all-to-all | bytes 49152 | tf_op jit(solution)/shard_map/all_to_all | solution.py:535
  131.4 0.8 slots.1.refs_0_.refs_5_
  132.2 0.9 collective-permute-start.22
  133.1 1.2 collective-permute-start.23
  134.3 0.8 copy-done.16
  135.1 0.5 collective-permute-start.28
  135.5 2.1 %collective-permute-start.29 = (bf16[32,2176]{1,0:T(8,128)(2,1)S(1)}, bf16[32,2176]{1,0:T(8,128)(2,1)S(1)}, u32[]{:S(2)}, u32[]{:S(2)}) collective-permute-start(bf16[32,2176]{1,0:T(8,128)(2,1)S(1)} %swap_sum.7.refs_0_), channel_id=1, source_target_pairs={{0,64},{16,80},{32,96},{48,112},{64,0},{80,16},{96,32},{112,48},{1... | collective-permute-start | bytes 417800 | tf_op jit(solution)/shard_map/ppermute | solution.py:304
  137.6 0.5 collective-permute-start.30
  138.4 0.7 key_grad.1.refs_4_
  139.1 2.9 %collective-permute-done.28.refs_1_ = bf16[32,2176]{1,0:T(8,128)(2,1)S(1)} collective-permute-done((bf16[32,2176]{1,0:T(8,128)(2,1)S(1)}, bf16[32,2176]{1,0:T(8,128)(2,1)S(1)}, u32[]{:S(2)}, u32[]{:S(2)}) %collective-permute-start.28) | collective-permute-done | bytes 139296 | tf_op jit(solution)/shard_map/ppermute | solution.py:304
  142.0 0.6 collective-permute-done.30.refs_3_
  142.7 0.9 copy-done.15
  143.6 5.4 %collective-permute-start.31 = (bf16[32,8704]{1,0:T(8,128)(2,1)S(1)}, bf16[32,8704]{1,0:T(8,128)(2,1)S(1)}, u32[]{:S(2)}, u32[]{:S(2)}) collective-permute-start(bf16[32,8704]{1,0:T(8,128)(2,1)S(1)} %assemble.1.mine), channel_id=1, source_target_pairs={{0,16},{16,0},{32,48},{48,32},{64,80},{80,64},{96,112},{112,96},{1... | collective-permute-start | bytes 1671176 | tf_op jit(solution)/shard_map/ppermute | solution.py:308
  149.0 1.6 %collective-permute-done.31.other = bf16[32,8704]{1,0:T(8,128)(2,1)S(1)} collective-permute-done((bf16[32,8704]{1,0:T(8,128)(2,1)S(1)}, bf16[32,8704]{1,0:T(8,128)(2,1)S(1)}, u32[]{:S(2)}, u32[]{:S(2)}) %collective-permute-start.31) | collective-permute-done | bytes 557088 | tf_op jit(solution)/shard_map/ppermute | solution.py:308
  150.6 1.5 totals.1
  (77 shorter events, 2.7 us)
Async XLA Ops:
  0.6 11.7 %copy-start = (bf16[8192,64]{0,1:T(8,128)(2,1)S(1)}, bf16[8192,64]{0,1:T(8,128)(2,1)}, u32[]{:S(2)}) copy-start(bf16[8192,64]{0,1:T(8,128)(2,1)} %param.13) | copy-start | bytes 3145732
  0.6 6.3 %copy-start.1 = (bf16[1,128,8192]{2,1,0:T(8,128)(2,1)S(1)}, bf16[1,128,8192]{2,1,0:T(8,128)(2,1)}, u32[]{:S(2)}) copy-start(bf16[1,128,8192]{2,1,0:T(8,128)(2,1)} %param.9) | copy-start | bytes 6291460
  0.7 1.1 copy-start.9
  1.7 0.7 copy-start.12
  2.4 11.1 %copy-start.8 = (bf16[144,512]{1,0:T(8,128)(2,1)}, bf16[144,512]{1,0:T(8,128)(2,1)S(1)}, u32[]{:S(2)}) copy-start(bf16[144,512]{1,0:T(8,128)(2,1)S(1)} %pack.1.own.rest_0_) | copy-start | bytes 442372
  2.4 10.6 %collective-permute-start = (bf16[144,512]{1,0:T(8,128)(2,1)S(1)}, bf16[144,512]{1,0:T(8,128)(2,1)S(1)}, u32[]{:S(2)}, u32[]{:S(2)}) collective-permute-start(bf16[144,512]{1,0:T(8,128)(2,1)S(1)} %pack.1.own.rest_0_), channel_id=1, source_target_pairs={{0,4},{1,5},{2,6},{3,7},{4,8},{5,9},{6,10},{7,11},{8,12},{9,13},{1... | collective-permute-start | bytes 442376 | tf_op jit(solution)/shard_map/ppermute | solution.py:300
  4.5 9.0 %collective-permute-start.1 = (bf16[144,512]{1,0:T(8,128)(2,1)S(1)}, bf16[144,512]{1,0:T(8,128)(2,1)}, u32[]{:S(2)}, u32[]{:S(2)}) collective-permute-start(bf16[144,512]{1,0:T(8,128)(2,1)S(1)} %pack.1.own.rest_0_), channel_id=1, source_target_pairs={{0,8},{1,9},{2,10},{3,11},{4,12},{5,13},{6,14},{7,15},{8,0},{9,1},... | collective-permute-start | bytes 442376 | tf_op jit(solution)/shard_map/ppermute | solution.py:300
  12.3 8.7 %copy-start.6 = (bf16[64,512]{1,0:T(8,128)(2,1)S(1)}, bf16[64,512]{1,0:T(8,128)(2,1)}, u32[]{:S(2)}) copy-start(bf16[64,512]{1,0:T(8,128)(2,1)} %refs_3_.1) | copy-start | bytes 196612
  13.0 9.8 %copy-start.4 = (bf16[144,512]{1,0:T(8,128)(2,1)}, bf16[144,512]{1,0:T(8,128)(2,1)S(1)}, u32[]{:S(2)}) copy-start(bf16[144,512]{1,0:T(8,128)(2,1)S(1)} %collective-permute-done.row_1.refs_1_.rest_1_) | copy-start | bytes 442372
  15.3 16.9 %collective-permute-start.2 = (bf16[2,144,512]{2,1,0:T(8,128)(2,1)}, bf16[2,144,512]{2,1,0:T(8,128)(2,1)}, u32[]{:S(2)}, u32[]{:S(2)}) collective-permute-start(bf16[2,144,512]{2,1,0:T(8,128)(2,1)} %get-tuple-element.50), channel_id=1, source_target_pairs={{0,1},{1,2},{2,3},{3,0},{4,5},{5,6},{6,7},{7,4},{8,9},{9,10},{10,1... | collective-permute-start | bytes 884744 | tf_op jit(solution)/shard_map/ppermute | solution.py:296
  17.0 17.0 %collective-permute-start.3 = (bf16[2,144,512]{2,1,0:T(8,128)(2,1)}, bf16[2,144,512]{2,1,0:T(8,128)(2,1)}, u32[]{:S(2)}, u32[]{:S(2)}) collective-permute-start(bf16[2,144,512]{2,1,0:T(8,128)(2,1)} %get-tuple-element.51), channel_id=1, source_target_pairs={{0,2},{1,3},{2,0},{3,1},{4,6},{5,7},{6,4},{7,5},{8,10},{9,11},{10,... | collective-permute-start | bytes 884744 | tf_op jit(solution)/shard_map/ppermute | solution.py:296
  20.3 13.7 %collective-permute-start.4 = (bf16[2,144,512]{2,1,0:T(8,128)(2,1)}, bf16[2,144,512]{2,1,0:T(8,128)(2,1)}, u32[]{:S(2)}, u32[]{:S(2)}) collective-permute-start(bf16[2,144,512]{2,1,0:T(8,128)(2,1)} %get-tuple-element.52), channel_id=1, source_target_pairs={{0,3},{1,0},{2,1},{3,2},{4,7},{5,4},{6,5},{7,6},{8,11},{9,8},{10,9... | collective-permute-start | bytes 884744 | tf_op jit(solution)/shard_map/ppermute | solution.py:296
  22.8 6.6 %collective-permute-start.5 = (bf16[128,512]{1,0:T(8,128)(2,1)}, bf16[128,512]{1,0:T(8,128)(2,1)S(1)}, u32[]{:S(2)}, u32[]{:S(2)}) collective-permute-start(bf16[128,512]{1,0:T(8,128)(2,1)} %gate.2.own.rest_6_), channel_id=1, source_target_pairs={{0,4},{1,5},{2,6},{3,7},{4,8},{5,9},{6,10},{7,11},{8,12},{9,13},{1... | collective-permute-start | bytes 393224 | tf_op jit(solution)/shard_map/ppermute | solution.py:300
  22.8 6.6 %collective-permute-start.6 = (bf16[128,512]{1,0:T(8,128)(2,1)}, bf16[128,512]{1,0:T(8,128)(2,1)S(1)}, u32[]{:S(2)}, u32[]{:S(2)}) collective-permute-start(bf16[128,512]{1,0:T(8,128)(2,1)} %gate.2.own.rest_6_), channel_id=1, source_target_pairs={{0,8},{1,9},{2,10},{3,11},{4,12},{5,13},{6,14},{7,15},{8,0},{9,1},... | collective-permute-start | bytes 393224 | tf_op jit(solution)/shard_map/ppermute | solution.py:300
  29.4 17.0 %copy-start.10 = (bf16[128,512]{1,0:T(8,128)(2,1)}, bf16[128,512]{1,0:T(8,128)(2,1)S(1)}, u32[]{:S(2)}) copy-start(bf16[128,512]{1,0:T(8,128)(2,1)S(1)} %collective-permute-done.5.row_1.rest_7_) | copy-start | bytes 393220
  29.4 1.0 copy-start.3
  30.4 16.0 %copy-start.11 = (bf16[128,512]{1,0:T(8,128)(2,1)}, bf16[128,512]{1,0:T(8,128)(2,1)S(1)}, u32[]{:S(2)}) copy-start(bf16[128,512]{1,0:T(8,128)(2,1)S(1)} %collective-permute-done.6.row_2.rest_8_) | copy-start | bytes 393220
  30.5 3.6 %copy-start.7 = (bf16[2,128,512]{2,1,0:T(8,128)(2,1)}, bf16[2,128,512]{2,1,0:T(8,128)(2,1)S(1)}, u32[]{:S(2)}) copy-start(bf16[2,128,512]{2,1,0:T(8,128)(2,1)S(1)} %get-tuple-element.53.rest_6_) | copy-start | bytes 786436
  30.5 18.5 %collective-permute-start.7 = (bf16[2,128,512]{2,1,0:T(8,128)(2,1)S(1)}, bf16[2,128,512]{2,1,0:T(8,128)(2,1)S(1)}, u32[]{:S(2)}, u32[]{:S(2)}) collective-permute-start(bf16[2,128,512]{2,1,0:T(8,128)(2,1)S(1)} %get-tuple-element.53.rest_6_), channel_id=1, source_target_pairs={{0,1},{1,2},{2,3},{3,0},{4,5},{5,6},{6,7},{7,4},{8,9},{9,10},{10,1... | collective-permute-start | bytes 786440 | tf_op jit(solution)/shard_map/ppermute | solution.py:296
  31.5 17.8 %collective-permute-start.8 = (bf16[2,128,512]{2,1,0:T(8,128)(2,1)S(1)}, bf16[2,128,512]{2,1,0:T(8,128)(2,1)S(1)}, u32[]{:S(2)}, u32[]{:S(2)}) collective-permute-start(bf16[2,128,512]{2,1,0:T(8,128)(2,1)S(1)} %get-tuple-element.55), channel_id=1, source_target_pairs={{0,2},{1,3},{2,0},{3,1},{4,6},{5,7},{6,4},{7,5},{8,10},{9,11},{10,... | collective-permute-start | bytes 786440 | tf_op jit(solution)/shard_map/ppermute | solution.py:296
  32.3 17.0 %collective-permute-start.9 = (bf16[2,128,512]{2,1,0:T(8,128)(2,1)S(1)}, bf16[2,128,512]{2,1,0:T(8,128)(2,1)S(1)}, u32[]{:S(2)}, u32[]{:S(2)}) collective-permute-start(bf16[2,128,512]{2,1,0:T(8,128)(2,1)S(1)} %get-tuple-element.56), channel_id=1, source_target_pairs={{0,3},{1,0},{2,1},{3,2},{4,7},{5,4},{6,5},{7,6},{8,11},{9,8},{10,9... | collective-permute-start | bytes 786440 | tf_op jit(solution)/shard_map/ppermute | solution.py:296
  46.4 13.8 %collective-permute-start.10 = (bf16[2,128,512]{2,1,0:T(8,128)(2,1)}, bf16[2,128,512]{2,1,0:T(8,128)(2,1)S(1)}, u32[]{:S(2)}, u32[]{:S(2)}) collective-permute-start(bf16[2,128,512]{2,1,0:T(8,128)(2,1)} %get-tuple-element.70), channel_id=1, source_target_pairs={{0,3},{1,0},{2,1},{3,2},{4,7},{5,4},{6,5},{7,6},{8,11},{9,8},{10,9... | collective-permute-start | bytes 786440 | tf_op jit(solution)/shard_map/ppermute | solution.py:296
  48.6 11.6 %collective-permute-start.11 = (bf16[2,128,512]{2,1,0:T(8,128)(2,1)}, bf16[2,128,512]{2,1,0:T(8,128)(2,1)S(1)}, u32[]{:S(2)}, u32[]{:S(2)}) collective-permute-start(bf16[2,128,512]{2,1,0:T(8,128)(2,1)} %get-tuple-element.71), channel_id=1, source_target_pairs={{0,2},{1,3},{2,0},{3,1},{4,6},{5,7},{6,4},{7,5},{8,10},{9,11},{10,... | collective-permute-start | bytes 786440 | tf_op jit(solution)/shard_map/ppermute | solution.py:296
  49.0 0.7 copy-start.22
  49.0 14.1 %collective-permute-start.12 = (bf16[2,128,512]{2,1,0:T(8,128)(2,1)}, bf16[2,128,512]{2,1,0:T(8,128)(2,1)S(1)}, u32[]{:S(2)}, u32[]{:S(2)}) collective-permute-start(bf16[2,128,512]{2,1,0:T(8,128)(2,1)} %get-tuple-element.72), channel_id=1, source_target_pairs={{0,1},{1,2},{2,3},{3,0},{4,5},{5,6},{6,7},{7,4},{8,9},{9,10},{10,1... | collective-permute-start | bytes 786440 | tf_op jit(solution)/shard_map/ppermute | solution.py:296
  49.3 0.7 copy-start.23
  49.3 0.8 copy-start.24
  50.1 13.0 %copy-start.17 = (bf16[3,128,512]{2,1,0:T(8,128)(2,1)S(1)}, bf16[3,128,512]{2,1,0:T(8,128)(2,1)}, u32[]{:S(2)}) copy-start(bf16[3,128,512]{2,1,0:T(8,128)(2,1)} %get-tuple-element.69.own) | copy-start | bytes 1179652
  63.1 1.2 copy-start.13
  64.6 11.2 %collective-permute-start.13 = (bf16[128,512]{1,0:T(8,128)(2,1)S(1)}, bf16[128,512]{1,0:T(8,128)(2,1)S(1)}, u32[]{:S(2)}, u32[]{:S(2)}) collective-permute-start(bf16[128,512]{1,0:T(8,128)(2,1)S(1)} %get-tuple-element.74), channel_id=1, source_target_pairs={{0,12},{1,13},{2,14},{3,15},{4,0},{5,1},{6,2},{7,3},{8,4},{9,5},{1... | collective-permute-start | bytes 393224 | tf_op jit(solution)/shard_map/ppermute | solution.py:300
  64.7 11.2 %collective-permute-start.14 = (bf16[128,512]{1,0:T(8,128)(2,1)S(1)}, bf16[128,512]{1,0:T(8,128)(2,1)S(1)}, u32[]{:S(2)}, u32[]{:S(2)}) collective-permute-start(bf16[128,512]{1,0:T(8,128)(2,1)S(1)} %get-tuple-element.75), channel_id=1, source_target_pairs={{0,8},{1,9},{2,10},{3,11},{4,12},{5,13},{6,14},{7,15},{8,0},{9,1},... | collective-permute-start | bytes 393224 | tf_op jit(solution)/shard_map/ppermute | solution.py:300
  75.9 1.2 copy-start.14
  78.6 0.8 copy-start.18
  79.4 4.8 %copy-start.19 = (bf16[32,8704]{1,0:T(8,128)(2,1)S(1)}, bf16[32,8704]{1,0:T(8,128)(2,1)}, u32[]{:S(2)}) copy-start(bf16[32,8704]{1,0:T(8,128)(2,1)} %copy-done.18) | copy-start | bytes 1671172
  79.4 4.8 %collective-permute-start.15 = (bf16[32,8704]{1,0:T(8,128)(2,1)}, bf16[32,8704]{1,0:T(8,128)(2,1)S(1)}, u32[]{:S(2)}, u32[]{:S(2)}) collective-permute-start(bf16[32,8704]{1,0:T(8,128)(2,1)} %get-tuple-element.77), channel_id=1, source_target_pairs={{0,16},{16,0},{32,48},{48,32},{64,80},{80,64},{96,112},{112,96},{1... | collective-permute-start | bytes 1671176 | tf_op jit(solution)/shard_map/ppermute | solution.py:308
  84.3 11.3 %collective-permute-start.16 = (bf16[32,2176]{1,0:T(8,128)(2,1)S(1)}, bf16[32,2176]{1,0:T(8,128)(2,1)S(1)}, u32[]{:S(2)}, u32[]{:S(2)}) collective-permute-start(bf16[32,2176]{1,0:T(8,128)(2,1)S(1)} %get-tuple-element.79), channel_id=1, source_target_pairs={{0,32},{16,48},{32,64},{48,80},{64,96},{80,112},{96,0},{112,16},{1... | collective-permute-start | bytes 417800 | tf_op jit(solution)/shard_map/ppermute | solution.py:304
  85.7 9.9 %collective-permute-start.17 = (bf16[32,2176]{1,0:T(8,128)(2,1)S(1)}, bf16[32,2176]{1,0:T(8,128)(2,1)S(1)}, u32[]{:S(2)}, u32[]{:S(2)}) collective-permute-start(bf16[32,2176]{1,0:T(8,128)(2,1)S(1)} %get-tuple-element.80), channel_id=1, source_target_pairs={{0,64},{16,80},{32,96},{48,112},{64,0},{80,16},{96,32},{112,48},{1... | collective-permute-start | bytes 417800 | tf_op jit(solution)/shard_map/ppermute | solution.py:304
  88.3 7.3 %collective-permute-start.18 = (bf16[32,2176]{1,0:T(8,128)(2,1)S(1)}, bf16[32,2176]{1,0:T(8,128)(2,1)S(1)}, u32[]{:S(2)}, u32[]{:S(2)}) collective-permute-start(bf16[32,2176]{1,0:T(8,128)(2,1)S(1)} %get-tuple-element.81), channel_id=1, source_target_pairs={{0,96},{16,112},{32,0},{48,16},{64,32},{80,48},{96,64},{112,80},{1... | collective-permute-start | bytes 417800 | tf_op jit(solution)/shard_map/ppermute | solution.py:304
  95.6 7.5 %copy-start.2 = (bf16[128,8192]{1,0:T(8,128)(2,1)}, bf16[128,8192]{1,0:T(8,128)(2,1)S(1)}, u32[]{:S(2)}) copy-start(bf16[128,8192]{1,0:T(8,128)(2,1)S(1)} %fusion.refs_4_) | copy-start | bytes 6291460
  95.7 7.4 %copy-start.5 = (bf16[32,2176]{1,0:T(8,128)(2,1)}, bf16[32,2176]{1,0:T(8,128)(2,1)S(1)}, u32[]{:S(2)}) copy-start(bf16[32,2176]{1,0:T(8,128)(2,1)S(1)} %y_sum.1.refs_3_.own) | copy-start | bytes 417796
  95.8 4.0 %collective-permute-start.24 = (bf16[32,2176]{1,0:T(8,128)(2,1)S(1)}, bf16[32,2176]{1,0:T(8,128)(2,1)S(1)}, u32[]{:S(2)}, u32[]{:S(2)}) collective-permute-start(bf16[32,2176]{1,0:T(8,128)(2,1)S(1)} %y_sum.1.refs_3_.own), channel_id=1, source_target_pairs={{0,4},{1,5},{2,6},{3,7},{4,0},{5,1},{6,2},{7,3},{8,12},{9,13},{10,... | collective-permute-start | bytes 417800 | tf_op jit(solution)/shard_map/ppermute | solution.py:331
  99.8 6.3 %collective-permute-start.25 = (bf16[32,2176]{1,0:T(8,128)(2,1)S(1)}, bf16[32,2176]{1,0:T(8,128)(2,1)}, u32[]{:S(2)}, u32[]{:S(2)}) collective-permute-start(bf16[32,2176]{1,0:T(8,128)(2,1)S(1)} %swap_sum.4.own), channel_id=1, source_target_pairs={{0,8},{1,9},{2,10},{3,11},{4,12},{5,13},{6,14},{7,15},{8,0},{9,1},... | collective-permute-start | bytes 417800 | tf_op jit(solution)/shard_map/ppermute | solution.py:331
  103.1 5.9 %collective-permute-start.19 = (bf16[2,128,512]{2,1,0:T(8,128)(2,1)}, bf16[2,128,512]{2,1,0:T(8,128)(2,1)S(1)}, u32[]{:S(2)}, u32[]{:S(2)}) collective-permute-start(bf16[2,128,512]{2,1,0:T(8,128)(2,1)} %get-tuple-element.84), channel_id=1, source_target_pairs={{0,3},{1,0},{2,1},{3,2},{4,7},{5,4},{6,5},{7,6},{8,11},{9,8},{10,9... | collective-permute-start | bytes 786440 | tf_op jit(solution)/shard_map/ppermute | solution.py:296
  104.7 7.0 %collective-permute-start.20 = (bf16[2,128,512]{2,1,0:T(8,128)(2,1)}, bf16[2,128,512]{2,1,0:T(8,128)(2,1)S(1)}, u32[]{:S(2)}, u32[]{:S(2)}) collective-permute-start(bf16[2,128,512]{2,1,0:T(8,128)(2,1)} %get-tuple-element.85), channel_id=1, source_target_pairs={{0,2},{1,3},{2,0},{3,1},{4,6},{5,7},{6,4},{7,5},{8,10},{9,11},{10,... | collective-permute-start | bytes 786440 | tf_op jit(solution)/shard_map/ppermute | solution.py:296
  105.6 13.7 %collective-permute-start.21 = (bf16[2,128,512]{2,1,0:T(8,128)(2,1)}, bf16[2,128,512]{2,1,0:T(8,128)(2,1)S(1)}, u32[]{:S(2)}, u32[]{:S(2)}) collective-permute-start(bf16[2,128,512]{2,1,0:T(8,128)(2,1)} %get-tuple-element.86), channel_id=1, source_target_pairs={{0,1},{1,2},{2,3},{3,0},{4,5},{5,6},{6,7},{7,4},{8,9},{9,10},{10,1... | collective-permute-start | bytes 786440 | tf_op jit(solution)/shard_map/ppermute | solution.py:296
  106.0 15.6 %copy-start.21 = (f32[16,1,384]{2,1,0:T(1,128)S(1)}, f32[16,1,384]{2,1,0:T(1,128)}, u32[]{:S(2)}) copy-start(f32[16,1,384]{2,1,0:T(1,128)} %get-tuple-element.90) | copy-start | bytes 73732
  107.0 13.6 %collective-permute-start.26 = (bf16[32,2176]{1,0:T(8,128)(2,1)S(1)}, bf16[32,2176]{1,0:T(8,128)(2,1)S(1)}, u32[]{:S(2)}, u32[]{:S(2)}) collective-permute-start(bf16[32,2176]{1,0:T(8,128)(2,1)S(1)} %swap_sum.5.own), channel_id=1, source_target_pairs={{0,1},{1,0},{2,3},{3,2},{4,5},{5,4},{6,7},{7,6},{8,9},{9,8},{10,11... | collective-permute-start | bytes 417800 | tf_op jit(solution)/shard_map/ppermute | solution.py:331
  119.3 1.0 copy-start.20
  120.6 13.6 %collective-permute-start.27 = (bf16[32,2176]{1,0:T(8,128)(2,1)S(1)}, bf16[32,2176]{1,0:T(8,128)(2,1)S(1)}, u32[]{:S(2)}, u32[]{:S(2)}) collective-permute-start(bf16[32,2176]{1,0:T(8,128)(2,1)S(1)} %swap_sum.6.own), channel_id=1, source_target_pairs={{0,2},{1,3},{2,0},{3,1},{4,6},{5,7},{6,4},{7,5},{8,10},{9,11},{10,... | collective-permute-start | bytes 417800 | tf_op jit(solution)/shard_map/ppermute | solution.py:331
  132.2 5.8 %collective-permute-start.22 = (bf16[128,512]{1,0:T(8,128)(2,1)S(1)}, bf16[128,512]{1,0:T(8,128)(2,1)S(1)}, u32[]{:S(2)}, u32[]{:S(2)}) collective-permute-start(bf16[128,512]{1,0:T(8,128)(2,1)S(1)} %get-tuple-element.88), channel_id=1, source_target_pairs={{0,12},{1,13},{2,14},{3,15},{4,0},{5,1},{6,2},{7,3},{8,4},{9,5},{1... | collective-permute-start | bytes 393224 | tf_op jit(solution)/shard_map/ppermute | solution.py:300
  133.1 5.3 %collective-permute-start.23 = (bf16[128,512]{1,0:T(8,128)(2,1)S(1)}, bf16[128,512]{1,0:T(8,128)(2,1)S(1)}, u32[]{:S(2)}, u32[]{:S(2)}) collective-permute-start(bf16[128,512]{1,0:T(8,128)(2,1)S(1)} %get-tuple-element.89), channel_id=1, source_target_pairs={{0,8},{1,9},{2,10},{3,11},{4,12},{5,13},{6,14},{7,15},{8,0},{9,1},... | collective-permute-start | bytes 393224 | tf_op jit(solution)/shard_map/ppermute | solution.py:300
  134.3 0.8 copy-start.16
  135.1 7.0 %collective-permute-start.28 = (bf16[32,2176]{1,0:T(8,128)(2,1)S(1)}, bf16[32,2176]{1,0:T(8,128)(2,1)S(1)}, u32[]{:S(2)}, u32[]{:S(2)}) collective-permute-start(bf16[32,2176]{1,0:T(8,128)(2,1)S(1)} %swap_sum.7.refs_0_), channel_id=1, source_target_pairs={{0,32},{16,48},{32,64},{48,80},{64,96},{80,112},{96,0},{112,16},{1... | collective-permute-start | bytes 417800 | tf_op jit(solution)/shard_map/ppermute | solution.py:304
  135.5 6.5 %collective-permute-start.29 = (bf16[32,2176]{1,0:T(8,128)(2,1)S(1)}, bf16[32,2176]{1,0:T(8,128)(2,1)S(1)}, u32[]{:S(2)}, u32[]{:S(2)}) collective-permute-start(bf16[32,2176]{1,0:T(8,128)(2,1)S(1)} %swap_sum.7.refs_0_), channel_id=1, source_target_pairs={{0,64},{16,80},{32,96},{48,112},{64,0},{80,16},{96,32},{112,48},{1... | collective-permute-start | bytes 417800 | tf_op jit(solution)/shard_map/ppermute | solution.py:304
  137.6 5.1 %collective-permute-start.30 = (bf16[32,2176]{1,0:T(8,128)(2,1)S(1)}, bf16[32,2176]{1,0:T(8,128)(2,1)S(1)}, u32[]{:S(2)}, u32[]{:S(2)}) collective-permute-start(bf16[32,2176]{1,0:T(8,128)(2,1)S(1)} %swap_sum.7.refs_0_), channel_id=1, source_target_pairs={{0,96},{16,112},{32,0},{48,16},{64,32},{80,48},{96,64},{112,80},{1... | collective-permute-start | bytes 417800 | tf_op jit(solution)/shard_map/ppermute | solution.py:304
  142.7 0.9 copy-start.15
  143.6 6.9 %collective-permute-start.31 = (bf16[32,8704]{1,0:T(8,128)(2,1)S(1)}, bf16[32,8704]{1,0:T(8,128)(2,1)S(1)}, u32[]{:S(2)}, u32[]{:S(2)}) collective-permute-start(bf16[32,8704]{1,0:T(8,128)(2,1)S(1)} %assemble.1.mine), channel_id=1, source_target_pairs={{0,16},{16,0},{32,48},{48,32},{64,80},{80,64},{96,112},{112,96},{1... | collective-permute-start | bytes 1671176 | tf_op jit(solution)/shard_map/ppermute | solution.py:308
